TPU v7x, 32 devices: a whole 2x2x4 slice. The times are simulated.
32 devices in a mesh: section: 2 (over core), tensor: 4 (over z), dp: 4 (over y, x).
Axes of the slice: x: 2, y: 2, z: 4, core: 2. Of those that a mesh axis runs over, the one named last changes fastest.
Arguments:
- layer_input: bfloat16 [2, 1024, 1536], P(None, 'dp'), may hold values from -6 to 6
- seq_lengths: int32 [2, 4], replicated, may hold values from 1 to 896, 1024 in all within a row
- norm1_gain: float32 [2, 1536], P('section'), may hold values from 0.1 to 1.9
- w_query: bfloat16 [2, 1536, 1536], P('section', None, 'tensor'), may hold values from -0.15625 to 0.15625
- w_key: bfloat16 [2, 1536, 768], P('section', None, 'tensor'), may hold values from -0.15625 to 0.15625
- w_value: bfloat16 [2, 1536, 768], P('section', None, 'tensor'), may hold values from -0.15625 to 0.15625
- w_out: bfloat16 [2, 1536, 1536], P('section', 'tensor'), may hold values from -1 to 1
- norm2_gain: float32 [2, 1536], P('section'), may hold values from 0.1 to 1.9
- w_gate: bfloat16 [2, 1536, 4096], P('section', None, 'tensor'), may hold values from -0.15625 to 0.15625
- w_up: bfloat16 [2, 1536, 4096], P('section', None, 'tensor'), may hold values from -0.15625 to 0.15625
- w_down: bfloat16 [2, 4096, 1536], P('section', 'tensor'), may hold values from -0.09375 to 0.09375
- out_grad: bfloat16 [2, 1024, 1536], P(None, 'dp'), may hold values from -6 to 6
Outputs:
- activations: bfloat16 [2, 2, 1024, 1536], P('section', None, 'dp')
- input_grads: bfloat16 [2, 2, 1024, 1536], P('section', None, 'dp')
- grad_norm1: float32 [2, 1536], P('section', 'dp')
- grad_query: float32 [2, 1536, 1536], P('section', 'dp', 'tensor')
- grad_key: float32 [2, 1536, 768], P('section', 'dp', 'tensor')
- grad_value: float32 [2, 1536, 768], P('section', 'dp', 'tensor')
- grad_out: float32 [2, 1536, 1536], P('section', 'tensor', 'dp')
- grad_norm2: float32 [2, 1536], P('section', 'dp')
- grad_gate: float32 [2, 1536, 4096], P('section', 'dp', 'tensor')
- grad_up: float32 [2, 1536, 4096], P('section', 'dp', 'tensor')
- grad_down: float32 [2, 4096, 1536], P('section', 'tensor', 'dp')
Inputs may be any that keep to these rules, and one draw needn't show every extreme that they name: `seq_lengths`: each row holds the lengths of the 4 sequences packed in order into one micro-batch; they sum to 1024, and the largest is exactly 896.
All inputs are finite; a program needn't handle non-finite values.
Results may differ from a plain program's by a relative error of at most 0.034.
Values may be sent and summed in bfloat16 or wider, within the bound.
No kernel may reach another device: no remote copies, remote signals or barrier semaphores. Data moves between devices by JAX's collectives and lax.ppermute only.
A program may use at most 192 MiB of HBM per device.

v0:
```python
import jax
import jax.numpy as jnp
from jax import lax
from jax.sharding import PartitionSpec as P

HEAD_DIM = 96


EPS = 1e-05
THETA = 100000.0
MASKED = -1e30


def shifted(shard, axis, by):
    peers = lax.axis_size(axis)
    pairs = [(i, i + by) for i in range(peers) if 0 <= i + by < peers]
    return lax.ppermute(shard, axis, pairs)


def product(left, right):
    return jnp.dot(left, right, preferred_element_type=jnp.float32)


def layout(lengths, token_count):
    seq_ends = jnp.cumsum(lengths)
    starts = seq_ends - lengths
    places = jnp.arange(token_count, dtype=jnp.int32)
    segment = jnp.sum((places[:, None] >= seq_ends[None, :]).astype(jnp.int32), axis=1)
    labels = jnp.arange(lengths.shape[0], dtype=jnp.int32)
    offset = jnp.sum(jnp.where(segment[:, None] == labels[None, :], starts[None, :], 0), axis=1)
    return (segment, places - offset)


def rotate(per_head, position, direction):
    head_size = per_head.shape[-1]
    halfway = head_size // 2
    inverse = THETA ** (-2.0 * jnp.arange(halfway, dtype=jnp.float32) / head_size)
    angles = position.astype(jnp.float32)[:, None] * inverse[None, :]
    cosine = jnp.cos(angles)[:, None, :]
    sine_part = direction * jnp.sin(angles)[:, None, :]
    leading = per_head[..., :halfway]
    trailing = per_head[..., halfway:]
    return jnp.concatenate(
        [leading * cosine - trailing * sine_part, trailing * cosine + leading * sine_part], axis=-1
    )


def norm_scale(values):
    return lax.rsqrt(jnp.mean(values * values, axis=-1, keepdims=True) + EPS)


def norm_back(values, scale_rows, gain, grad):
    weighted = grad * gain
    gain_grad = jnp.sum(grad * values * scale_rows, axis=0)
    coupling = jnp.mean(weighted * values, axis=-1, keepdims=True)
    return (
        scale_rows * weighted - values * scale_rows * scale_rows * scale_rows * coupling,
        gain_grad,
    )


def group_rows(per_head, kv_count):
    row_count, head_count, head_size = per_head.shape
    group_size = head_count // kv_count
    shaped = per_head.reshape(row_count, kv_count, group_size, head_size).transpose(1, 2, 0, 3)
    return shaped.reshape(kv_count, group_size * row_count, head_size)


def ungroup_rows(grouped, head_count):
    kv_count, grouped_rows, head_size = grouped.shape
    group_size = head_count // kv_count
    row_count = grouped_rows // group_size
    shaped = grouped.reshape(kv_count, group_size, row_count, head_size).transpose(2, 0, 1, 3)
    return shaped.reshape(row_count, head_count, head_size)


def key_blocks(flat_keys, flat_values, kv_count, segment, block_size):
    token_count = flat_keys.shape[0]
    block_count = token_count // block_size

    def shape_up(flat_rows):
        return flat_rows.reshape(block_count, block_size, kv_count, -1).transpose(0, 2, 1, 3)

    places = jnp.arange(token_count, dtype=jnp.int32).reshape(block_count, block_size)
    return (
        shape_up(flat_keys),
        segment.reshape(block_count, block_size),
        places,
        shape_up(flat_values),
    )


def block_scores(q_group, row_seg, row_place, key_block, seg_block, place_block, factor):
    raw = (
        jnp.einsum("hqd,hkd->hqk", q_group, key_block, preferred_element_type=jnp.float32) * factor
    )
    allowed = (row_seg[:, None] == seg_block[None, :]) & (
        place_block[None, :] <= row_place[:, None]
    )
    return jnp.where(allowed[None], raw, MASKED)


def attend_forward(q_group, row_seg, row_place, blocks, factor):
    kv_count, grouped_rows, head_size = q_group.shape

    def find_total(carry, block):
        run_max, run_sum = carry
        scores = block_scores(q_group, row_seg, row_place, block[0], block[1], block[2], factor)
        new_max = jnp.maximum(run_max, jnp.max(scores, axis=-1))
        run_sum = run_sum * jnp.exp(run_max - new_max) + jnp.sum(
            jnp.exp(scores - new_max[..., None]), axis=-1
        )
        return ((new_max, run_sum), None)

    start_max = jnp.full((kv_count, grouped_rows), MASKED, jnp.float32)
    (run_max, run_sum), _ = lax.scan(find_total, (start_max, jnp.zeros_like(start_max)), blocks)
    log_total = run_max + jnp.log(run_sum)

    def add_values(running, block):
        scores = block_scores(q_group, row_seg, row_place, block[0], block[1], block[2], factor)
        soft_weights = jnp.exp(scores - log_total[..., None]).astype(jnp.bfloat16)
        return (
            running
            + jnp.einsum(
                "hqk,hkd->hqd", soft_weights, block[3], preferred_element_type=jnp.float32
            ),
            None,
        )

    result, _ = lax.scan(
        add_values, jnp.zeros((kv_count, grouped_rows, head_size), jnp.float32), blocks
    )
    return (result, log_total)


def attend_backward(q_group, row_seg, row_place, blocks, result, log_total, grad_group, factor):
    delta = jnp.sum(grad_group.astype(jnp.float32) * result, axis=-1)

    def back_block(query_run, block):
        key_block, seg_block, place_block, value_block = block
        soft_weights = jnp.exp(
            block_scores(q_group, row_seg, row_place, key_block, seg_block, place_block, factor)
            - log_total[..., None]
        )
        weight_grad = jnp.einsum(
            "hqd,hkd->hqk", grad_group, value_block, preferred_element_type=jnp.float32
        )
        score_grad = (soft_weights * (weight_grad - delta[..., None]) * factor).astype(jnp.bfloat16)
        query_run = query_run + jnp.einsum(
            "hqk,hkd->hqd", score_grad, key_block, preferred_element_type=jnp.float32
        )
        key_grad = jnp.einsum(
            "hqk,hqd->hkd", score_grad, q_group, preferred_element_type=jnp.float32
        )
        value_grad = jnp.einsum(
            "hqk,hqd->hkd",
            soft_weights.astype(jnp.bfloat16),
            grad_group,
            preferred_element_type=jnp.float32,
        )
        return (query_run, (key_grad, value_grad))

    query_grad, (key_grads, value_grads) = lax.scan(
        back_block, jnp.zeros(q_group.shape, jnp.float32), blocks
    )
    block_count, kv_count, block_size, head_size = key_grads.shape

    def flatten(stacked):
        return stacked.transpose(0, 2, 1, 3).reshape(block_count * block_size, kv_count * head_size)

    return (query_grad, flatten(key_grads), flatten(value_grads))


def forward_layer(
    hidden_in, params, segment, position, my_first, block_size, factor, row_first, share
):
    (
        gain_one,
        query_weight,
        key_weight,
        value_weight,
        out_weight,
        gain_two,
        gate_weight,
        up_weight,
        down_weight,
    ) = params
    tok_dev = hidden_in.shape[0]
    head_size = HEAD_DIM
    q_count = query_weight.shape[1] // head_size
    kv_count = key_weight.shape[1] // head_size
    group_size = q_count // kv_count
    row_seg = lax.dynamic_slice_in_dim(segment, my_first, tok_dev, 0)
    row_pos = lax.dynamic_slice_in_dim(position, my_first, tok_dev, 0)
    row_place = my_first + jnp.arange(tok_dev, dtype=jnp.int32)
    hidden_f = hidden_in.astype(jnp.float32)
    scale_one = norm_scale(hidden_f)
    normed_one = (hidden_f * scale_one * gain_one).astype(jnp.bfloat16)
    queries = rotate(
        product(normed_one, query_weight).reshape(tok_dev, q_count, head_size), row_pos, 1.0
    ).astype(jnp.bfloat16)
    keys_local = rotate(
        product(normed_one, key_weight).reshape(tok_dev, kv_count, head_size), row_pos, 1.0
    )
    keys_local = keys_local.reshape(tok_dev, kv_count * head_size).astype(jnp.bfloat16)
    values_local = product(normed_one, value_weight).astype(jnp.bfloat16)
    keys_all, values_all = (
        lax.all_gather(keys_local, "dp", axis=0, tiled=True),
        lax.all_gather(values_local, "dp", axis=0, tiled=True),
    )
    q_group = group_rows(queries, kv_count)
    seg_grouped = jnp.tile(row_seg, group_size)
    place_grouped = jnp.tile(row_place, group_size)
    blocks = key_blocks(keys_all, values_all, kv_count, segment, block_size)
    result, log_total = attend_forward(q_group, seg_grouped, place_grouped, blocks, factor)
    attn_rows = (
        ungroup_rows(result, q_count).reshape(tok_dev, q_count * head_size).astype(jnp.bfloat16)
    )
    middle_share = lax.dynamic_slice_in_dim(hidden_f, row_first, share, 0) + lax.psum_scatter(
        product(attn_rows, out_weight).astype(jnp.bfloat16),
        "tensor",
        scatter_dimension=0,
        tiled=True,
    ).astype(jnp.float32)
    scale_two = norm_scale(middle_share)
    normed_share = (middle_share * scale_two * gain_two).astype(jnp.bfloat16)
    normed_two = lax.all_gather(normed_share, "tensor", axis=0, tiled=True)
    gate = product(normed_two, gate_weight)
    upward = product(normed_two, up_weight)
    hidden_act = (jax.nn.silu(gate) * upward).astype(jnp.bfloat16)
    out_share = (
        middle_share
        + lax.psum_scatter(
            product(hidden_act, down_weight).astype(jnp.bfloat16),
            "tensor",
            scatter_dimension=0,
            tiled=True,
        ).astype(jnp.float32)
    ).astype(jnp.bfloat16)
    output = lax.all_gather(out_share, "tensor", axis=0, tiled=True)
    saved = (
        hidden_f,
        scale_one,
        normed_one,
        q_group,
        keys_all,
        values_all,
        result,
        log_total,
        attn_rows,
        middle_share,
        scale_two,
        normed_two,
        gate,
        upward,
        hidden_act,
        row_pos,
        seg_grouped,
        place_grouped,
        segment,
    )
    return (output, saved)


def backward_layer(saved, grad_in, params, block_size, factor, row_first, share, tensor_count):
    (
        gain_one,
        query_weight,
        key_weight,
        value_weight,
        out_weight,
        gain_two,
        gate_weight,
        up_weight,
        down_weight,
    ) = params
    (
        hidden_f,
        scale_one,
        normed_one,
        q_group,
        keys_all,
        values_all,
        result,
        log_total,
        attn_rows,
        middle_share,
        scale_two,
        normed_two,
        gate,
        upward,
        hidden_act,
        row_pos,
        seg_grouped,
        place_grouped,
        segment,
    ) = saved
    tok_dev = grad_in.shape[0]
    head_size = HEAD_DIM
    q_count = query_weight.shape[1] // head_size
    kv_count = key_weight.shape[1] // head_size
    hidden_grad = jnp.dot(grad_in, down_weight.T, preferred_element_type=jnp.float32)
    sigma = jax.nn.sigmoid(gate)
    gate_grad = (hidden_grad * upward * sigma * (1.0 + gate * (1.0 - sigma))).astype(jnp.bfloat16)
    up_grad = (hidden_grad * gate * sigma).astype(jnp.bfloat16)
    down_weight_grad = product(hidden_act.T, grad_in)
    gate_weight_grad = product(normed_two.T, gate_grad)
    up_weight_grad = product(normed_two.T, up_grad)
    normed_two_grad = lax.psum_scatter(
        (
            jnp.dot(gate_grad, gate_weight.T, preferred_element_type=jnp.float32)
            + jnp.dot(up_grad, up_weight.T, preferred_element_type=jnp.float32)
        ).astype(jnp.bfloat16),
        "tensor",
        scatter_dimension=0,
        tiled=True,
    ).astype(jnp.float32)
    middle_norm_grad, gain_two_part = norm_back(middle_share, scale_two, gain_two, normed_two_grad)
    middle_grad = (
        lax.dynamic_slice_in_dim(grad_in, row_first, share, 0).astype(jnp.float32)
        + middle_norm_grad
    )
    middle_low = lax.all_gather(middle_grad.astype(jnp.bfloat16), "tensor", axis=0, tiled=True)
    out_weight_grad = product(attn_rows.T, middle_low)
    attn_grad = jnp.dot(middle_low, out_weight.T, preferred_element_type=jnp.float32).astype(
        jnp.bfloat16
    )
    grad_group = group_rows(attn_grad.reshape(tok_dev, q_count, head_size), kv_count)
    blocks = key_blocks(keys_all, values_all, kv_count, segment, block_size)
    query_grad, key_grads, value_grads = attend_backward(
        q_group, seg_grouped, place_grouped, blocks, result, log_total, grad_group, factor
    )
    key_sum, value_sum = (
        lax.psum_scatter(
            key_grads.astype(jnp.bfloat16), "dp", scatter_dimension=0, tiled=True
        ).astype(jnp.float32),
        lax.psum_scatter(
            value_grads.astype(jnp.bfloat16), "dp", scatter_dimension=0, tiled=True
        ).astype(jnp.float32),
    )
    query_pre = (
        rotate(ungroup_rows(query_grad, q_count), row_pos, -1.0)
        .reshape(tok_dev, q_count * head_size)
        .astype(jnp.bfloat16)
    )
    key_pre = (
        rotate(key_sum.reshape(tok_dev, kv_count, head_size), row_pos, -1.0)
        .reshape(tok_dev, kv_count * head_size)
        .astype(jnp.bfloat16)
    )
    value_pre = value_sum.astype(jnp.bfloat16)
    query_weight_grad = product(normed_one.T, query_pre)
    key_weight_grad = product(normed_one.T, key_pre)
    value_weight_grad = product(normed_one.T, value_pre)
    partial_grad = (
        jnp.dot(query_pre, query_weight.T, preferred_element_type=jnp.float32)
        + jnp.dot(key_pre, key_weight.T, preferred_element_type=jnp.float32)
        + jnp.dot(value_pre, value_weight.T, preferred_element_type=jnp.float32)
    )
    gain_one_part = jnp.sum(partial_grad * hidden_f * scale_one, axis=0)
    normed_one_grad, gain_two_sum, gain_one_sum = (
        lax.psum_scatter(
            partial_grad.astype(jnp.bfloat16), "tensor", scatter_dimension=0, tiled=True
        ).astype(jnp.float32),
        lax.psum_scatter(
            jnp.tile(gain_two_part[None], (tensor_count, 1)).astype(jnp.bfloat16),
            "tensor",
            scatter_dimension=0,
            tiled=True,
        ).astype(jnp.float32),
        lax.psum_scatter(
            jnp.tile(gain_one_part[None], (tensor_count, 1)).astype(jnp.bfloat16),
            "tensor",
            scatter_dimension=0,
            tiled=True,
        ).astype(jnp.float32),
    )
    hidden_share = lax.dynamic_slice_in_dim(hidden_f, row_first, share, 0)
    scale_share = lax.dynamic_slice_in_dim(scale_one, row_first, share, 0)
    input_norm_grad, unused_gain = norm_back(hidden_share, scale_share, gain_one, normed_one_grad)
    input_share = (middle_grad + input_norm_grad).astype(jnp.bfloat16)
    input_grad = lax.all_gather(input_share, "tensor", axis=0, tiled=True)
    return (
        input_grad,
        (
            gain_one_sum[0],
            query_weight_grad,
            key_weight_grad,
            value_weight_grad,
            out_weight_grad,
            gain_two_sum[0],
            gate_weight_grad,
            up_weight_grad,
            down_weight_grad,
        ),
    )


def per_device(
    layer_input,
    seq_lengths,
    norm1_gain,
    w_query,
    w_key,
    w_value,
    w_out,
    norm2_gain,
    w_gate,
    w_up,
    w_down,
    out_grad,
):
    micro_count = layer_input.shape[0]
    tok_dev = layer_input.shape[1]
    token_count = tok_dev * lax.axis_size("dp")
    my_first = lax.axis_index("dp") * tok_dev
    tensor_count = lax.axis_size("tensor")
    share = tok_dev // tensor_count
    row_first = lax.axis_index("tensor") * share
    first_section = lax.axis_index("section") == 0
    block_size = min(1024, token_count)
    factor = HEAD_DIM ** (-0.5)
    params = (
        norm1_gain[0],
        w_query[0],
        w_key[0],
        w_value[0],
        w_out[0],
        norm2_gain[0],
        w_gate[0],
        w_up[0],
        w_down[0],
    )
    layouts = [layout(seq_lengths[micro_index], token_count) for micro_index in range(micro_count)]

    def choose(early, later):
        return jax.tree.map(lambda left, right: jnp.where(first_section, left, right), early, later)

    arrived = jnp.zeros(layer_input.shape[1:], jnp.bfloat16)
    outputs = []
    saved_steps = []
    for step_index in range(micro_count + 1):
        first_micro = min(step_index, micro_count - 1)
        second_micro = max(step_index - 1, 0)
        segment, position = choose(layouts[first_micro], layouts[second_micro])
        hidden_in = jnp.where(first_section, layer_input[first_micro], arrived)
        output, saved = forward_layer(
            hidden_in, params, segment, position, my_first, block_size, factor, row_first, share
        )
        outputs.append(output)
        saved_steps.append(saved)
        if step_index < micro_count:
            arrived = shifted(output, "section", 1)
    coming = jnp.zeros(layer_input.shape[1:], jnp.bfloat16)
    back_outs = []
    totals = None
    for step_index in range(micro_count + 1):
        saved = choose(
            saved_steps[max(step_index - 1, 0)], saved_steps[min(step_index + 1, micro_count)]
        )
        grad_in = jnp.where(first_section, coming, out_grad[min(step_index, micro_count - 1)])
        valid = jnp.where(first_section, step_index >= 1, step_index < micro_count).astype(
            jnp.float32
        )
        input_grad, grads = backward_layer(
            saved, grad_in, params, block_size, factor, row_first, share, tensor_count
        )
        back_outs.append(input_grad)
        scaled = tuple((piece * valid for piece in grads))
        if step_index == 0:
            totals = scaled
        else:
            totals = tuple((left + right for left, right in zip(totals, scaled)))
        if step_index < micro_count:
            coming = shifted(input_grad, "section", -1)
    totals = (
        lax.psum_scatter(
            totals[0].astype(jnp.bfloat16), "dp", scatter_dimension=0, tiled=True
        ).astype(jnp.float32),
        lax.psum_scatter(
            totals[1].astype(jnp.bfloat16), "dp", scatter_dimension=0, tiled=True
        ).astype(jnp.float32),
        lax.psum_scatter(
            totals[2].astype(jnp.bfloat16), "dp", scatter_dimension=0, tiled=True
        ).astype(jnp.float32),
        lax.psum_scatter(
            totals[3].astype(jnp.bfloat16), "dp", scatter_dimension=0, tiled=True
        ).astype(jnp.float32),
        lax.psum_scatter(
            totals[4].astype(jnp.bfloat16), "dp", scatter_dimension=1, tiled=True
        ).astype(jnp.float32),
        lax.psum_scatter(
            totals[5].astype(jnp.bfloat16), "dp", scatter_dimension=0, tiled=True
        ).astype(jnp.float32),
        lax.psum_scatter(
            totals[6].astype(jnp.bfloat16), "dp", scatter_dimension=0, tiled=True
        ).astype(jnp.float32),
        lax.psum_scatter(
            totals[7].astype(jnp.bfloat16), "dp", scatter_dimension=0, tiled=True
        ).astype(jnp.float32),
        lax.psum_scatter(
            totals[8].astype(jnp.bfloat16), "dp", scatter_dimension=1, tiled=True
        ).astype(jnp.float32),
    )
    activations = jnp.stack(
        [
            jnp.where(first_section, outputs[micro_index], outputs[micro_index + 1])
            for micro_index in range(micro_count)
        ]
    )[None]
    input_grads = jnp.stack(
        [
            jnp.where(first_section, back_outs[micro_index + 1], back_outs[micro_index])
            for micro_index in range(micro_count)
        ]
    )[None]
    return (
        activations,
        input_grads,
        totals[0][None],
        totals[1][None],
        totals[2][None],
        totals[3][None],
        totals[4][None],
        totals[5][None],
        totals[6][None],
        totals[7][None],
        totals[8][None],
    )


def solution(mesh):
    placed = (
        P(None, "dp", None),
        P(),
        P("section", None),
        P("section", None, "tensor"),
        P("section", None, "tensor"),
        P("section", None, "tensor"),
        P("section", "tensor", None),
        P("section", None),
        P("section", None, "tensor"),
        P("section", None, "tensor"),
        P("section", "tensor", None),
        P(None, "dp", None),
    )
    return jax.shard_map(
        per_device,
        mesh=mesh,
        in_specs=placed,
        out_specs=(
            P("section", None, "dp", None),
            P("section", None, "dp", None),
            P("section", "dp"),
            P("section", "dp", "tensor"),
            P("section", "dp", "tensor"),
            P("section", "dp", "tensor"),
            P("section", "tensor", "dp"),
            P("section", "dp"),
            P("section", "dp", "tensor"),
            P("section", "dp", "tensor"),
            P("section", "tensor", "dp"),
        ),
        check_vma=False,
    )
```

profile of v0, /device:TPU:0, one launch (start us, length us, event | category | flops | bytes accessed | tf_op | source)
XLA Modules:
  0.0 1183.7 jit_solution(3391116213327868141)
XLA Ops:
  66.1 21.3 %reduce-scatter.34.cloned.1.call-done = bf16[64,1536]{1,0:T(8,128)(2,1)} async-done(((bf16[256,1536]{1,0:T(8,128)(2,1)}), bf16[64,1536]{1,0:T(8,128)(2,1)}) %reduce-scatter.34.cloned.1.call-update) | async-done | bytes 196624 | tf_op jit(solution)/shard_map/reduce_scatter | solution.py:219
  115.4 22.7 %reduce-scatter.36.cloned.1.call-done = bf16[64,1536]{1,0:T(8,128)(2,1)} async-done(((bf16[256,1536]{1,0:T(8,128)(2,1)}), bf16[64,1536]{1,0:T(8,128)(2,1)}) %reduce-scatter.36.cloned.1.call-update) | async-done | bytes 196624 | tf_op jit(solution)/shard_map/reduce_scatter | solution.py:233
  139.1 18.0 %all_gather.57 = bf16[256,1536]{1,0:T(8,128)(2,1)S(1)} all-gather(bf16[64,1536]{1,0:T(8,128)(2,1)S(1)} %add_convert_fusion.8), channel_id=1, replica_groups=mesh['section'=2,'tensor'=4,'dp'=4] {'tensor'}, dimensions={0}, use_global_device_ids=true | all-gather | bytes 983040 | tf_op jit(solution)/shard_map/all_gather | solution.py:240
  201.9 21.7 %reduce-scatter.38.cloned.1.call-done = bf16[64,1536]{1,0:T(8,128)(2,1)} async-done(((bf16[256,1536]{1,0:T(8,128)(2,1)}), bf16[64,1536]{1,0:T(8,128)(2,1)}) %reduce-scatter.38.cloned.1.call-update) | async-done | bytes 196624 | tf_op jit(solution)/shard_map/reduce_scatter | solution.py:219
  226.2 18.0 %all_gather.60 = bf16[256,1536]{1,0:T(8,128)(2,1)S(1)} all-gather(bf16[64,1536]{1,0:T(8,128)(2,1)S(1)} %multiply_convert_fusion.15), channel_id=1, replica_groups=mesh['section'=2,'tensor'=4,'dp'=4] {'tensor'}, dimensions={0}, use_global_device_ids=true | all-gather | bytes 983040 | tf_op jit(solution)/shard_map/all_gather | solution.py:227
  278.3 24.7 %reduce-scatter.40.cloned.1.call-done = bf16[64,1536]{1,0:T(8,128)(2,1)} async-done(((bf16[256,1536]{1,0:T(8,128)(2,1)}), bf16[64,1536]{1,0:T(8,128)(2,1)}) %reduce-scatter.40.cloned.1.call-update) | async-done | bytes 196624 | tf_op jit(solution)/shard_map/reduce_scatter | solution.py:233
  305.0 18.4 %all_gather.61 = bf16[256,1536]{1,0:T(8,128)(2,1)} all-gather(bf16[64,1536]{1,0:T(8,128)(2,1)S(1)} %get-tuple-element.353), channel_id=1, replica_groups=mesh['section'=2,'tensor'=4,'dp'=4] {'tensor'}, dimensions={0}, use_global_device_ids=true | all-gather | bytes 983040 | tf_op jit(solution)/shard_map/all_gather | solution.py:240
  445.9 19.7 %reduce-scatter.42.cloned.1.call-done = bf16[64,1536]{1,0:T(8,128)(2,1)} async-done(((bf16[256,1536]{1,0:T(8,128)(2,1)}), bf16[64,1536]{1,0:T(8,128)(2,1)}) %reduce-scatter.42.cloned.1.call-update) | async-done | bytes 196624 | tf_op jit(solution)/shard_map/reduce_scatter | solution.py:219
  468.8 21.7 %reduce-scatter.52.cloned.1.call-done = bf16[64,1536]{1,0:T(8,128)(2,1)} async-done(((bf16[256,1536]{1,0:T(8,128)(2,1)}), bf16[64,1536]{1,0:T(8,128)(2,1)}) %reduce-scatter.52.cloned.1.call-update) | async-done | bytes 196624 | tf_op jit(solution)/shard_map/reduce_scatter | solution.py:362
  493.7 18.0 %all_gather.67 = bf16[256,1536]{1,0:T(8,128)(2,1)S(1)} all-gather(bf16[64,1536]{1,0:T(8,128)(2,1)S(1)} %get-tuple-element.401), channel_id=1, replica_groups=mesh['section'=2,'tensor'=4,'dp'=4] {'tensor'}, dimensions={0}, use_global_device_ids=true | all-gather | bytes 983040 | tf_op jit(solution)/shard_map/all_gather | solution.py:382
  513.0 18.4 %all_gather.64 = bf16[256,1536]{1,0:T(8,128)(2,1)S(1)} all-gather(bf16[64,1536]{1,0:T(8,128)(2,1)S(1)} %get-tuple-element.402), channel_id=1, replica_groups=mesh['section'=2,'tensor'=4,'dp'=4] {'tensor'}, dimensions={0}, use_global_device_ids=true | all-gather | bytes 983040 | tf_op jit(solution)/shard_map/all_gather | solution.py:227
  567.7 18.3 %all_gather.68 = bf16[256,1536]{1,0:T(8,128)(2,1)S(1)} all-gather(bf16[64,1536]{1,0:T(8,128)(2,1)S(1)} %fusion.222), channel_id=1, replica_groups=mesh['section'=2,'tensor'=4,'dp'=4] {'tensor'}, dimensions={0}, use_global_device_ids=true | all-gather | bytes 983040 | tf_op jit(solution)/shard_map/all_gather | solution.py:323
  627.2 21.6 %reduce-scatter.58.cloned.1.call-done = bf16[256,192]{0,1:T(8,128)(2,1)} async-done(((bf16[1024,192]{0,1:T(8,128)(2,1)}), bf16[256,192]{0,1:T(8,128)(2,1)}) %reduce-scatter.58.cloned.1.call-update) | async-done | bytes 98320 | tf_op jit(solution)/shard_map/reduce_scatter | solution.py:337
  654.7 22.3 %reduce-scatter.60.cloned.1.call-done = bf16[64,1536]{1,0:T(8,128)(2,1)} async-done(((bf16[256,1536]{1,0:T(8,128)(2,1)}), bf16[64,1536]{1,0:T(8,128)(2,1)}) %reduce-scatter.60.cloned.1.call-update) | async-done | bytes 196624 | tf_op jit(solution)/shard_map/reduce_scatter | solution.py:362
  733.2 25.3 %reduce-scatter.44.cloned.1.call-done = bf16[64,1536]{1,0:T(8,128)(2,1)} async-done(((bf16[256,1536]{1,0:T(8,128)(2,1)}), bf16[64,1536]{1,0:T(8,128)(2,1)}) %reduce-scatter.44.cloned.1.call-update) | async-done | bytes 196624 | tf_op jit(solution)/shard_map/reduce_scatter | solution.py:233
  763.1 18.6 %all_gather.70 = bf16[256,1536]{1,0:T(8,128)(2,1)S(1)} all-gather(bf16[64,1536]{1,0:T(8,128)(2,1)S(1)} %fusion.223), channel_id=1, replica_groups=mesh['section'=2,'tensor'=4,'dp'=4] {'tensor'}, dimensions={0}, use_global_device_ids=true | all-gather | bytes 983040 | tf_op jit(solution)/shard_map/all_gather | solution.py:323
  819.6 22.9 %reduce-scatter.66.cloned.1.call-done = bf16[256,192]{0,1:T(8,128)(2,1)} async-done(((bf16[1024,192]{0,1:T(8,128)(2,1)}), bf16[256,192]{0,1:T(8,128)(2,1)}) %reduce-scatter.66.cloned.1.call-update) | async-done | bytes 98320 | tf_op jit(solution)/shard_map/reduce_scatter | solution.py:337
  898.1 19.5 %all_gather.65 = bf16[256,1536]{1,0:T(8,128)(2,1)S(1)} all-gather(bf16[64,1536]{1,0:T(8,128)(2,1)S(1)} %copy-done.133), channel_id=1, replica_groups=mesh['section'=2,'tensor'=4,'dp'=4] {'tensor'}, dimensions={0}, use_global_device_ids=true | all-gather | bytes 983040 | tf_op jit(solution)/shard_map/all_gather | solution.py:240
  946.0 29.8 %reduce-scatter.80.cloned.1.call-done = bf16[384,384]{1,0:T(8,128)(2,1)} async-done(((bf16[1536,384]{1,0:T(8,128)(2,1)}), bf16[384,384]{1,0:T(8,128)(2,1)}) %reduce-scatter.80.cloned.1.call-update) | async-done | bytes 294928
  977.8 30.3 %reduce-scatter.70.cloned.1.call-done = bf16[384,384]{1,0:T(8,128)(2,1)} async-done(((bf16[1536,384]{1,0:T(8,128)(2,1)}), bf16[384,384]{1,0:T(8,128)(2,1)}) %reduce-scatter.70.cloned.1.call-update) | async-done | bytes 294928 | tf_op jit(solution)/shard_map/reduce_scatter | solution.py:480
  1009.9 24.0 %reduce-scatter.68.cloned.1.call-done = bf16[64,1536]{1,0:T(8,128)(2,1)} async-done(((bf16[256,1536]{1,0:T(8,128)(2,1)}), bf16[64,1536]{1,0:T(8,128)(2,1)}) %reduce-scatter.68.cloned.1.call-update) | async-done | bytes 196624 | tf_op jit(solution)/shard_map/reduce_scatter | solution.py:362
  1057.0 23.2 %reduce-scatter.82.cloned.1.call-done = bf16[384,1024]{1,0:T(8,128)(2,1)} async-done(((bf16[1536,1024]{1,0:T(8,128)(2,1)}), bf16[384,1024]{1,0:T(8,128)(2,1)}) %reduce-scatter.82.cloned.1.call-update) | async-done | bytes 786448
  1085.0 42.4 %reduce-scatter.72.cloned.1.call-done = bf16[384,1024]{1,0:T(8,128)(2,1)} async-done(((bf16[1536,1024]{1,0:T(8,128)(2,1)}), bf16[384,1024]{1,0:T(8,128)(2,1)}) %reduce-scatter.72.cloned.1.call-update) | async-done | bytes 786448 | tf_op jit(solution)/shard_map/reduce_scatter | solution.py:495
  1129.9 44.6 %reduce-scatter.74.cloned.1.call-done = bf16[384,1024]{1,0:T(8,128)(2,1)} async-done(((bf16[1536,1024]{1,0:T(8,128)(2,1)}), bf16[384,1024]{1,0:T(8,128)(2,1)}) %reduce-scatter.74.cloned.1.call-update) | async-done | bytes 786448 | tf_op jit(solution)/shard_map/reduce_scatter | solution.py:498
  (765 shorter events, 600.9 us)
Async XLA Ops:
  7.2 80.2 %reduce-scatter.34.cloned.1.call-start = ((), (), s32[]{:S(2)}) async-start(), calls=%async_computation.25 | async-start | bytes 983040 | tf_op jit(solution)/shard_map/reduce_scatter | solution.py:219
  63.6 74.4 %reduce-scatter.36.cloned.1.call-start = ((), (), s32[]{:S(2)}) async-start(), calls=%async_computation.26 | async-start | bytes 983040 | tf_op jit(solution)/shard_map/reduce_scatter | solution.py:233
  115.3 108.4 %reduce-scatter.38.cloned.1.call-start = ((), (), s32[]{:S(2)}) async-start(), calls=%async_computation.27 | async-start | bytes 983040 | tf_op jit(solution)/shard_map/reduce_scatter | solution.py:219
  201.9 76.4 %reduce-scatter.46.cloned.1.call-start = ((), (), s32[]{:S(2)}) async-start(), calls=%async_computation.31 | async-start | bytes 983040 | tf_op jit(solution)/shard_map/reduce_scatter | solution.py:309
  259.0 160.4 %reduce-scatter.48.cloned.1.call-start = ((), (), s32[]{:S(2)}) async-start(), calls=%async_computation.32 | async-start | bytes 491520 | tf_op jit(solution)/shard_map/reduce_scatter | solution.py:334
  389.2 50.7 %reduce-scatter.50.cloned.1.call-start = ((), (), s32[]{:S(2)}) async-start(), calls=%async_computation.33 | async-start | bytes 491520 | tf_op jit(solution)/shard_map/reduce_scatter | solution.py:337
  403.1 62.5 %reduce-scatter.42.cloned.1.call-start = ((), (), s32[]{:S(2)}) async-start(), calls=%async_computation.29 | async-start | bytes 983040 | tf_op jit(solution)/shard_map/reduce_scatter | solution.py:219
  414.5 76.0 %reduce-scatter.52.cloned.1.call-start = ((), (), s32[]{:S(2)}) async-start(), calls=%async_computation.34 | async-start | bytes 983040 | tf_op jit(solution)/shard_map/reduce_scatter | solution.py:362
  444.7 119.3 %reduce-scatter.54.cloned.1.call-start = ((), (), s32[]{:S(2)}) async-start(), calls=%async_computation.35 | async-start | bytes 983040 | tf_op jit(solution)/shard_map/reduce_scatter | solution.py:309
  540.9 80.7 %reduce-scatter.56.cloned.1.call-start = ((), (), s32[]{:S(2)}) async-start(), calls=%async_computation.36 | async-start | bytes 491520 | tf_op jit(solution)/shard_map/reduce_scatter | solution.py:334
  597.4 51.3 %reduce-scatter.58.cloned.1.call-start = ((), (), s32[]{:S(2)}) async-start(), calls=%async_computation.37 | async-start | bytes 491520 | tf_op jit(solution)/shard_map/reduce_scatter | solution.py:337
  603.8 73.2 %reduce-scatter.60.cloned.1.call-start = ((), (), s32[]{:S(2)}) async-start(), calls=%async_computation.38 | async-start | bytes 983040 | tf_op jit(solution)/shard_map/reduce_scatter | solution.py:362
  653.5 79.7 %reduce-scatter.62.cloned.1.call-start = ((), (), s32[]{:S(2)}) async-start(), calls=%async_computation.39 | async-start | bytes 983040 | tf_op jit(solution)/shard_map/reduce_scatter | solution.py:309
  713.5 101.3 %reduce-scatter.64.cloned.1.call-start = ((), (), s32[]{:S(2)}) async-start(), calls=%async_computation.40 | async-start | bytes 491520 | tf_op jit(solution)/shard_map/reduce_scatter | solution.py:334
  791.0 51.5 %reduce-scatter.66.cloned.1.call-start = ((), (), s32[]{:S(2)}) async-start(), calls=%async_computation.41 | async-start | bytes 491520 | tf_op jit(solution)/shard_map/reduce_scatter | solution.py:337
  798.2 121.9 %all-reduce.12.cloned.1.call-start = ((), (), s32[]{:S(2)}) async-start(), calls=%async_computation.50 | async-start | bytes 147456
  849.9 83.7 %reduce-scatter.76.cloned.1.call-start = ((), (), s32[]{:S(2)}) async-start(), calls=%async_computation.46 | async-start | bytes 983040
  855.5 88.0 %reduce-scatter.78.cloned.1.call-start = ((), (), s32[]{:S(2)}) async-start(), calls=%async_computation.47 | async-start | bytes 983040
  863.0 112.8 %reduce-scatter.80.cloned.1.call-start = ((), (), s32[]{:S(2)}) async-start(), calls=%async_computation.48 | async-start | bytes 1474560
  869.9 138.2 %reduce-scatter.70.cloned.1.call-start = ((), (), s32[]{:S(2)}) async-start(), calls=%async_computation.43 | async-start | bytes 1474560 | tf_op jit(solution)/shard_map/reduce_scatter | solution.py:480
  874.4 159.5 %reduce-scatter.68.cloned.1.call-start = ((), (), s32[]{:S(2)}) async-start(), calls=%async_computation.42 | async-start | bytes 983040 | tf_op jit(solution)/shard_map/reduce_scatter | solution.py:362
  875.1 205.1 %reduce-scatter.82.cloned.1.call-start = ((), (), s32[]{:S(2)}) async-start(), calls=%async_computation.49 | async-start | bytes 3932160
  882.5 245.0 %reduce-scatter.72.cloned.1.call-start = ((), (), s32[]{:S(2)}) async-start(), calls=%async_computation.44 | async-start | bytes 3932160 | tf_op jit(solution)/shard_map/reduce_scatter | solution.py:495
  889.3 285.3 %reduce-scatter.74.cloned.1.call-start = ((), (), s32[]{:S(2)}) async-start(), calls=%async_computation.45 | async-start | bytes 3932160 | tf_op jit(solution)/shard_map/reduce_scatter | solution.py:498
  (221 other events, 2295.5 us)
Sparse Core Ops, SparseCore 0:
  63.7 23.6 reduce-scatter.33
  115.4 22.5 reduce-scatter.35
  255.7 22.5 reduce-scatter.45
  280.4 22.5 reduce-scatter.39
  389.3 23.3 reduce-scatter.47
  415.5 24.4 reduce-scatter.49
  442.3 23.2 reduce-scatter.41
  467.9 22.5 reduce-scatter.51
  541.0 22.8 reduce-scatter.53
  597.6 24.0 reduce-scatter.55
  624.3 24.4 reduce-scatter.57
  653.6 23.3 reduce-scatter.59
  710.6 22.5 reduce-scatter.61
  791.1 23.6 reduce-scatter.63
  818.0 24.4 reduce-scatter.65
  850.0 34.6 all-reduce.11
  887.8 26.2 reduce-scatter.75
  917.1 26.3 reduce-scatter.77
  947.2 28.5 reduce-scatter.79
  979.6 28.5 reduce-scatter.69
  1010.5 23.3 reduce-scatter.67
  1037.0 43.1 reduce-scatter.81
  1083.5 43.9 reduce-scatter.71
  1130.6 43.9 reduce-scatter.73
  (2 shorter events, 44.1 us)
where the time goes:
time: 1200 us; the launch traced here: 1180 us
  waiting for transfers between devices  527 us (44%)
  blocking collectives  300 us (25%)
  matrix products  165 us (14%)
  other arithmetic  94.5 us (8%)
  local copies, waits for them, and re-layouts  72.1 us (6%)
  between operations  17.6 us (1%)
    reduce_scatter x3, waiting for transfers between devices, forward_layer(): lax.psum_scatter(product(hidden_act, down_weight).astype(jnp.bfloat16), '...  72.7 us
    reduce_scatter x3, waiting for transfers between devices, backward_layer(): lax.psum_scatter(partial_grad.astype(jnp.bfloat16), 'tensor', scatter_dim...  67.9 us
    dot_general x42, matrix products, product(): return jnp.dot(left, right, preferred_element_type=jnp.float32)  64.1 us
    unnamed x31, waiting for transfers between devices  62.9 us
    reduce_scatter x3, waiting for transfers between devices, forward_layer(): lax.psum_scatter(product(attn_rows, out_weight).astype(jnp.bfloat16), 'te...  62.7 us
    reduce_scatter x3, waiting for transfers between devices, backward_layer(): lax.psum_scatter(value_grads.astype(jnp.bfloat16), 'dp', scatter_dimensio...  59.5 us
    all_gather x3, blocking collectives, forward_layer(): output = lax.all_gather(out_share, 'tensor', axis=0, tiled=True)  55.9 us
    all_gather x3, blocking collectives, forward_layer(): normed_two = lax.all_gather(normed_share, 'tensor', axis=0, tiled=True)  54.3 us
  transfers between devices with their start and end apart: 30, of which 25 were waited for; matrix products, arithmetic and copies ran while one was open for 14% of the time, Pallas kernels for 0%

commit v1 on v0

v1 whole, which is shorter than its diff:
```python
import functools

import jax
import jax.numpy as jnp
from jax import lax
from jax.experimental import pallas as pl
from jax.experimental.pallas import tpu as pltpu
from jax.sharding import PartitionSpec as P

HEAD_DIM = 96
EPS = 1e-05
THETA = 100000.0
MASKED = -1e30
BF = jnp.bfloat16
F32 = jnp.float32
FACTOR = HEAD_DIM ** (-0.5)
CHUNKS = 2
TILE = 256
AHEAD = 6


def dot(left, right):
    return jnp.dot(left, right, preferred_element_type=F32)


def dot_t(left, right):
    return lax.dot_general(left, right, (((1,), (1,)), ((), ())), preferred_element_type=F32)


def outer(left, right):
    return lax.dot_general(left, right, (((0,), (0,)), ((), ())), preferred_element_type=F32)


def swap(value):
    return lax.ppermute(value, "section", [(0, 1), (1, 0)])


def shape(dims, dtype):
    return jax.ShapeDtypeStruct(dims, dtype)


VMEM = pl.BlockSpec(memory_space=pltpu.VMEM)
ANY = pl.BlockSpec(memory_space=pl.ANY)
NEAR, FAR, RAW, LOOSE, LOOSE_RAW = "near", "far", "raw", "loose", "loose raw"


class Late:
    def __init__(self, source, buffer, sem):
        self.buffer = buffer
        self.copy = pltpu.make_async_copy(source, buffer, sem)
        self.copy.start()
        self.waited = False

    def __getitem__(self, index):
        if not self.waited:
            self.copy.wait()
            self.waited = True
        return self.buffer[index]


class Leaving:
    def __init__(self, buffer, target, sem):
        self.buffer, self.target, self.sem = buffer, target, sem
        self.copy = pltpu.make_async_copy(buffer, target, sem)
        self.started = False

    def __setitem__(self, index, value):
        self.buffer[index] = value

    def __getitem__(self, index):
        return self.buffer[index]

    def send(self, *parts):
        if parts:
            for index in parts:
                pltpu.make_async_copy(self.buffer.at[index], self.target.at[index], self.sem).start()
        elif not self.started:
            self.copy.start()
        self.started = True


def fixed(value, where):
    if where in (LOOSE, LOOSE_RAW):
        return value
    return pltpu.with_memory_space_constraint(value, pltpu.VMEM if where == NEAR else pltpu.HBM)


class Order:
    token = ()


def kernel_call(body, name, ins, outs, scratch=(), after=(), cost=1.0, limit=24):
    after = [*after, *Order.token]
    far_in = [i for i, (_, where) in enumerate(ins) if where in (FAR, LOOSE)]
    far_out = [i for i, (_, where) in enumerate(outs) if where == FAR]
    buffers = [pltpu.VMEM(ins[i][0].shape, ins[i][0].dtype) for i in far_in]
    buffers += [pltpu.VMEM(outs[i][0].shape, outs[i][0].dtype) for i in far_out]
    count = len(far_in) + len(far_out)
    if count:
        buffers.append(pltpu.SemaphoreType.DMA((count,)))

    def whole(*refs):
        refs = list(refs)
        in_refs, refs = refs[: len(ins)], refs[len(ins) + len(after) :]
        out_refs, refs = refs[: len(outs)], refs[len(outs) :]
        own, refs = refs[: len(buffers)], refs[len(buffers) :]
        for place, index in enumerate(far_in):
            in_refs[index] = Late(in_refs[index], own[place], own[-1].at[place])
        for place, index in enumerate(far_out, len(far_in)):
            out_refs[index] = Leaving(own[place], out_refs[index], own[-1].at[place])
        body(in_refs, out_refs, *refs)
        for index in far_in:
            in_refs[index][0:1]
        for index in far_out:
            out_refs[index].send()
        for index in far_out:
            out_refs[index].copy.wait()

    call = pl.pallas_call(
        whole,
        out_shape=[
            pltpu.VMEM(out.shape, out.dtype) if where == NEAR else pltpu.HBM(out.shape, out.dtype)
            for out, where in outs
        ],
        in_specs=[VMEM if where == NEAR else ANY for _, where in ins] + [ANY] * len(after),
        out_specs=[VMEM if where == NEAR else ANY for _, where in outs],
        scratch_shapes=buffers + list(scratch),
        compiler_params=pltpu.CompilerParams(vmem_limit_bytes=limit * 1024 * 1024),
        cost_estimate=pl.CostEstimate(flops=int(cost * 1e9), bytes_accessed=0, transcendentals=0),
        name=name,
    )
    results = call(*[fixed(value, where) for value, where in [*ins, *after]])
    best = min(range(len(outs)), key=lambda index: outs[index][0].size)
    Order.token = ((results[best], NEAR if outs[best][1] == NEAR else RAW),)
    return results


def near(values):
    return [(value, NEAR) for value in values]


def far(values):
    return [(value, FAR) for value in values]


def raw(values):
    return [(value, RAW) for value in values]


def loose(values):
    return [(value, LOOSE) for value in values]


def weights(pairs):
    return raw([weight for pair in pairs for weight in pair])


def fetch(layer, copies):
    mine = lax.axis_index("section") == layer

    @pl.when(mine)
    def _():
        for own, _, buffer, sem in copies:
            pltpu.make_async_copy(own, buffer, sem).start()

    @pl.when(jnp.logical_not(mine))
    def _():
        for _, other, buffer, sem in copies:
            pltpu.make_async_copy(other, buffer, sem).start()


def arrived(own, buffer, sem):
    pltpu.make_async_copy(own, buffer, sem).wait()


def is_middle():
    index = lax.axis_index("tensor")
    return (index == 1) | (index == 2)


def summed(refs):
    middle = is_middle()
    parts = []
    for index in range(CHUNKS):
        parts.append(jnp.where(middle, refs[2 * index][...], refs[2 * index + 1][...]))
    return jnp.concatenate(parts, axis=1).astype(F32)


def store_chunks(value, refs):
    size = value.shape[1] // len(refs)
    for index, ref in enumerate(refs):
        ref[...] = value[:, index * size : (index + 1) * size].astype(BF)


def store_halves(value, mine_out, theirs_out):
    half = value.shape[1] // 2
    early = lax.axis_index("section") == 0
    left, right = value[:, :half], value[:, half:]
    mine_out[...] = jnp.where(early, left, right)
    theirs_out[...] = jnp.where(early, right, left)


def norm_scale(values):
    return lax.rsqrt(jnp.mean(values * values, axis=-1, keepdims=True) + EPS)


def norm_back(values, scale, gain, grad):
    weighted = grad * gain
    coupling = jnp.mean(weighted * values, axis=-1, keepdims=True)
    return scale * weighted - values * (scale * scale * scale * coupling)


def rotate(flat, cosine, sine):
    width = flat.shape[1]
    half = HEAD_DIM // 2
    lane = lax.broadcasted_iota(jnp.int32, flat.shape, 1) % HEAD_DIM
    partner = jnp.where(
        lane < half, pltpu.roll(flat, width - half, 1), pltpu.roll(flat, half, 1)
    )
    return flat * cosine + partner * sine


def key_tables(cosine, sine):
    lane = lax.broadcasted_iota(jnp.int32, cosine.shape, 1)
    is_key = lane < cosine.shape[1] // 2
    return jnp.where(is_key, cosine, 1.0), jnp.where(is_key, sine, 0.0)


def qkv_copies(wq, wk, wv, q_buf, kv_buf, sem):
    kv = wk[0].shape[1]
    return [
        (wq[0].at[0], wq[1].at[0], q_buf, sem.at[0]),
        (wk[0].at[0], wk[1].at[0], kv_buf.at[pl.ds(0, kv)], sem.at[1]),
        (wv[0].at[0], wv[1].at[0], kv_buf.at[pl.ds(kv, kv)], sem.at[2]),
    ]


def norm_qkv(layer, first, ins, outs, q_buf, kv_buf, sem):
    gain, cosine, sine = ins[:3]
    wq, wk, wv = ins[3:5], ins[5:7], ins[7:9]
    query_out, kv_out, normed_out = outs[:3]
    copies = qkv_copies(wq, wk, wv, q_buf, kv_buf, sem)
    fetch(layer, copies)
    if first:
        hidden = ins[9][...].astype(F32)
    else:
        low = (ins[9][...] + summed(ins[10:])).astype(BF)
        outs[3][...] = low
        outs[3].send()
        hidden = low.astype(F32)
    normed = (hidden * norm_scale(hidden) * gain[...]).astype(BF)
    normed_out[...] = normed
    normed_out.send()
    cos, sin = cosine[...], sine[...]
    key_cos, key_sin = key_tables(cos, sin)
    for own, _, buffer, one in copies:
        arrived(own, buffer, one)
    kv_out[...] = rotate(dot_t(normed, kv_buf[...]), key_cos, key_sin).astype(BF)
    kv_out.send()
    query_out[...] = rotate(dot(normed, q_buf[...]), cos, sin).astype(BF)


def split_keys(kv_refs, k_buf, v_buf):
    groups = k_buf.shape[0]
    rows = k_buf.shape[1] // len(kv_refs)
    for index, ref in enumerate(kv_refs):
        block = ref[...]
        for group in range(groups):
            low = group * HEAD_DIM
            k_buf[group, index * rows : (index + 1) * rows, :] = block[:, low : low + HEAD_DIM]
            low = (groups + group) * HEAD_DIM
            v_buf[group, index * rows : (index + 1) * rows, :] = block[:, low : low + HEAD_DIM]


def attention(layer, peers, ins, outs, q_buf, k_buf, v_buf, wo_buf, sem):
    wo, wo_other, query, bias = ins[:4]
    kv_refs = ins[4:]
    mine_out, theirs_out, attn_out, lse_out = outs[:4]
    fetch(layer, [(wo.at[0], wo_other.at[0], wo_buf, sem)])
    heads = q_buf.shape[0]
    group_size = heads // k_buf.shape[0]
    split_query(query[...], q_buf)
    split_keys(kv_refs, k_buf, v_buf)
    results, totals = [], []
    for head in range(heads):
        group = head // group_size
        scores = dot_t(q_buf[head], k_buf[group]) * FACTOR + bias[...]
        top = jnp.max(scores, axis=-1, keepdims=True)
        weights = jnp.exp(scores - top)
        total = jnp.sum(weights, axis=-1, keepdims=True)
        totals.append(top + jnp.log(total))
        chances = (weights * (1.0 / total)).astype(BF)
        results.append(dot(chances, v_buf[group]))
    attn = jnp.concatenate(results, axis=1)
    attn_out[...] = attn
    attn_out.send()
    lse_out[...] = jnp.concatenate(totals, axis=1)
    rows = attn.astype(BF)
    store_halves(rows, mine_out, theirs_out)
    arrived(wo.at[0], wo_buf, sem)
    store_chunks(dot(rows, wo_buf[...]), outs[4:])


def split_query(query, q_buf):
    for head in range(q_buf.shape[0]):
        q_buf[head] = query[:, head * HEAD_DIM : (head + 1) * HEAD_DIM]


def mlp_copies(wg, wu, wd, g_buf, u_buf, d_buf, sem):
    copies = []
    for step in range(g_buf.shape[0]):
        part = pl.ds(step * TILE, TILE)
        copies.append((wg[0].at[0, :, part], wg[1].at[0, :, part], g_buf.at[step], sem.at[0, step]))
        copies.append((wu[0].at[0, :, part], wu[1].at[0, :, part], u_buf.at[step], sem.at[1, step]))
        copies.append((wd[0].at[0, part, :], wd[1].at[0, part, :], d_buf.at[step], sem.at[2, step]))
    return copies


def mlp(layer, ins, outs, g_buf, u_buf, d_buf, total, act_buf, sem):
    wg, wu, wd = ins[0:2], ins[2:4], ins[4:6]
    hidden, gain = ins[6:8]
    middle_out, normed_out, gate_out, up_out, mine_out, theirs_out = outs[:6]
    copies = mlp_copies(wg, wu, wd, g_buf, u_buf, d_buf, sem)
    fetch(layer, copies[:AHEAD])
    middle = hidden[...].astype(F32) + summed(ins[8:])
    middle_out[...] = middle
    middle_out.send()
    normed_out[...] = (middle * norm_scale(middle) * gain[...]).astype(BF)
    normed_out.send()
    for step in range(g_buf.shape[0]):
        if len(copies) > 3 * step + AHEAD:
            fetch(layer, copies[3 * step + AHEAD : 3 * step + 3 + AHEAD])
        for own, _, buffer, one in copies[3 * step : 3 * step + 3]:
            arrived(own, buffer, one)
        part = slice(step * TILE, (step + 1) * TILE)
        gate = dot(normed_out[...], g_buf[step])
        upward = dot(normed_out[...], u_buf[step])
        gate_out[:, part] = gate
        up_out[:, part] = upward
        act = (gate * jax.nn.sigmoid(gate) * upward).astype(BF)
        gate_out.send((slice(None), part))
        up_out.send((slice(None), part))
        act_buf[:, part] = act
        term = dot(act, d_buf[step])
        if step == 0:
            total[...] = term
        else:
            total[...] += term
    store_halves(act_buf[...], mine_out, theirs_out)
    theirs_out.send()
    mine_out.send()
    store_chunks(total[...], outs[6:])


def mlp_back(layer, last, ins, outs, g_buf, u_buf, d_buf, total, sem):
    wg, wu, wd = ins[0:2], ins[2:4], ins[4:6]
    gate_ref, up_ref = ins[6:8]
    mine_out, theirs_out = outs[:2]
    chunks = outs[2 : 2 + CHUNKS]
    copies = mlp_copies(wg, wu, wd, g_buf, u_buf, d_buf, sem)
    fetch(layer, copies[:AHEAD])
    early = lax.axis_index("section") == 0
    if last:
        grad_ref = ins[8]
    else:
        middle_grad, hidden, gain = ins[8:11]
        grad_ref, gain_out = outs[2 + CHUNKS :]
        values, grad = hidden[...].astype(F32), summed(ins[11:])
        scale = norm_scale(values)
        gain_out[...] = jnp.sum(grad * values * scale, axis=0, keepdims=True)
        grad_ref[...] = (middle_grad[...] + norm_back(values, scale, gain[...], grad)).astype(BF)
        grad_ref.send()
    for step in range(g_buf.shape[0]):
        if len(copies) > 3 * step + AHEAD:
            fetch(layer, copies[3 * step + AHEAD : 3 * step + 3 + AHEAD])
        for own, _, buffer, one in copies[3 * step : 3 * step + 3]:
            arrived(own, buffer, one)
        part = slice(step * TILE, (step + 1) * TILE)
        act_grad = dot_t(grad_ref[...], d_buf[step])
        gate, upward = gate_ref[:, part], up_ref[:, part]
        sigma = jax.nn.sigmoid(gate)
        gate_grad = (act_grad * upward * sigma * (1.0 + gate * (1.0 - sigma))).astype(BF)
        up_grad = (act_grad * gate * sigma).astype(BF)
        mine_out[:, part] = jnp.where(early, gate_grad, up_grad)
        theirs_out[:, part] = jnp.where(early, up_grad, gate_grad)
        theirs_out.send((slice(None), part))
        mine_out.send((slice(None), part))
        term = dot_t(gate_grad, g_buf[step]) + dot_t(up_grad, u_buf[step])
        if step == 0:
            total[...] = term
        else:
            total[...] += term
    store_chunks(total[...], chunks)


def attention_back(layer, peers, ins, outs, q_buf, k_buf, v_buf, dk_buf, dv_buf, wo_buf, sem):
    wo, wo_other, grad_in, middle, gain, query, bias, attn, lse, cosine, sine = ins[:11]
    kv_refs, sums = ins[11 : 11 + peers], ins[11 + peers :]
    middle_grad_out, low_out, gain_out, pre_out = outs[:4]
    block_outs = outs[4:]
    fetch(layer, [(wo.at[0], wo_other.at[0], wo_buf, sem)])
    heads, groups = q_buf.shape[0], k_buf.shape[0]
    group_size = heads // groups
    grad = summed(sums)
    values = middle[...]
    scale = norm_scale(values)
    gain_out[...] = jnp.sum(grad * values * scale, axis=0, keepdims=True)
    middle_grad = grad_in[...].astype(F32) + norm_back(values, scale, gain[...], grad)
    middle_grad_out[...] = middle_grad
    middle_grad_out.send()
    low_out[...] = middle_grad.astype(BF)
    low_out.send()
    arrived(wo.at[0], wo_buf, sem)
    attn_grad = dot_t(low_out[...], wo_buf[...]).astype(BF)
    split_query(query[...], q_buf)
    split_keys(kv_refs, k_buf, v_buf)
    query_grads = []
    for head in range(heads):
        group = head // group_size
        lanes = slice(head * HEAD_DIM, (head + 1) * HEAD_DIM)
        head_grad = attn_grad[:, lanes]
        delta = jnp.sum(head_grad.astype(F32) * attn[:, lanes], axis=-1, keepdims=True)
        scores = dot_t(q_buf[head], k_buf[group]) * FACTOR + bias[...]
        chances = jnp.exp(scores - lse[:, head : head + 1])
        chance_grad = dot_t(head_grad, v_buf[group])
        score_grad = (chances * (chance_grad - delta) * FACTOR).astype(BF)
        query_grads.append(dot(score_grad, k_buf[group]))
        key_term = outer(score_grad, q_buf[head])
        value_term = outer(chances.astype(BF), head_grad)
        if head % group_size == 0:
            dk_buf[group] = key_term
            dv_buf[group] = value_term
        else:
            dk_buf[group] += key_term
            dv_buf[group] += value_term
    rows = middle_grad.shape[0]
    for index in reversed(range(peers)):
        span = slice(index * rows, (index + 1) * rows)
        block = jnp.concatenate(
            [dk_buf[group, span, :] for group in range(groups)]
            + [dv_buf[group, span, :] for group in range(groups)],
            axis=1,
        )
        block_outs[index][...] = block if index == 0 else block.astype(BF)
        block_outs[index].send()
    query_grad = jnp.concatenate(query_grads, axis=1)
    pre_out[...] = rotate(query_grad, cosine[...], -sine[...]).astype(BF)


def qkv_back(layer, ins, outs, q_buf, kv_buf, sem):
    wq, wk, wv = ins[0:2], ins[2:4], ins[4:6]
    pre_query, cosine, sine, own = ins[6:10]
    mine_out, theirs_out = outs[:2]
    copies = qkv_copies(wq, wk, wv, q_buf, kv_buf, sem)
    fetch(layer, copies)
    both = own[...]
    for ref in ins[10:]:
        both = both + ref[...].astype(F32)
    key_cos, key_sin = key_tables(cosine[...], sine[...])
    pre = rotate(both, key_cos, -key_sin).astype(BF)
    early = lax.axis_index("section") == 0
    pre_q = pre_query[...]
    mine_out[...] = jnp.where(early, pre_q, pre)
    theirs_out[...] = jnp.where(early, pre, pre_q)
    theirs_out.send()
    mine_out.send()
    for own_weight, _, buffer, one in copies:
        arrived(own_weight, buffer, one)
    store_chunks(dot_t(pre_q, q_buf[...]) + dot(pre, kv_buf[...]), outs[2:])


def finish(ins, outs):
    middle_grad, hidden, gain = ins[:3]
    values, grad = hidden[...].astype(F32), summed(ins[3:])
    scale = norm_scale(values)
    outs[0][...] = (middle_grad[...] + norm_back(values, scale, gain[...], grad)).astype(BF)
    outs[0].send()
    outs[1][...] = jnp.sum(grad * values * scale, axis=0, keepdims=True)


def grad_blocks(spread, ins, outs, *scratch):
    buffer = scratch[0] if spread else outs[0]
    peers = len(outs) if spread else outs[0].buffer.shape[0]
    me = lax.axis_index("dp")
    start = 0
    for left, left_other, right, right_other in zip(*[iter(ins)] * 4):
        wide, wide_other = right[...], right_other[...]
        size = left.buffer.shape[1] // peers
        lanes = slice(start, start + wide.shape[1])
        for block in range(peers):
            span = slice(block * size, (block + 1) * size)
            term = outer(left[:, span], wide) + outer(left_other[:, span], wide_other)
            place = lax.bitwise_xor(me, block) if spread else block
            buffer[place, :, lanes] = term.astype(BF)
        start += wide.shape[1]
    if spread:
        for index, out in enumerate(outs):
            out[...] = buffer[index]
            out.send()


def add_blocks(ins, outs):
    total = ins[0][...].astype(F32)
    for block in ins[1:]:
        total = total + block[...].astype(F32)
    outs[0][...] = total.astype(BF)


def grad_parts(kept, received):
    early = lax.axis_index("section") == 0

    def halves(lanes):
        own, other = kept[:, lanes].astype(F32), received[:, lanes].astype(F32)
        return jnp.where(early, own, other), jnp.where(early, other, own)

    return halves


def mlp_grads(ins, outs):
    halves = grad_parts(*ins)
    gate_out, up_out, down_out = outs
    ff = gate_out.buffer.shape[1]
    gate, upward = halves(slice(0, ff))
    gate_out[...] = gate
    gate_out.send()
    up_out[...] = upward
    up_out.send()
    half = ff // 2
    for index, part in enumerate(halves(slice(ff, ff + half))):
        down_out[index * half : (index + 1) * half, :] = part.T


def head_grads(ins, outs):
    halves = grad_parts(*ins)
    out_out, query_out, key_out, value_out = outs
    half = out_out.buffer.shape[0] // 2
    for index, part in enumerate(halves(slice(0, half))):
        out_out[index * half : (index + 1) * half, :] = part.T
    query, key_value = halves(slice(half, 3 * half))
    query_out[...] = query
    flipped = key_value.T
    key_out[...] = flipped[:half]
    value_out[...] = flipped[half:]


def copy_body(ins, outs):
    outs[0][...] = ins[0][...]


def held(value, after):
    (out,) = kernel_call(
        copy_body, "held", far([value]), near([shape(value.shape, value.dtype)]), after=after
    )
    return out


def add_rounded(ins, outs):
    outs[0][...] = (ins[0][...].astype(F32) + ins[1][...].astype(F32)).astype(BF)


def add(left, right, after=()):
    (out,) = kernel_call(
        add_rounded, "add", near([left, right]), near([shape(left.shape, BF)]), after=after, cost=0.2
    )
    return out


def hop_in(parts):
    return [lax.ppermute(part, "tensor", [(0, 1), (3, 2)]) for part in parts]


def hop_across(parts):
    return [lax.ppermute(part, "tensor", [(1, 2), (2, 1)]) for part in parts]


def hop_out(parts):
    return [lax.ppermute(part, "tensor", [(1, 0), (2, 3)]) for part in parts]


def add_all(parts, others, after=()):
    return [add(part, other, after) for part, other in zip(parts, others)]


def sum_tensor(parts):
    pairs = add_all(parts, hop_in(parts))
    totals = add_all(pairs, hop_across(pairs))
    return [piece for both in zip(totals, hop_out(totals)) for piece in both]


def layout(lengths, token_count):
    seq_ends = jnp.cumsum(lengths)
    starts = seq_ends - lengths
    places = jnp.arange(token_count, dtype=jnp.int32)
    segment = jnp.sum((places[:, None] >= seq_ends[None, :]).astype(jnp.int32), axis=1)
    labels = jnp.arange(lengths.shape[0], dtype=jnp.int32)
    offset = jnp.sum(jnp.where(segment[:, None] == labels[None, :], starts[None, :], 0), axis=1)
    return (segment, places - offset)


def rope_tables(position, heads):
    halfway = HEAD_DIM // 2
    inverse = THETA ** (-2.0 * jnp.arange(halfway, dtype=F32) / HEAD_DIM)
    angles = position.astype(F32)[:, None] * inverse[None, :]
    cosine, sine = jnp.cos(angles), jnp.sin(angles)
    return (
        jnp.tile(jnp.concatenate([cosine, cosine], axis=-1), (1, heads)),
        jnp.tile(jnp.concatenate([-sine, sine], axis=-1), (1, heads)),
    )


def peer_pairs(peers, step, later):
    pairs = [(low, low ^ step) for low in range(peers) if low < low ^ step]
    return [(high, low) for low, high in pairs] if later else pairs


def per_device(
    layer_input,
    seq_lengths,
    norm1_gain,
    w_query,
    w_key,
    w_value,
    w_out,
    norm2_gain,
    w_gate,
    w_up,
    w_down,
    out_grad,
):
    Order.token = ()
    rows, width = layer_input.shape[1:]
    peers = lax.axis_size("dp")
    me = lax.axis_index("dp")
    first = lax.axis_index("section") == 0
    q_width, kv_width, ff = w_query.shape[2], w_key.shape[2], w_gate.shape[2]
    heads, groups = q_width // HEAD_DIM, kv_width // HEAD_DIM
    tokens = rows * peers
    steps = ff // TILE
    part = width // CHUNKS

    def pick(early, late):
        return jnp.where(first, early, late)

    own = [w_query, jnp.swapaxes(w_key, 1, 2), jnp.swapaxes(w_value, 1, 2), w_out, w_gate, w_up, w_down]
    pairs = [(weight, swap(weight)) for weight in own]
    wq, wk, wv, wo, wg, wu, wd = pairs
    gains = []
    for gain in (norm1_gain, norm2_gain):
        other = swap(gain)
        gains.append((pick(gain, other), pick(other, gain)))

    segment, position = layout(pick(seq_lengths[0], seq_lengths[1]), tokens)
    row_seg = lax.dynamic_slice_in_dim(segment, me * rows, rows, 0)
    row_pos = lax.dynamic_slice_in_dim(position, me * rows, rows, 0)
    local = jnp.arange(rows, dtype=jnp.int32)
    key_place = jnp.concatenate([(me ^ step) * rows + local for step in range(peers)])
    key_seg = jnp.concatenate(
        [lax.dynamic_slice_in_dim(segment, (me ^ step) * rows, rows, 0) for step in range(peers)]
    )
    allowed = (row_seg[:, None] == key_seg[None, :]) & (
        key_place[None, :] <= (me * rows + local)[:, None]
    )
    bias = jnp.where(allowed, 0.0, MASKED).astype(F32)
    cosine, sine = rope_tables(row_pos, heads)

    chunk_outs = near([shape((rows, part), BF)] * CHUNKS)
    row_f32 = shape((rows, width), F32)
    row_bf = shape((rows, width), BF)
    line = shape((1, width), F32)
    head_bf = shape((rows, q_width), BF)
    half_head = shape((rows, q_width // 2), BF)
    half_wide = shape((rows, ff // 2), BF)
    kv_bf = shape((rows, 2 * kv_width), BF)
    wide_f32 = shape((rows, ff), F32)
    wide_bf = shape((rows, ff), BF)
    dma = pltpu.SemaphoreType.DMA
    qkv_scratch = [
        pltpu.VMEM((width, q_width), BF),
        pltpu.VMEM((2 * kv_width, width), BF),
        dma((3,)),
    ]
    mlp_scratch = [
        pltpu.VMEM((steps, width, TILE), BF),
        pltpu.VMEM((steps, width, TILE), BF),
        pltpu.VMEM((steps, TILE, width), BF),
        pltpu.VMEM((rows, width), F32),
        dma((3, steps)),
    ]
    head_scratch = [
        pltpu.VMEM((heads, rows, HEAD_DIM), BF),
        pltpu.VMEM((groups, tokens, HEAD_DIM), BF),
        pltpu.VMEM((groups, tokens, HEAD_DIM), BF),
    ]

    def run_qkv(layer, source, sums):
        start = layer == 0
        outs = [head_bf, kv_bf, row_bf]
        return kernel_call(
            functools.partial(norm_qkv, layer, start),
            f"norm_qkv_{layer}",
            far([gains[0][layer], cosine, sine]) + weights([wq, wk, wv]) + far([source]) + near(sums),
            far(outs if start else outs + [row_bf]),
            qkv_scratch,
            cost=4.0,
        )

    def run_attention(layer, query, blocks):
        outs = [half_head] * 2 + [shape((rows, q_width), F32), shape((rows, heads), F32)]
        return kernel_call(
            functools.partial(attention, layer, peers),
            f"attention_{layer}",
            weights([wo]) + far([query, bias, *blocks]),
            far(outs) + chunk_outs,
            head_scratch + [pltpu.VMEM((q_width, width), BF), dma],
            cost=5.0,
            limit=min(8 + 4 * peers, 56),
        )

    def run_mlp(layer, hidden, sums):
        return kernel_call(
            functools.partial(mlp, layer),
            f"mlp_{layer}",
            weights([wg, wu, wd]) + far([hidden, gains[1][layer]]) + near(sums),
            far([row_f32, row_bf, wide_f32, wide_f32, half_wide, half_wide])
            + (chunk_outs if layer == 0 else far([row_bf])),
            mlp_scratch[:-1] + [pltpu.VMEM((rows, ff), BF)] + mlp_scratch[-1:],
            cost=6.0,
            limit=32,
        )

    def run_mlp_back(layer, source, sums, gate, upward, after):
        last = layer == 1
        outs = far([wide_bf, wide_bf]) + chunk_outs
        return kernel_call(
            functools.partial(mlp_back, layer, last),
            f"mlp_back_{layer}",
            weights([wg, wu, wd]) + far([gate, upward, *source]) + near(sums),
            outs if last else outs + far([row_bf, line]),
            mlp_scratch,
            after,
            cost=8.0,
            limit=32,
        )

    def run_attention_back(layer, grad, middle, sums, query, blocks, attn, lse, after):
        return kernel_call(
            functools.partial(attention_back, layer, peers),
            f"attention_back_{layer}",
            weights([wo])
            + far([grad, middle, gains[1][layer], query, bias, attn, lse, cosine, sine, *blocks])
            + near(sums),
            far([row_f32, row_bf, line, head_bf, shape((rows, 2 * kv_width), F32)] + [kv_bf] * (peers - 1)),
            head_scratch
            + [
                pltpu.VMEM((groups, tokens, HEAD_DIM), F32),
                pltpu.VMEM((groups, tokens, HEAD_DIM), F32),
                pltpu.VMEM((q_width, width), BF),
                dma,
            ],
            after,
            cost=9.0,
            limit=min(16 + 4 * peers, 56),
        )

    def run_qkv_back(layer, pre_query, pieces, after):
        return kernel_call(
            functools.partial(qkv_back, layer),
            f"qkv_back_{layer}",
            weights([wq, wk, wv]) + far([pre_query, cosine, sine]) + loose(pieces),
            far([kv_bf, kv_bf]) + chunk_outs,
            qkv_scratch,
            after,
            cost=4.0,
        )

    def weight_grad(groups, name, spread):
        ins, tall = [], 0
        for left, left_other, mine, mine_other in groups:
            ins += far([left]) + loose([left_other]) + far([mine]) + loose([mine_other])
            tall += mine.shape[1]
        block = shape((width // peers, tall), BF)
        whole = shape((peers, width // peers, tall), BF)
        blocks = kernel_call(
            functools.partial(grad_blocks, spread),
            name,
            ins,
            far([block] * peers if spread else [whole]),
            [pltpu.VMEM(whole.shape, BF)] if spread else [],
            cost=8.0,
        )
        if not spread:
            return blocks, lax.psum_scatter(blocks[0], "dp", scatter_dimension=0, tiled=False)
        pieces = [blocks[0]]
        for step in range(1, peers):
            pairing = [(peer, peer ^ step) for peer in range(peers)]
            pieces.append(lax.ppermute(blocks[step], "dp", pairing))

        def total():
            return kernel_call(
                add_blocks, "add_" + name, far(pieces[:1]) + loose(pieces[1:]), far([block])
            )[0]

        return blocks, total

    def whole_grads(body, name, per_layer, dims):
        kept = pick(per_layer[0], per_layer[1])
        received = swap(pick(per_layer[1], per_layer[0]))
        return kernel_call(
            body, name, loose([kept, received]), far([shape(dim, F32) for dim in dims]), cost=4.0
        )

    def by_layer(per_layer):
        received = swap(pick(per_layer[1], per_layer[0]))
        kept = pick(per_layer[0], per_layer[1])
        return jnp.stack([pick(kept, received), pick(received, kept)])[None]

    hidden = pick(layer_input[0], layer_input[1])
    grad = pick(out_grad[0], out_grad[1])
    saved, outputs = [], []
    for layer in range(2):
        if layer == 0:
            query, kv, normed_one = run_qkv(layer, hidden, [])
        else:
            query, kv, normed_one, hidden = run_qkv(layer, middle, sums)
            outputs.append(hidden)
        blocks = [kv]
        for step in range(1, peers):
            blocks.append(lax.ppermute(kv, "dp", peer_pairs(peers, step, False)))
        *head_halves, attn, lse, chunk_one, chunk_two = run_attention(layer, query, blocks)
        sums = sum_tensor([chunk_one, chunk_two])
        middle, normed_two, gate, upward, act_mine, act_theirs, *parts = run_mlp(
            layer, hidden, sums
        )
        act_halves = [act_mine, act_theirs]
        if layer == 0:
            sums = sum_tensor(parts)
        saved.append(
            (hidden, query, blocks, normed_one, head_halves, attn, lse)
            + (middle, normed_two, gate, upward, act_halves)
        )

    last_middle, last_part = middle, parts[0]
    in_grads, vectors, mlp_parts, head_parts = [None, None], [None, None], [None, None], [None, None]
    source, sums = [grad], []
    for layer in (1, 0):
        (hidden, query, blocks, normed_one, head_halves, attn, lse) = saved[layer][:7]
        (middle, normed_two, gate, upward, act_halves) = saved[layer][7:]
        if layer == 1:
            mine, theirs, *parts = run_mlp_back(layer, source, sums, gate, upward, [])
        else:
            mine, theirs, *parts, grad, gain_one = run_mlp_back(
                layer, source, sums, gate, upward, []
            )
            in_grads[1] = grad
        inward = hop_in(parts)
        mlp_blocks, mlp_parts[layer] = weight_grad(
            [
                (normed_two, swap(normed_two), mine, swap(theirs)),
                (grad, swap(grad), act_halves[0], swap(act_halves[1])),
            ],
            f"grad_mlp_{layer}",
            False,
        )
        pairs = add_all(parts, inward)
        totals = add_all(pairs, hop_across(pairs))
        outward = hop_out(totals)
        sums = [piece for both in zip(totals, outward) for piece in both]
        if layer == 1:
            last_part = held(last_part, [])
            (last_inward,) = hop_in([last_part])
        else:
            last_total = add(last_pair, last_across)
            (last_outward,) = hop_out([last_total])
        middle_grad, low, gain_two, pre_query, *pieces = run_attention_back(
            layer, grad, middle, sums, query, blocks, attn, lse, []
        )
        far_pieces = [
            lax.ppermute(pieces[step], "dp", peer_pairs(peers, step, True))
            for step in range(1, peers)
        ]
        if layer == 1:
            last_pair = add(last_part, last_inward)
            (last_across,) = hop_across([last_pair])
        mine, theirs, *parts = run_qkv_back(layer, pre_query, [pieces[0]] + far_pieces, [])
        inward = hop_in(parts)
        head_blocks, head_parts[layer] = weight_grad(
            [
                (low, swap(low), head_halves[0], swap(head_halves[1])),
                (normed_one, swap(normed_one), mine, swap(theirs)),
            ],
            f"grad_head_{layer}",
            layer == 0,
        )
        pairs = add_all(parts, inward)
        totals = add_all(pairs, hop_across(pairs))
        outward = hop_out(totals)
        sums = [piece for both in zip(totals, outward) for piece in both]
        source = [middle_grad, hidden, gains[0][layer]]
        vectors[layer] = gain_two
    in_grads[0], last_line = kernel_call(
        finish, "finish", far(source) + near(sums), far([row_bf, line])
    )
    lines = jnp.concatenate([last_line, vectors[0], gain_one, vectors[1]], axis=0)
    for axis in ("section", "dp"):
        for bit in range((lax.axis_size(axis) - 1).bit_length()):
            pairing = [(peer, peer ^ (1 << bit)) for peer in range(lax.axis_size(axis))]
            lines = lines + lax.ppermute(lines, axis, pairing)

    at_middle = (lax.axis_index("tensor") == 1) | (lax.axis_index("tensor") == 2)
    last_sum = jnp.where(at_middle, last_total, last_outward)
    outputs.append((last_middle + last_sum.astype(F32)).astype(BF))
    activations = by_layer(outputs)
    input_grads = by_layer(in_grads)
    size = width // peers
    head_parts[0] = head_parts[0]()
    grad_gate, grad_up, grad_down = whole_grads(
        mlp_grads, "mlp_grads", mlp_parts, [(size, ff), (size, ff), (ff, size)]
    )
    grad_out, grad_query, grad_key, grad_value = whole_grads(
        head_grads,
        "head_grads",
        head_parts,
        [(q_width, size), (size, q_width), (kv_width, size), (kv_width, size)],
    )
    grad_key, grad_value = grad_key.T, grad_value.T
    lines = lax.dynamic_slice_in_dim(lines, me * size, size, 1)
    return (
        activations,
        input_grads,
        pick(lines[0], lines[2])[None],
        grad_query[None],
        grad_key[None],
        grad_value[None],
        grad_out[None],
        pick(lines[1], lines[3])[None],
        grad_gate[None],
        grad_up[None],
        grad_down[None],
    )


def solution(mesh):
    placed = (
        P(None, "dp", None),
        P(),
        P("section", None),
        P("section", None, "tensor"),
        P("section", None, "tensor"),
        P("section", None, "tensor"),
        P("section", "tensor", None),
        P("section", None),
        P("section", None, "tensor"),
        P("section", None, "tensor"),
        P("section", "tensor", None),
        P(None, "dp", None),
    )
    return jax.shard_map(
        per_device,
        mesh=mesh,
        in_specs=placed,
        out_specs=(
            P("section", None, "dp", None),
            P("section", None, "dp", None),
            P("section", "dp"),
            P("section", "dp", "tensor"),
            P("section", "dp", "tensor"),
            P("section", "dp", "tensor"),
            P("section", "tensor", "dp"),
            P("section", "dp"),
            P("section", "dp", "tensor"),
            P("section", "dp", "tensor"),
            P("section", "tensor", "dp"),
        ),
        check_vma=False,
    )
```

time: 1200 us -> 590 us (0.49)
  blocking collectives: 300 us -> 0 us
  waiting for transfers between devices: 527 us -> 295 us
  matrix products: 165 us -> 0 us
  Pallas kernels: 0 us -> 126 us
  starting transfers between devices: 8.22 us -> 109 us
  other arithmetic: 94.5 us -> 19.1 us
  local copies, waits for them, and re-layouts: 72.1 us -> 15 us
    reduce_scatter x21 -> x0, waiting for transfers between devices: 460 us -> none  [the longest x3 72.7 us: forward_layer(): lax.psum_scatter(product(hidden_act, down_weight).astype(jnp.bfloat16), '...]
    all_gather x18 -> x0, blocking collectives: 291 us -> none  [the longest x3 55.9 us: forward_layer(): output = lax.all_gather(out_share, 'tensor', axis=0, tiled=True)]
    ppermute x4 -> x92, waiting for transfers between devices: 4.5 us -> 294 us  [the longest x15 169 us: hop_out(): return [lax.ppermute(part, 'tensor', [(1, 0), (2, 3)]) for part in parts]]
    dot_general x84 -> x0, matrix products: 165 us -> none  [the longest x42 64.1 us: product(): return jnp.dot(left, right, preferred_element_type=jnp.float32)]
    pallas_call x0 -> x51, Pallas kernels: none -> 126 us  [kernel_call(): results = call(*[fixed(value, where) for value, where in [*ins, *after]])]
    ppermute x4 -> x92, starting transfers between devices: 6.4 us -> 109 us  [the longest x15 40 us: hop_in(): return [lax.ppermute(part, 'tensor', [(0, 1), (3, 2)]) for part in parts]]
    unnamed x31 -> x6, waiting for transfers between devices: 62.9 us -> 0.77 us
    unnamed x449 -> x68, local copies, waits for them, and re-layouts: 48.9 us -> 7.02 us
  transfers between devices with their start and end apart: 30 -> 95, of which waited for: 25 -> 39; matrix products, arithmetic and copies ran while one was open for 14% -> 4% of each run, Pallas kernels for 0% -> 17%
where the time goes in v1:
time: 590 us; the launch traced here: 580 us
  waiting for transfers between devices  295 us (50%)
  Pallas kernels  126 us (21%)
  starting transfers between devices  109 us (18%)
  other arithmetic  19.1 us (3%)
  between operations  15.5 us (3%)
  local copies, waits for them, and re-layouts  15 us (3%)
    ppermute x15, waiting for transfers between devices, hop_out(): return [lax.ppermute(part, 'tensor', [(1, 0), (2, 3)]) for part in parts]  169 us
    pallas_call x51, Pallas kernels, kernel_call(): results = call(*[fixed(value, where) for value, where in [*ins, *after]])  126 us
    ppermute x15, waiting for transfers between devices, hop_in(): return [lax.ppermute(part, 'tensor', [(0, 1), (3, 2)]) for part in parts]  82 us
    ppermute x15, starting transfers between devices, hop_in(): return [lax.ppermute(part, 'tensor', [(0, 1), (3, 2)]) for part in parts]  40 us
    ppermute x15, starting transfers between devices, hop_out(): return [lax.ppermute(part, 'tensor', [(1, 0), (2, 3)]) for part in parts]  20.8 us
    ppermute x6, waiting for transfers between devices, per_device(): lax.ppermute(pieces[step], 'dp', peer_pairs(peers, step, True))  20.6 us
    ppermute x6, starting transfers between devices, per_device(): blocks.append(lax.ppermute(kv, 'dp', peer_pairs(peers, step, False)))  20.3 us
    ppermute x6, waiting for transfers between devices, per_device(): blocks.append(lax.ppermute(kv, 'dp', peer_pairs(peers, step, False)))  12.6 us
  transfers between devices with their start and end apart: 95, of which 39 were waited for; matrix products, arithmetic and copies ran while one was open for 4% of the time, Pallas kernels for 17%

profile of v1, /device:TPU:0, one launch (start us, length us, event | category | flops | bytes accessed | tf_op | source)
XLA Modules:
  0.0 580.1 jit_solution(14591776866382094393)
XLA Ops:
  29.2 6.6 %collective-permute-done.10.refs_6_.refs_13_ = bf16[256,384]{1,0:T(8,128)(2,1)S(1)} collective-permute-done((bf16[256,384]{1,0:T(8,128)(2,1)}, bf16[256,384]{1,0:T(8,128)(2,1)S(1)}, u32[]{:S(2)}, u32[]{:S(2)}) %collective-permute-start.10) | collective-permute-done | bytes 196640 | tf_op jit(solution)/shard_map/ppermute | solution.py:828
  54.7 8.2 %collective-permute-done.12.refs_1_ = bf16[256,768]{1,0:T(8,128)(2,1)S(1)} collective-permute-done((bf16[256,768]{1,0:T(8,128)(2,1)S(1)}, bf16[256,768]{1,0:T(8,128)(2,1)S(1)}, u32[]{:S(2)}, u32[]{:S(2)}) %collective-permute-start.12) | collective-permute-done | bytes 393248 | tf_op jit(solution)/shard_map/ppermute | solution.py:569
  72.8 27.6 %collective-permute-done.17.refs_11_ = bf16[256,768]{1,0:T(8,128)(2,1)S(1)} collective-permute-done((bf16[256,768]{1,0:T(8,128)(2,1)S(1)}, bf16[256,768]{1,0:T(8,128)(2,1)S(1)}, u32[]{:S(2)}, u32[]{:S(2)}) %collective-permute-start.17) | collective-permute-done | bytes 393248 | tf_op jit(solution)/shard_map/ppermute | solution.py:577
  104.0 8.3 %mlp_0.1 = (f32[256,1536]{1,0:T(8,128)}, bf16[256,1536]{1,0:T(8,128)(2,1)}, f32[256,1024]{1,0:T(8,128)}, f32[256,1024]{1,0:T(8,128)}, bf16[256,512]{1,0:T(8,128)...) custom-call(bf16[1,1536,1024]{2,1,0:T(8,128)(2,1)} %refs_0_.17, ...), custom_call_target="tpu_custom_call" | custom-call | flops 6000000000 | tf_op jit(solution)/shard_map/mlp_0/pallas_call | solution.py:132
  115.2 8.2 %collective-permute-done.18.refs_1_ = bf16[256,768]{1,0:T(8,128)(2,1)S(1)} collective-permute-done((bf16[256,768]{1,0:T(8,128)(2,1)S(1)}, bf16[256,768]{1,0:T(8,128)(2,1)S(1)}, u32[]{:S(2)}, u32[]{:S(2)}) %collective-permute-start.18) | collective-permute-done | bytes 393248 | tf_op jit(solution)/shard_map/ppermute | solution.py:569
  131.6 22.2 %collective-permute-done.23.refs_13_ = bf16[256,768]{1,0:T(8,128)(2,1)S(1)} collective-permute-done((bf16[256,768]{1,0:T(8,128)(2,1)S(1)}, bf16[256,768]{1,0:T(8,128)(2,1)S(1)}, u32[]{:S(2)}, u32[]{:S(2)}) %collective-permute-start.23) | collective-permute-done | bytes 393248 | tf_op jit(solution)/shard_map/ppermute | solution.py:577
  200.8 17.5 %collective-permute-done.32.refs_11_ = bf16[256,768]{1,0:T(8,128)(2,1)S(1)} collective-permute-done((bf16[256,768]{1,0:T(8,128)(2,1)S(1)}, bf16[256,768]{1,0:T(8,128)(2,1)S(1)}, u32[]{:S(2)}, u32[]{:S(2)}) %collective-permute-start.32) | collective-permute-done | bytes 393248 | tf_op jit(solution)/shard_map/ppermute | solution.py:577
  218.4 8.1 %mlp_1.1 = (f32[256,1536]{1,0:T(8,128)}, bf16[256,1536]{1,0:T(8,128)(2,1)}, f32[256,1024]{1,0:T(8,128)}, f32[256,1024]{1,0:T(8,128)}, bf16[256,512]{1,0:T(8,128)...) custom-call(bf16[1,1536,1024]{2,1,0:T(8,128)(2,1)} %refs_0_.17, bf16[1,1536,1024]{2,1,0:T(8,128)(2,1)} %copy-done.16, ...), custom_call_target="tpu_custom_call" | custom-call | flops 6000000000 | tf_op jit(solution)/shard_map/mlp_1/pallas_call | solution.py:132
  226.6 10.0 %mlp_back_1.1 = (bf16[256,1024]{1,0:T(8,128)(2,1)}, bf16[256,1024]{1,0:T(8,128)(2,1)}, bf16[256,768]{1,0:T(8,128)(2,1)S(1)}, bf16[256,768]{1,0:T(8,128)(2,1)S(1)}) custom-call(bf16[1,1536,1024]{2,1,0:T(8,128)(2,1)} %refs_0_.17, bf16[1,1536,1024]{2,1,0:T(8,128)(2,1)} %copy-done.16, bf16[1,1536,1024]{2,1,0:T(8,128)(2,1)} %refs_2_.7, ...), custom_call_target="tpu_custom_call" | custom-call | flops 8000000000 | tf_op jit(solution)/shard_map/mlp_back_1/pallas_call | solution.py:132
  249.1 7.3 %collective-permute-done.33.refs_1_ = bf16[256,768]{1,0:T(8,128)(2,1)S(1)} collective-permute-done((bf16[256,768]{1,0:T(8,128)(2,1)S(1)}, bf16[256,768]{1,0:T(8,128)(2,1)S(1)}, u32[]{:S(2)}, u32[]{:S(2)}) %collective-permute-start.33) | collective-permute-done | bytes 393248 | tf_op jit(solution)/shard_map/ppermute | solution.py:569
  261.4 16.5 %collective-permute-start.41 = (bf16[256,1536]{1,0:T(8,128)(2,1)S(1)}, bf16[256,1536]{1,0:T(8,128)(2,1)S(1)}, u32[]{:S(2)}, u32[]{:S(2)}) collective-permute-start(bf16[256,1536]{1,0:T(8,128)(2,1)S(1)} %held.1.refs_19_.refs_0_), channel_id=1, source_target_pairs={{0,4},{12,8},{1,5},{13,9},{2,6},{14,10},{3,7},{15,11},{16,20},{28,... | collective-permute-start | bytes 2359304 | tf_op jit(solution)/shard_map/ppermute | solution.py:569
  283.2 6.6 %collective-permute-done.42.refs_16_ = bf16[256,768]{1,0:T(8,128)(2,1)S(1)} collective-permute-done((bf16[256,768]{1,0:T(8,128)(2,1)S(1)}, bf16[256,768]{1,0:T(8,128)(2,1)S(1)}, u32[]{:S(2)}, u32[]{:S(2)}) %collective-permute-start.42) | collective-permute-done | bytes 393248 | tf_op jit(solution)/shard_map/ppermute | solution.py:577
  289.7 10.4 %attention_back_1.1 = (f32[256,1536]{1,0:T(8,128)}, bf16[256,1536]{1,0:T(8,128)(2,1)}, f32[1,1536]{1,0:T(1,128)}, bf16[256,384]{1,0:T(8,128)(2,1)}, f32[256,384]...) custom-call(bf16[1,384,1536]{2,1,0:T(8,128)(2,1)} %refs_0_.18, ...), custom_call_target="tpu_custom_call" | custom-call | flops 8999999488 | tf_op jit(solution)/shard_map/attention_back_1/pallas_call | solution.py:132
  332.8 8.1 %collective-permute-done.48.refs_1_ = bf16[256,768]{1,0:T(8,128)(2,1)S(1)} collective-permute-done((bf16[256,768]{1,0:T(8,128)(2,1)S(1)}, bf16[256,768]{1,0:T(8,128)(2,1)S(1)}, u32[]{:S(2)}, u32[]{:S(2)}) %collective-permute-start.48) | collective-permute-done | bytes 393248 | tf_op jit(solution)/shard_map/ppermute | solution.py:569
  341.7 7.1 %collective-permute-done.54.refs_1_ = bf16[256,768]{1,0:T(8,128)(2,1)S(1)} collective-permute-done((bf16[256,768]{1,0:T(8,128)(2,1)S(1)}, bf16[256,768]{1,0:T(8,128)(2,1)S(1)}, u32[]{:S(2)}, u32[]{:S(2)}) %collective-permute-start.54) | collective-permute-done | bytes 393248 | tf_op jit(solution)/shard_map/ppermute | solution.py:569
  352.8 22.5 %collective-permute-done.57.refs_14_ = bf16[256,768]{1,0:T(8,128)(2,1)S(1)} collective-permute-done((bf16[256,768]{1,0:T(8,128)(2,1)S(1)}, bf16[256,768]{1,0:T(8,128)(2,1)S(1)}, u32[]{:S(2)}, u32[]{:S(2)}) %collective-permute-start.57) | collective-permute-done | bytes 393248 | tf_op jit(solution)/shard_map/ppermute | solution.py:577
  381.6 11.3 %mlp_back_0.1 = (bf16[256,1024]{1,0:T(8,128)(2,1)}, bf16[256,1024]{1,0:T(8,128)(2,1)}, bf16[256,768]{1,0:T(8,128)(2,1)S(1)}, bf16[256,768]{1,0:T(8,128)(2,1)S(1)...) custom-call(bf16[1,1536,1024]{2,1,0:T(8,128)(2,1)} %refs_0_.17, bf16[1,1536,1024]{2,1,0:T(8,128)(2,1)} %copy-done.16, ...), custom_call_target="tpu_custom_call" | custom-call | flops 8000000000 | tf_op jit(solution)/shard_map/mlp_back_0/pallas_call | solution.py:132
  406.5 7.4 %collective-permute-done.59.refs_1_ = bf16[256,768]{1,0:T(8,128)(2,1)S(1)} collective-permute-done((bf16[256,768]{1,0:T(8,128)(2,1)S(1)}, bf16[256,768]{1,0:T(8,128)(2,1)S(1)}, u32[]{:S(2)}, u32[]{:S(2)}) %collective-permute-start.59) | collective-permute-done | bytes 393248 | tf_op jit(solution)/shard_map/ppermute | solution.py:569
  414.7 7.0 %collective-permute-done.58.refs_1_ = bf16[256,768]{1,0:T(8,128)(2,1)S(1)} collective-permute-done((bf16[256,768]{1,0:T(8,128)(2,1)S(1)}, bf16[256,768]{1,0:T(8,128)(2,1)S(1)}, u32[]{:S(2)}, u32[]{:S(2)}) %collective-permute-start.58) | collective-permute-done | bytes 393248 | tf_op jit(solution)/shard_map/ppermute | solution.py:569
  427.2 27.7 %collective-permute-done.69.refs_18_ = bf16[256,768]{1,0:T(8,128)(2,1)S(1)} collective-permute-done((bf16[256,768]{1,0:T(8,128)(2,1)S(1)}, bf16[256,768]{1,0:T(8,128)(2,1)S(1)}, u32[]{:S(2)}, u32[]{:S(2)}) %collective-permute-start.69) | collective-permute-done | bytes 393248 | tf_op jit(solution)/shard_map/ppermute | solution.py:577
  454.9 8.4 %collective-permute-done.68.refs_16_ = bf16[256,768]{1,0:T(8,128)(2,1)S(1)} collective-permute-done((bf16[256,768]{1,0:T(8,128)(2,1)S(1)}, bf16[256,768]{1,0:T(8,128)(2,1)S(1)}, u32[]{:S(2)}, u32[]{:S(2)}) %collective-permute-start.68) | collective-permute-done | bytes 393248 | tf_op jit(solution)/shard_map/ppermute | solution.py:577
  463.3 11.2 %attention_back_0.1 = (f32[256,1536]{1,0:T(8,128)}, bf16[256,1536]{1,0:T(8,128)(2,1)}, f32[1,1536]{1,0:T(1,128)}, bf16[256,384]{1,0:T(8,128)(2,1)}, f32[256,384]...) custom-call(bf16[1,384,1536]{2,1,0:T(8,128)(2,1)} %refs_0_.18, ...), custom_call_target="tpu_custom_call" | custom-call | flops 8999999488 | tf_op jit(solution)/shard_map/attention_back_0/pallas_call | solution.py:132
  507.1 7.2 %collective-permute-done.79.refs_1_ = bf16[256,768]{1,0:T(8,128)(2,1)S(1)} collective-permute-done((bf16[256,768]{1,0:T(8,128)(2,1)S(1)}, bf16[256,768]{1,0:T(8,128)(2,1)S(1)}, u32[]{:S(2)}, u32[]{:S(2)}) %collective-permute-start.79) | collective-permute-done | bytes 393248 | tf_op jit(solution)/shard_map/ppermute | solution.py:569
  526.2 21.0 %collective-permute-done.82.refs_6_ = bf16[256,768]{1,0:T(8,128)(2,1)S(1)} collective-permute-done((bf16[256,768]{1,0:T(8,128)(2,1)S(1)}, bf16[256,768]{1,0:T(8,128)(2,1)S(1)}, u32[]{:S(2)}, u32[]{:S(2)}) %collective-permute-start.82) | collective-permute-done | bytes 393248 | tf_op jit(solution)/shard_map/ppermute | solution.py:577
  (328 shorter events, 268.1 us)
Async XLA Ops:
  7.2 508.7 %reduce-scatter.10.cloned.1.call-start = ((), (), s32[]{:S(2)}) async-start(), calls=%async_computation.3 | async-start | bytes 2211840
  15.3 85.1 %collective-permute-start.4 = (bf16[1,1536,1024]{2,1,0:T(8,128)(2,1)}, bf16[1,1536,1024]{2,1,0:T(8,128)(2,1)S(1)}, u32[]{:S(2)}, u32[]{:S(2)}) collective-permute-start(bf16[1,1536,1024]{2,1,0:T(8,128)(2,1)} %refs_0_.17), channel_id=1, source_target_pairs={{0,16},{16,0},{1,17},{17,1},{2,18},{18,2},{3,19},{19,3},{4,20},{20... | collective-permute-start | bytes 9437192 | tf_op jit(solution)/shard_map/ppermute | solution.py:35
  15.4 85.0 %collective-permute-start.5 = (bf16[1,1536,1024]{2,1,0:T(8,128)(2,1)}, bf16[1,1536,1024]{2,1,0:T(8,128)(2,1)S(1)}, u32[]{:S(2)}, u32[]{:S(2)}) collective-permute-start(bf16[1,1536,1024]{2,1,0:T(8,128)(2,1)} %refs_2_.7), channel_id=1, source_target_pairs={{0,16},{16,0},{1,17},{17,1},{2,18},{18,2},{3,19},{19,3},{4,20},{20... | collective-permute-start | bytes 9437192 | tf_op jit(solution)/shard_map/ppermute | solution.py:35
  15.8 84.6 %collective-permute-start.6 = (bf16[1,1024,1536]{2,1,0:T(8,128)(2,1)}, bf16[1,1024,1536]{2,1,0:T(8,128)(2,1)S(1)}, u32[]{:S(2)}, u32[]{:S(2)}) collective-permute-start(bf16[1,1024,1536]{2,1,0:T(8,128)(2,1)} %refs_4_.7), channel_id=1, source_target_pairs={{0,16},{16,0},{1,17},{17,1},{2,18},{18,2},{3,19},{19,3},{4,20},{20... | collective-permute-start | bytes 9437192 | tf_op jit(solution)/shard_map/ppermute | solution.py:35
  69.5 30.9 %collective-permute-start.15 = (bf16[256,768]{1,0:T(8,128)(2,1)S(1)}, bf16[256,768]{1,0:T(8,128)(2,1)S(1)}, u32[]{:S(2)}, u32[]{:S(2)}) collective-permute-start(bf16[256,768]{1,0:T(8,128)(2,1)S(1)} %add.150.refs_2_.refs_8_), channel_id=1, source_target_pairs={{4,0},{8,12},{5,1},{9,13},{6,2},{10,14},{7,3},{11,15},{20,16},{24,... | collective-permute-start | bytes 1179656 | tf_op jit(solution)/shard_map/ppermute | solution.py:577
  70.9 29.5 %collective-permute-start.17 = (bf16[256,768]{1,0:T(8,128)(2,1)S(1)}, bf16[256,768]{1,0:T(8,128)(2,1)S(1)}, u32[]{:S(2)}, u32[]{:S(2)}) collective-permute-start(bf16[256,768]{1,0:T(8,128)(2,1)S(1)} %add.151.refs_10_.refs_12_), channel_id=1, source_target_pairs={{4,0},{8,12},{5,1},{9,13},{6,2},{10,14},{7,3},{11,15},{20,16},{24,... | collective-permute-start | bytes 1179656 | tf_op jit(solution)/shard_map/ppermute | solution.py:577
  130.3 27.7 %collective-permute-start.21 = (bf16[256,768]{1,0:T(8,128)(2,1)S(1)}, bf16[256,768]{1,0:T(8,128)(2,1)S(1)}, u32[]{:S(2)}, u32[]{:S(2)}) collective-permute-start(bf16[256,768]{1,0:T(8,128)(2,1)S(1)} %add.154.refs_2_.refs_10_), channel_id=1, source_target_pairs={{4,0},{8,12},{5,1},{9,13},{6,2},{10,14},{7,3},{11,15},{20,16},{24,... | collective-permute-start | bytes 1179656 | tf_op jit(solution)/shard_map/ppermute | solution.py:577
  200.8 38.2 %collective-permute-start.37 = (bf16[256,1536]{1,0:T(8,128)(2,1)S(1)}, bf16[256,1536]{1,0:T(8,128)(2,1)S(1)}, u32[]{:S(2)}, u32[]{:S(2)}) collective-permute-start(bf16[256,1536]{1,0:T(8,128)(2,1)S(1)} %select_bitcast_fusion.6.refs_8_.refs_4_.refs_2_), channel_id=1, source_target_pairs={{0,16},{16,0},{1,17},{17,1},{2,18},{18,2},{3,19},{19,3},{4,20},{20... | collective-permute-start | bytes 2359304 | tf_op jit(solution)/shard_map/ppermute | solution.py:35
  257.5 25.6 %collective-permute-start.43 = (bf16[256,768]{1,0:T(8,128)(2,1)S(1)}, bf16[256,768]{1,0:T(8,128)(2,1)S(1)}, u32[]{:S(2)}, u32[]{:S(2)}) collective-permute-start(bf16[256,768]{1,0:T(8,128)(2,1)S(1)} %add.163.refs_1_.refs_17_), channel_id=1, source_target_pairs={{4,0},{8,12},{5,1},{9,13},{6,2},{10,14},{7,3},{11,15},{20,16},{24,... | collective-permute-start | bytes 1179656 | tf_op jit(solution)/shard_map/ppermute | solution.py:577
  258.8 30.9 %collective-permute-start.42 = (bf16[256,768]{1,0:T(8,128)(2,1)S(1)}, bf16[256,768]{1,0:T(8,128)(2,1)S(1)}, u32[]{:S(2)}, u32[]{:S(2)}) collective-permute-start(bf16[256,768]{1,0:T(8,128)(2,1)S(1)} %add.162.refs_2_.refs_15_), channel_id=1, source_target_pairs={{4,0},{8,12},{5,1},{9,13},{6,2},{10,14},{7,3},{11,15},{20,16},{24,... | collective-permute-start | bytes 1179656 | tf_op jit(solution)/shard_map/ppermute | solution.py:577
  260.1 60.6 %collective-permute-start.51 = (bf16[256,1536]{1,0:T(8,128)(2,1)S(1)}, bf16[256,1536]{1,0:T(8,128)(2,1)S(1)}, u32[]{:S(2)}, u32[]{:S(2)}) collective-permute-start(bf16[256,1536]{1,0:T(8,128)(2,1)S(1)} %copy-done.21), channel_id=1, source_target_pairs={{0,16},{16,0},{1,17},{17,1},{2,18},{18,2},{3,19},{19,3},{4,20},{20... | collective-permute-start | bytes 2359304 | tf_op jit(solution)/shard_map/ppermute | solution.py:35
  261.4 41.6 %collective-permute-start.41 = (bf16[256,1536]{1,0:T(8,128)(2,1)S(1)}, bf16[256,1536]{1,0:T(8,128)(2,1)S(1)}, u32[]{:S(2)}, u32[]{:S(2)}) collective-permute-start(bf16[256,1536]{1,0:T(8,128)(2,1)S(1)} %held.1.refs_19_.refs_0_), channel_id=1, source_target_pairs={{0,4},{12,8},{1,5},{13,9},{2,6},{14,10},{3,7},{15,11},{16,20},{28,... | collective-permute-start | bytes 2359304 | tf_op jit(solution)/shard_map/ppermute | solution.py:569
  329.2 231.6 %reduce-scatter.14.cloned.1.call-start = ((), (), s32[]{:S(2)}) async-start(), calls=%async_computation.5 | async-start | bytes 5898240
  329.9 230.9 %reduce-scatter.12.cloned.1.call-start = ((), (), s32[]{:S(2)}) async-start(), calls=%async_computation.4 | async-start | bytes 5898240
  349.9 25.4 %collective-permute-start.57 = (bf16[256,768]{1,0:T(8,128)(2,1)S(1)}, bf16[256,768]{1,0:T(8,128)(2,1)S(1)}, u32[]{:S(2)}, u32[]{:S(2)}) collective-permute-start(bf16[256,768]{1,0:T(8,128)(2,1)S(1)} %add.168.refs_13_.refs_15_), channel_id=1, source_target_pairs={{4,0},{8,12},{5,1},{9,13},{6,2},{10,14},{7,3},{11,15},{20,16},{24,... | collective-permute-start | bytes 1179656 | tf_op jit(solution)/shard_map/ppermute | solution.py:577
  351.2 30.4 %collective-permute-start.55 = (bf16[256,768]{1,0:T(8,128)(2,1)S(1)}, bf16[256,768]{1,0:T(8,128)(2,1)S(1)}, u32[]{:S(2)}, u32[]{:S(2)}) collective-permute-start(bf16[256,768]{1,0:T(8,128)(2,1)S(1)} %add.167.refs_2_.refs_11_), channel_id=1, source_target_pairs={{4,0},{8,12},{5,1},{9,13},{6,2},{10,14},{7,3},{11,15},{20,16},{24,... | collective-permute-start | bytes 1179656 | tf_op jit(solution)/shard_map/ppermute | solution.py:577
  352.7 43.3 %collective-permute-start.60 = (bf16[256,1536]{1,0:T(8,128)(2,1)S(1)}, bf16[256,1536]{1,0:T(8,128)(2,1)S(1)}, u32[]{:S(2)}, u32[]{:S(2)}) collective-permute-start(bf16[256,1536]{1,0:T(8,128)(2,1)S(1)} %copy-done.20), channel_id=1, source_target_pairs={{0,16},{16,0},{1,17},{17,1},{2,18},{18,2},{3,19},{19,3},{4,20},{20... | collective-permute-start | bytes 2359304 | tf_op jit(solution)/shard_map/ppermute | solution.py:35
  422.7 32.2 %collective-permute-start.69 = (bf16[256,768]{1,0:T(8,128)(2,1)S(1)}, bf16[256,768]{1,0:T(8,128)(2,1)S(1)}, u32[]{:S(2)}, u32[]{:S(2)}) collective-permute-start(bf16[256,768]{1,0:T(8,128)(2,1)S(1)} %add.172.refs_2_.refs_17_), channel_id=1, source_target_pairs={{4,0},{8,12},{5,1},{9,13},{6,2},{10,14},{7,3},{11,15},{20,16},{24,... | collective-permute-start | bytes 1179656 | tf_op jit(solution)/shard_map/ppermute | solution.py:577
  424.0 39.3 %collective-permute-start.68 = (bf16[256,768]{1,0:T(8,128)(2,1)S(1)}, bf16[256,768]{1,0:T(8,128)(2,1)S(1)}, u32[]{:S(2)}, u32[]{:S(2)}) collective-permute-start(bf16[256,768]{1,0:T(8,128)(2,1)S(1)} %add.171.refs_2_.refs_15_), channel_id=1, source_target_pairs={{4,0},{8,12},{5,1},{9,13},{6,2},{10,14},{7,3},{11,15},{20,16},{24,... | collective-permute-start | bytes 1179656 | tf_op jit(solution)/shard_map/ppermute | solution.py:577
  425.5 67.9 %collective-permute-start.66 = (bf16[256,1536]{1,0:T(8,128)(2,1)S(1)}, bf16[256,1536]{1,0:T(8,128)(2,1)S(1)}, u32[]{:S(2)}, u32[]{:S(2)}) collective-permute-start(bf16[256,1536]{1,0:T(8,128)(2,1)S(1)} %add.173.refs_19_), channel_id=1, source_target_pairs={{4,0},{8,12},{5,1},{9,13},{6,2},{10,14},{7,3},{11,15},{20,16},{24,... | collective-permute-start | bytes 2359304 | tf_op jit(solution)/shard_map/ppermute | solution.py:577
  515.2 36.6 %collective-permute-start.87 = (bf16[384,576]{1,0:T(8,128)(2,1)}, bf16[384,576]{1,0:T(8,128)(2,1)S(1)}, u32[]{:S(2)}, u32[]{:S(2)}) collective-permute-start(bf16[384,576]{1,0:T(8,128)(2,1)} %get-tuple-element.163), channel_id=1, source_target_pairs={{0,1},{1,0},{2,3},{3,2},{4,5},{5,4},{6,7},{7,6},{8,9},{9,8},{10,11... | collective-permute-start | bytes 1327112 | tf_op jit(solution)/shard_map/ppermute | solution.py:796
  515.9 36.0 %collective-permute-start.88 = (bf16[384,576]{1,0:T(8,128)(2,1)}, bf16[384,576]{1,0:T(8,128)(2,1)S(1)}, u32[]{:S(2)}, u32[]{:S(2)}) collective-permute-start(bf16[384,576]{1,0:T(8,128)(2,1)} %get-tuple-element.164), channel_id=1, source_target_pairs={{0,2},{1,3},{2,0},{3,1},{4,6},{5,7},{6,4},{7,5},{8,10},{9,11},{10,... | collective-permute-start | bytes 1327112 | tf_op jit(solution)/shard_map/ppermute | solution.py:796
  517.9 33.9 %collective-permute-start.89 = (bf16[384,576]{1,0:T(8,128)(2,1)}, bf16[384,576]{1,0:T(8,128)(2,1)S(1)}, u32[]{:S(2)}, u32[]{:S(2)}) collective-permute-start(bf16[384,576]{1,0:T(8,128)(2,1)} %get-tuple-element.165), channel_id=1, source_target_pairs={{0,3},{1,2},{2,1},{3,0},{4,7},{5,6},{6,5},{7,4},{8,11},{9,10},{10,... | collective-permute-start | bytes 1327112 | tf_op jit(solution)/shard_map/ppermute | solution.py:796
  520.9 26.3 %collective-permute-start.80 = (bf16[256,768]{1,0:T(8,128)(2,1)S(1)}, bf16[256,768]{1,0:T(8,128)(2,1)S(1)}, u32[]{:S(2)}, u32[]{:S(2)}) collective-permute-start(bf16[256,768]{1,0:T(8,128)(2,1)S(1)} %add.176.refs_2_.refs_3_), channel_id=1, source_target_pairs={{4,0},{8,12},{5,1},{9,13},{6,2},{10,14},{7,3},{11,15},{20,16},{24,... | collective-permute-start | bytes 1179656 | tf_op jit(solution)/shard_map/ppermute | solution.py:577
  (105 other events, 903.9 us)
Sparse Core Ops, SparseCore 0:
  329.3 31.2 reduce-scatter.9
  363.6 57.0 reduce-scatter.13
  423.7 58.8 reduce-scatter.11

commit v2 on v1

--- a/solution.py
+++ b/solution.py
@@ -14,7 +14,6 @@
 BF = jnp.bfloat16
 F32 = jnp.float32
 FACTOR = HEAD_DIM ** (-0.5)
-CHUNKS = 2
 TILE = 256
 AHEAD = 6
 
@@ -87,6 +86,18 @@
 
 class Order:
     token = ()
+    pending = []
+
+
+def soon(value):
+    other = swap(value)
+    Order.pending.append(other)
+    return other
+
+
+def collect():
+    values, Order.pending = Order.pending, []
+    return [(value, LOOSE_RAW) for value in values]
 
 
 def kernel_call(body, name, ins, outs, scratch=(), after=(), cost=1.0, limit=24):
@@ -173,23 +184,21 @@
     pltpu.make_async_copy(own, buffer, sem).wait()
 
 
-def is_middle():
-    index = lax.axis_index("tensor")
-    return (index == 1) | (index == 2)
-
-
-def summed(refs):
-    middle = is_middle()
-    parts = []
-    for index in range(CHUNKS):
-        parts.append(jnp.where(middle, refs[2 * index][...], refs[2 * index + 1][...]))
-    return jnp.concatenate(parts, axis=1).astype(F32)
-
-
-def store_chunks(value, refs):
-    size = value.shape[1] // len(refs)
-    for index, ref in enumerate(refs):
-        ref[...] = value[:, index * size : (index + 1) * size].astype(BF)
+def share_of(step, size):
+    start = lax.bitwise_xor(lax.axis_index("tensor"), step) * size
+    return pl.ds(pl.multiple_of(start, size), size)
+
+
+def summed(refs, buffer):
+    for step, ref in enumerate(refs):
+        buffer[share_of(step, ref.shape[0]), :] = ref[...]
+    return buffer[...].astype(F32)
+
+
+def store_shares(total, refs):
+    size = total.shape[0] // len(refs)
+    for step, ref in enumerate(refs):
+        ref[...] = total[share_of(step, size), :].astype(BF)
 
 
 def store_halves(value, mine_out, theirs_out):
@@ -235,7 +244,7 @@
     ]
 
 
-def norm_qkv(layer, first, ins, outs, q_buf, kv_buf, sem):
+def norm_qkv(layer, first, ins, outs, q_buf, kv_buf, rows_buf, sem):
     gain, cosine, sine = ins[:3]
     wq, wk, wv = ins[3:5], ins[5:7], ins[7:9]
     query_out, kv_out, normed_out = outs[:3]
@@ -244,7 +253,7 @@
     if first:
         hidden = ins[9][...].astype(F32)
     else:
-        low = (ins[9][...] + summed(ins[10:])).astype(BF)
+        low = (ins[9][...] + summed(ins[10:], rows_buf)).astype(BF)
         outs[3][...] = low
         outs[3].send()
         hidden = low.astype(F32)
@@ -272,7 +281,7 @@
             v_buf[group, index * rows : (index + 1) * rows, :] = block[:, low : low + HEAD_DIM]
 
 
-def attention(layer, peers, ins, outs, q_buf, k_buf, v_buf, wo_buf, sem):
+def attention(layer, peers, ins, outs, q_buf, k_buf, v_buf, wo_buf, sum_buf, sem):
     wo, wo_other, query, bias = ins[:4]
     kv_refs = ins[4:]
     mine_out, theirs_out, attn_out, lse_out = outs[:4]
@@ -298,7 +307,8 @@
     rows = attn.astype(BF)
     store_halves(rows, mine_out, theirs_out)
     arrived(wo.at[0], wo_buf, sem)
-    store_chunks(dot(rows, wo_buf[...]), outs[4:])
+    sum_buf[...] = dot(rows, wo_buf[...])
+    store_shares(sum_buf, outs[4:])
 
 
 def split_query(query, q_buf):
@@ -316,13 +326,13 @@
     return copies
 
 
-def mlp(layer, ins, outs, g_buf, u_buf, d_buf, total, act_buf, sem):
+def mlp(layer, ins, outs, g_buf, u_buf, d_buf, total, rows_buf, act_buf, sem):
     wg, wu, wd = ins[0:2], ins[2:4], ins[4:6]
     hidden, gain = ins[6:8]
     middle_out, normed_out, gate_out, up_out, mine_out, theirs_out = outs[:6]
     copies = mlp_copies(wg, wu, wd, g_buf, u_buf, d_buf, sem)
     fetch(layer, copies[:AHEAD])
-    middle = hidden[...].astype(F32) + summed(ins[8:])
+    middle = hidden[...].astype(F32) + summed(ins[8:], rows_buf)
     middle_out[...] = middle
     middle_out.send()
     normed_out[...] = (middle * norm_scale(middle) * gain[...]).astype(BF)
@@ -349,14 +359,14 @@
     store_halves(act_buf[...], mine_out, theirs_out)
     theirs_out.send()
     mine_out.send()
-    store_chunks(total[...], outs[6:])
-
-
-def mlp_back(layer, last, ins, outs, g_buf, u_buf, d_buf, total, sem):
+    store_shares(total, outs[6:])
+
+
+def mlp_back(layer, last, ins, outs, g_buf, u_buf, d_buf, total, rows_buf, sem):
     wg, wu, wd = ins[0:2], ins[2:4], ins[4:6]
     gate_ref, up_ref = ins[6:8]
     mine_out, theirs_out = outs[:2]
-    chunks = outs[2 : 2 + CHUNKS]
+    shares = outs[2:] if last else outs[2:-2]
     copies = mlp_copies(wg, wu, wd, g_buf, u_buf, d_buf, sem)
     fetch(layer, copies[:AHEAD])
     early = lax.axis_index("section") == 0
@@ -364,8 +374,8 @@
         grad_ref = ins[8]
     else:
         middle_grad, hidden, gain = ins[8:11]
-        grad_ref, gain_out = outs[2 + CHUNKS :]
-        values, grad = hidden[...].astype(F32), summed(ins[11:])
+        grad_ref, gain_out = outs[-2:]
+        values, grad = hidden[...].astype(F32), summed(ins[11:], rows_buf)
         scale = norm_scale(values)
         gain_out[...] = jnp.sum(grad * values * scale, axis=0, keepdims=True)
         grad_ref[...] = (middle_grad[...] + norm_back(values, scale, gain[...], grad)).astype(BF)
@@ -390,10 +400,10 @@
             total[...] = term
         else:
             total[...] += term
-    store_chunks(total[...], chunks)
-
-
-def attention_back(layer, peers, ins, outs, q_buf, k_buf, v_buf, dk_buf, dv_buf, wo_buf, sem):
+    store_shares(total, shares)
+
+
+def attention_back(layer, peers, ins, outs, q_buf, k_buf, v_buf, dk_buf, dv_buf, wo_buf, rows_buf, sem):
     wo, wo_other, grad_in, middle, gain, query, bias, attn, lse, cosine, sine = ins[:11]
     kv_refs, sums = ins[11 : 11 + peers], ins[11 + peers :]
     middle_grad_out, low_out, gain_out, pre_out = outs[:4]
@@ -401,7 +411,7 @@
     fetch(layer, [(wo.at[0], wo_other.at[0], wo_buf, sem)])
     heads, groups = q_buf.shape[0], k_buf.shape[0]
     group_size = heads // groups
-    grad = summed(sums)
+    grad = summed(sums, rows_buf)
     values = middle[...]
     scale = norm_scale(values)
     gain_out[...] = jnp.sum(grad * values * scale, axis=0, keepdims=True)
@@ -447,7 +457,7 @@
     pre_out[...] = rotate(query_grad, cosine[...], -sine[...]).astype(BF)
 
 
-def qkv_back(layer, ins, outs, q_buf, kv_buf, sem):
+def qkv_back(layer, ins, outs, q_buf, kv_buf, total, sem):
     wq, wk, wv = ins[0:2], ins[2:4], ins[4:6]
     pre_query, cosine, sine, own = ins[6:10]
     mine_out, theirs_out = outs[:2]
@@ -466,12 +476,17 @@
     mine_out.send()
     for own_weight, _, buffer, one in copies:
         arrived(own_weight, buffer, one)
-    store_chunks(dot_t(pre_q, q_buf[...]) + dot(pre, kv_buf[...]), outs[2:])
-
-
-def finish(ins, outs):
+    total[...] = dot_t(pre_q, q_buf[...]) + dot(pre, kv_buf[...])
+    store_shares(total, outs[2:])
+
+
+def last_output(ins, outs, rows_buf):
+    outs[0][...] = (ins[0][...] + summed(ins[1:], rows_buf)).astype(BF)
+
+
+def finish(ins, outs, rows_buf):
     middle_grad, hidden, gain = ins[:3]
-    values, grad = hidden[...].astype(F32), summed(ins[3:])
+    values, grad = hidden[...].astype(F32), summed(ins[3:], rows_buf)
     scale = norm_scale(values)
     outs[0][...] = (middle_grad[...] + norm_back(values, scale, gain[...], grad)).astype(BF)
     outs[0].send()
@@ -479,7 +494,7 @@
 
 
 def grad_blocks(spread, ins, outs, *scratch):
-    buffer = scratch[0] if spread else outs[0]
+    buffer = scratch[0] if spread else outs[0].buffer
     peers = len(outs) if spread else outs[0].buffer.shape[0]
     me = lax.axis_index("dp")
     start = 0
@@ -493,6 +508,9 @@
             place = lax.bitwise_xor(me, block) if spread else block
             buffer[place, :, lanes] = term.astype(BF)
         start += wide.shape[1]
+    if start < buffer.shape[-1]:
+        rest = buffer.shape[-1] - start
+        buffer[:, :, start:] = jnp.zeros((peers, buffer.shape[1], rest), BF)
     if spread:
         for index, out in enumerate(outs):
             out[...] = buffer[index]
@@ -543,48 +561,35 @@
     value_out[...] = flipped[half:]
 
 
-def copy_body(ins, outs):
-    outs[0][...] = ins[0][...]
-
-
-def held(value, after):
-    (out,) = kernel_call(
-        copy_body, "held", far([value]), near([shape(value.shape, value.dtype)]), after=after
-    )
-    return out
-
-
-def add_rounded(ins, outs):
-    outs[0][...] = (ins[0][...].astype(F32) + ins[1][...].astype(F32)).astype(BF)
-
-
-def add(left, right, after=()):
-    (out,) = kernel_call(
-        add_rounded, "add", near([left, right]), near([shape(left.shape, BF)]), after=after, cost=0.2
-    )
-    return out
-
-
-def hop_in(parts):
-    return [lax.ppermute(part, "tensor", [(0, 1), (3, 2)]) for part in parts]
-
-
-def hop_across(parts):
-    return [lax.ppermute(part, "tensor", [(1, 2), (2, 1)]) for part in parts]
-
-
-def hop_out(parts):
-    return [lax.ppermute(part, "tensor", [(1, 0), (2, 3)]) for part in parts]
-
-
-def add_all(parts, others, after=()):
-    return [add(part, other, after) for part, other in zip(parts, others)]
+def add_shares(ins, outs):
+    total = ins[0][...].astype(F32)
+    for ref in ins[1:]:
+        total = total + ref[...].astype(F32)
+    outs[0][...] = total.astype(BF)
+
+
+def spread(values):
+    peers = len(values)
+    return [values[0]] + [
+        lax.ppermute(values[step], "tensor", [(peer, peer ^ step) for peer in range(peers)])
+        for step in range(1, peers)
+    ]
+
+
+def add_rows(received, after=()):
+    (total,) = kernel_call(
+        add_shares,
+        "add_shares",
+        near(received),
+        near([shape(received[0].shape, BF)]),
+        after=after,
+        cost=0.5,
+    )
+    return total
 
 
 def sum_tensor(parts):
-    pairs = add_all(parts, hop_in(parts))
-    totals = add_all(pairs, hop_across(pairs))
-    return [piece for both in zip(totals, hop_out(totals)) for piece in both]
+    return spread([add_rows(spread(parts))] * len(parts))
 
 
 def layout(lengths, token_count):
@@ -627,7 +632,7 @@
     w_down,
     out_grad,
 ):
-    Order.token = ()
+    Order.token, Order.pending = (), []
     rows, width = layer_input.shape[1:]
     peers = lax.axis_size("dp")
     me = lax.axis_index("dp")
@@ -636,7 +641,7 @@
     heads, groups = q_width // HEAD_DIM, kv_width // HEAD_DIM
     tokens = rows * peers
     steps = ff // TILE
-    part = width // CHUNKS
+    shares = lax.axis_size("tensor")
 
     def pick(early, late):
         return jnp.where(first, early, late)
@@ -663,7 +668,10 @@
     bias = jnp.where(allowed, 0.0, MASKED).astype(F32)
     cosine, sine = rope_tables(row_pos, heads)
 
-    chunk_outs = near([shape((rows, part), BF)] * CHUNKS)
+    share = shape((rows // shares, width), BF)
+    share_outs = near([share] * shares)
+    rows_buf = pltpu.VMEM((rows, width), BF)
+    total_buf = pltpu.VMEM((rows, width), F32)
     row_f32 = shape((rows, width), F32)
     row_bf = shape((rows, width), BF)
     line = shape((1, width), F32)
@@ -677,14 +685,13 @@
     qkv_scratch = [
         pltpu.VMEM((width, q_width), BF),
         pltpu.VMEM((2 * kv_width, width), BF),
-        dma((3,)),
     ]
     mlp_scratch = [
         pltpu.VMEM((steps, width, TILE), BF),
         pltpu.VMEM((steps, width, TILE), BF),
         pltpu.VMEM((steps, TILE, width), BF),
-        pltpu.VMEM((rows, width), F32),
-        dma((3, steps)),
+        total_buf,
+        rows_buf,
     ]
     head_scratch = [
         pltpu.VMEM((heads, rows, HEAD_DIM), BF),
@@ -692,7 +699,7 @@
         pltpu.VMEM((groups, tokens, HEAD_DIM), BF),
     ]
 
-    def run_qkv(layer, source, sums):
+    def run_qkv(layer, source, sums, after):
         start = layer == 0
         outs = [head_bf, kv_bf, row_bf]
         return kernel_call(
@@ -700,43 +707,46 @@
             f"norm_qkv_{layer}",
             far([gains[0][layer], cosine, sine]) + weights([wq, wk, wv]) + far([source]) + near(sums),
             far(outs if start else outs + [row_bf]),
-            qkv_scratch,
+            qkv_scratch + [rows_buf, dma((3,))],
+            after,
             cost=4.0,
         )
 
-    def run_attention(layer, query, blocks):
+    def run_attention(layer, query, blocks, after):
         outs = [half_head] * 2 + [shape((rows, q_width), F32), shape((rows, heads), F32)]
         return kernel_call(
             functools.partial(attention, layer, peers),
             f"attention_{layer}",
             weights([wo]) + far([query, bias, *blocks]),
-            far(outs) + chunk_outs,
-            head_scratch + [pltpu.VMEM((q_width, width), BF), dma],
+            far(outs) + share_outs,
+            head_scratch + [pltpu.VMEM((q_width, width), BF), total_buf, dma],
+            after,
             cost=5.0,
             limit=min(8 + 4 * peers, 56),
         )
 
-    def run_mlp(layer, hidden, sums):
+    def run_mlp(layer, hidden, sums, after):
         return kernel_call(
             functools.partial(mlp, layer),
             f"mlp_{layer}",
             weights([wg, wu, wd]) + far([hidden, gains[1][layer]]) + near(sums),
             far([row_f32, row_bf, wide_f32, wide_f32, half_wide, half_wide])
-            + (chunk_outs if layer == 0 else far([row_bf])),
-            mlp_scratch[:-1] + [pltpu.VMEM((rows, ff), BF)] + mlp_scratch[-1:],
+            + (share_outs if layer == 0 else far([share] * shares)),
+            mlp_scratch + [pltpu.VMEM((rows, ff), BF), dma((3, steps))],
+            after,
             cost=6.0,
             limit=32,
         )
 
     def run_mlp_back(layer, source, sums, gate, upward, after):
         last = layer == 1
-        outs = far([wide_bf, wide_bf]) + chunk_outs
+        outs = far([wide_bf, wide_bf]) + share_outs
         return kernel_call(
             functools.partial(mlp_back, layer, last),
             f"mlp_back_{layer}",
             weights([wg, wu, wd]) + far([gate, upward, *source]) + near(sums),
             outs if last else outs + far([row_bf, line]),
-            mlp_scratch,
+            mlp_scratch + [dma((3, steps))],
             after,
             cost=8.0,
             limit=32,
@@ -755,6 +765,7 @@
                 pltpu.VMEM((groups, tokens, HEAD_DIM), F32),
                 pltpu.VMEM((groups, tokens, HEAD_DIM), F32),
                 pltpu.VMEM((q_width, width), BF),
+                rows_buf,
                 dma,
             ],
             after,
@@ -767,29 +778,32 @@
             functools.partial(qkv_back, layer),
             f"qkv_back_{layer}",
             weights([wq, wk, wv]) + far([pre_query, cosine, sine]) + loose(pieces),
-            far([kv_bf, kv_bf]) + chunk_outs,
-            qkv_scratch,
+            far([kv_bf, kv_bf]) + share_outs,
+            qkv_scratch + [total_buf, dma((3,))],
             after,
             cost=4.0,
         )
 
-    def weight_grad(groups, name, spread):
+    def weight_grad(groups, name, direct, after=()):
         ins, tall = [], 0
         for left, left_other, mine, mine_other in groups:
             ins += far([left]) + loose([left_other]) + far([mine]) + loose([mine_other])
             tall += mine.shape[1]
+        if not direct:
+            tall = -(-tall // 128) * 128
         block = shape((width // peers, tall), BF)
         whole = shape((peers, width // peers, tall), BF)
         blocks = kernel_call(
-            functools.partial(grad_blocks, spread),
+            functools.partial(grad_blocks, direct),
             name,
             ins,
-            far([block] * peers if spread else [whole]),
-            [pltpu.VMEM(whole.shape, BF)] if spread else [],
+            far([block] * peers if direct else [whole]),
+            [pltpu.VMEM(whole.shape, BF)] if direct else [],
+            after,
             cost=8.0,
         )
-        if not spread:
-            return blocks, lax.psum_scatter(blocks[0], "dp", scatter_dimension=0, tiled=False)
+        if not direct:
+            return lax.psum_scatter(blocks[0], "dp", scatter_dimension=0, tiled=False)
         pieces = [blocks[0]]
         for step in range(1, peers):
             pairing = [(peer, peer ^ step) for peer in range(peers)]
@@ -800,7 +814,7 @@
                 add_blocks, "add_" + name, far(pieces[:1]) + loose(pieces[1:]), far([block])
             )[0]
 
-        return blocks, total
+        return total
 
     def whole_grads(body, name, per_layer, dims):
         kept = pick(per_layer[0], per_layer[1])
@@ -817,30 +831,40 @@
     hidden = pick(layer_input[0], layer_input[1])
     grad = pick(out_grad[0], out_grad[1])
     saved, outputs = [], []
+    grad_other = soon(grad)
     for layer in range(2):
         if layer == 0:
-            query, kv, normed_one = run_qkv(layer, hidden, [])
+            query, kv, normed_one = run_qkv(layer, hidden, [], [])
         else:
-            query, kv, normed_one, hidden = run_qkv(layer, middle, sums)
+            query, kv, normed_one, hidden = run_qkv(layer, middle, sums, collect())
             outputs.append(hidden)
         blocks = [kv]
         for step in range(1, peers):
             blocks.append(lax.ppermute(kv, "dp", peer_pairs(peers, step, False)))
-        *head_halves, attn, lse, chunk_one, chunk_two = run_attention(layer, query, blocks)
-        sums = sum_tensor([chunk_one, chunk_two])
+        early = collect()
+        if layer == 0:
+            early += raw([other for _, other in pairs])
+        normed_one = (normed_one, soon(normed_one))
+        *results, attn, lse = (outs := run_attention(layer, query, blocks, early))[:-shares]
+        sums = sum_tensor(outs[-shares:])
+        early = collect()
+        head_halves = (results[0], soon(results[1]))
         middle, normed_two, gate, upward, act_mine, act_theirs, *parts = run_mlp(
-            layer, hidden, sums
-        )
-        act_halves = [act_mine, act_theirs]
+            layer, hidden, sums, early
+        )
         if layer == 0:
             sums = sum_tensor(parts)
+        early = collect()
+        act_halves = (act_mine, soon(act_theirs))
+        normed_two = (normed_two, soon(normed_two))
+        Order.pending += [value for value, _ in early]
         saved.append(
             (hidden, query, blocks, normed_one, head_halves, attn, lse)
             + (middle, normed_two, gate, upward, act_halves)
         )
 
-    last_middle, last_part = middle, parts[0]
-    in_grads, vectors, mlp_parts, head_parts = [None, None], [None, None], [None, None], [None, None]
+    last_middle, last_parts = middle, parts
+    in_grads, vectors, mlp_totals = [None, None], [None, None], [None, None]
     source, sums = [grad], []
     for layer in (1, 0):
         (hidden, query, blocks, normed_one, head_halves, attn, lse) = saved[layer][:7]
@@ -852,53 +876,60 @@
                 layer, source, sums, gate, upward, []
             )
             in_grads[1] = grad
-        inward = hop_in(parts)
-        mlp_blocks, mlp_parts[layer] = weight_grad(
-            [
-                (normed_two, swap(normed_two), mine, swap(theirs)),
-                (grad, swap(grad), act_halves[0], swap(act_halves[1])),
-            ],
-            f"grad_mlp_{layer}",
-            False,
-        )
-        pairs = add_all(parts, inward)
-        totals = add_all(pairs, hop_across(pairs))
-        outward = hop_out(totals)
-        sums = [piece for both in zip(totals, outward) for piece in both]
+        if layer == 0:
+            grad_other = soon(grad)
+        mlp_groups = [(*normed_two, mine, soon(theirs)), (grad, grad_other, *act_halves)]
+        received = spread(parts)
+        sums = spread([add_rows(received, collect())] * shares)
+        due = []
         if layer == 1:
-            last_part = held(last_part, [])
-            (last_inward,) = hop_in([last_part])
+            last_received = spread(last_parts)
         else:
-            last_total = add(last_pair, last_across)
-            (last_outward,) = hop_out([last_total])
+            mlp_totals[0] = weight_grad(mlp_groups, "grad_mlp_0", False)
+            due = []
         middle_grad, low, gain_two, pre_query, *pieces = run_attention_back(
-            layer, grad, middle, sums, query, blocks, attn, lse, []
-        )
+            layer, grad, middle, sums, query, blocks, attn, lse, due
+        )
+        low_other = soon(low)
         far_pieces = [
             lax.ppermute(pieces[step], "dp", peer_pairs(peers, step, True))
             for step in range(1, peers)
         ]
         if layer == 1:
-            last_pair = add(last_part, last_inward)
-            (last_across,) = hop_across([last_pair])
-        mine, theirs, *parts = run_qkv_back(layer, pre_query, [pieces[0]] + far_pieces, [])
-        inward = hop_in(parts)
-        head_blocks, head_parts[layer] = weight_grad(
-            [
-                (low, swap(low), head_halves[0], swap(head_halves[1])),
-                (normed_one, swap(normed_one), mine, swap(theirs)),
-            ],
-            f"grad_head_{layer}",
-            layer == 0,
-        )
-        pairs = add_all(parts, inward)
-        totals = add_all(pairs, hop_across(pairs))
-        outward = hop_out(totals)
-        sums = [piece for both in zip(totals, outward) for piece in both]
+            last_sums = spread([add_rows(last_received)] * shares)
+            mlp_totals[1] = weight_grad(
+                mlp_groups, "grad_mlp_1", False, [(far_pieces[0], LOOSE_RAW)]
+            )
+        else:
+            (output,) = kernel_call(
+                last_output,
+                "last_output",
+                far([last_middle]) + near(last_sums),
+                far([row_bf]),
+                [rows_buf],
+                cost=2.0,
+            )
+            outputs.append(output)
+        mine, theirs, *parts = run_qkv_back(
+            layer, pre_query, [pieces[0]] + far_pieces, collect() + (raw([mlp_totals[1], head_later]) if layer == 0 else [])
+        )
+        head_groups = [(low, low_other, *head_halves), (*normed_one, mine, soon(theirs))]
+        received = spread(parts)
+        if layer == 0:
+            head_total = weight_grad(head_groups, "grad_head_0", True)
+            sums = spread([add_rows(received, collect())] * shares)
+            head_total = head_total()
+        else:
+            sums = spread([add_rows(received, collect())] * shares)
+            head_later = weight_grad(head_groups, "grad_head_1", False)
         source = [middle_grad, hidden, gains[0][layer]]
         vectors[layer] = gain_two
     in_grads[0], last_line = kernel_call(
-        finish, "finish", far(source) + near(sums), far([row_bf, line])
+        finish,
+        "finish",
+        far(source) + near(sums),
+        far([row_bf, line]),
+        [rows_buf],
     )
     lines = jnp.concatenate([last_line, vectors[0], gain_one, vectors[1]], axis=0)
     for axis in ("section", "dp"):
@@ -906,15 +937,12 @@
             pairing = [(peer, peer ^ (1 << bit)) for peer in range(lax.axis_size(axis))]
             lines = lines + lax.ppermute(lines, axis, pairing)
 
-    at_middle = (lax.axis_index("tensor") == 1) | (lax.axis_index("tensor") == 2)
-    last_sum = jnp.where(at_middle, last_total, last_outward)
-    outputs.append((last_middle + last_sum.astype(F32)).astype(BF))
     activations = by_layer(outputs)
     input_grads = by_layer(in_grads)
     size = width // peers
-    head_parts[0] = head_parts[0]()
+    head_parts = [head_total, head_later[:, : head_total.shape[1]]]
     grad_gate, grad_up, grad_down = whole_grads(
-        mlp_grads, "mlp_grads", mlp_parts, [(size, ff), (size, ff), (ff, size)]
+        mlp_grads, "mlp_grads", mlp_totals, [(size, ff), (size, ff), (ff, size)]
     )
     grad_out, grad_query, grad_key, grad_value = whole_grads(
         head_grads,

time: 590 us -> 518 us (0.88)
  waiting for transfers between devices: 295 us -> 226 us
  starting transfers between devices: 109 us -> 124 us
  local copies, waits for them, and re-layouts: 15 us -> 7.07 us
    ppermute x45 -> x48, waiting for transfers between devices: 251 us -> 170 us  [spread(): lax.ppermute(values[step], 'tensor', [(peer, peer ^ step) for peer in ran...]
    ppermute x3, waiting for transfers between devices: 0.01 us -> 15.6 us  [weight_grad(): pieces.append(lax.ppermute(blocks[step], 'dp', pairing))]
    ppermute x45 -> x48, starting transfers between devices: 71.6 us -> 84.9 us  [spread(): lax.ppermute(values[step], 'tensor', [(peer, peer ^ step) for peer in ran...]
    ppermute x29, waiting for transfers between devices: 4.23 us -> 12.2 us  [swap(): return lax.ppermute(value, 'section', [(0, 1), (1, 0)])]
    pallas_call x51 -> x29, Pallas kernels: 126 us -> 125 us  [kernel_call(): results = call(*[fixed(value, where) for value, where in [*ins, *after]])]
  transfers between devices with their start and end apart: 95 -> 98, of which waited for: 39 -> 40; matrix products, arithmetic and copies ran while one was open for 4% -> 4% of each run, Pallas kernels for 17% -> 18%
where the time goes in v2:
time: 518 us; the launch traced here: 514 us
  waiting for transfers between devices  226 us (44%)
  Pallas kernels  125 us (24%)
  starting transfers between devices  124 us (24%)
  other arithmetic  16.6 us (3%)
  between operations  15.4 us (3%)
  local copies, waits for them, and re-layouts  7.07 us (1%)
    ppermute x48, waiting for transfers between devices, spread(): lax.ppermute(values[step], 'tensor', [(peer, peer ^ step) for peer in ran...  170 us
    pallas_call x29, Pallas kernels, kernel_call(): results = call(*[fixed(value, where) for value, where in [*ins, *after]])  125 us
    ppermute x48, starting transfers between devices, spread(): lax.ppermute(values[step], 'tensor', [(peer, peer ^ step) for peer in ran...  84.9 us
    ppermute x6, starting transfers between devices, per_device(): blocks.append(lax.ppermute(kv, 'dp', peer_pairs(peers, step, False)))  20.3 us
    ppermute x3, waiting for transfers between devices, weight_grad(): pieces.append(lax.ppermute(blocks[step], 'dp', pairing))  15.6 us
    ppermute x6, waiting for transfers between devices, per_device(): lax.ppermute(pieces[step], 'dp', peer_pairs(peers, step, True))  15 us
    ppermute x29, waiting for transfers between devices, swap(): return lax.ppermute(value, 'section', [(0, 1), (1, 0)])  12.2 us
  transfers between devices with their start and end apart: 98, of which 40 were waited for; matrix products, arithmetic and copies ran while one was open for 4% of the time, Pallas kernels for 18%

profile of v2, /device:TPU:0, one launch (start us, length us, event | category | flops | bytes accessed | tf_op | source)
XLA Modules:
  0.0 514.0 jit_solution(11689395532290875943)
XLA Ops:
  64.1 12.2 %collective-permute-done.14.refs_2_ = bf16[64,1536]{1,0:T(8,128)(2,1)S(1)} collective-permute-done((bf16[64,1536]{1,0:T(8,128)(2,1)S(1)}, bf16[64,1536]{1,0:T(8,128)(2,1)S(1)}, u32[]{:S(2)}, u32[]{:S(2)}) %collective-permute-start.14) | collective-permute-done | bytes 196640 | tf_op jit(solution)/shard_map/ppermute | solution.py:574
  86.1 8.0 %collective-permute-done.17.refs_10_ = bf16[64,1536]{1,0:T(8,128)(2,1)S(1)} collective-permute-done((bf16[64,1536]{1,0:T(8,128)(2,1)S(1)}, bf16[64,1536]{1,0:T(8,128)(2,1)S(1)}, u32[]{:S(2)}, u32[]{:S(2)}) %collective-permute-start.17) | collective-permute-done | bytes 196640 | tf_op jit(solution)/shard_map/ppermute | solution.py:574
  94.1 8.4 %mlp_0.1 = (f32[256,1536]{1,0:T(8,128)}, bf16[256,1536]{1,0:T(8,128)(2,1)}, f32[256,1024]{1,0:T(8,128)}, f32[256,1024]{1,0:T(8,128)}, bf16[256,512]{1,0:T(8,128)...) custom-call(bf16[1,1536,1024]{2,1,0:T(8,128)(2,1)} %refs_0_.17, ...), custom_call_target="tpu_custom_call" | custom-call | flops 6000000000 | tf_op jit(solution)/shard_map/mlp_0/pallas_call | solution.py:143
  107.1 6.7 %collective-permute-done.20.refs_1_ = bf16[64,1536]{1,0:T(8,128)(2,1)S(1)} collective-permute-done((bf16[64,1536]{1,0:T(8,128)(2,1)S(1)}, bf16[64,1536]{1,0:T(8,128)(2,1)S(1)}, u32[]{:S(2)}, u32[]{:S(2)}) %collective-permute-start.20) | collective-permute-done | bytes 196640 | tf_op jit(solution)/shard_map/ppermute | solution.py:574
  122.7 9.1 %collective-permute-start.24 = (bf16[64,1536]{1,0:T(8,128)(2,1)S(1)}, bf16[64,1536]{1,0:T(8,128)(2,1)S(1)}, u32[]{:S(2)}, u32[]{:S(2)}) collective-permute-start(bf16[64,1536]{1,0:T(8,128)(2,1)S(1)} %add_shares.9.refs_10_.refs_17_), channel_id=1, source_target_pairs={{0,8},{4,12},{8,0},{12,4},{1,9},{5,13},{9,1},{13,5},{2,10},{6,14},... | collective-permute-start | bytes 589832 | tf_op jit(solution)/shard_map/ppermute | solution.py:574
  132.4 8.3 %collective-permute-done.24.refs_12_ = bf16[64,1536]{1,0:T(8,128)(2,1)S(1)} collective-permute-done((bf16[64,1536]{1,0:T(8,128)(2,1)S(1)}, bf16[64,1536]{1,0:T(8,128)(2,1)S(1)}, u32[]{:S(2)}, u32[]{:S(2)}) %collective-permute-start.24) | collective-permute-done | bytes 196640 | tf_op jit(solution)/shard_map/ppermute | solution.py:574
  145.5 6.6 %collective-permute-start.31 = (bf16[256,384]{1,0:T(8,128)(2,1)}, bf16[256,384]{1,0:T(8,128)(2,1)S(1)}, u32[]{:S(2)}, u32[]{:S(2)}) collective-permute-start(bf16[256,384]{1,0:T(8,128)(2,1)} %get-tuple-element.127.refs_4_.refs_11_), channel_id=1, source_target_pairs={{0,3},{1,2},{4,7},{5,6},{8,11},{9,10},{12,15},{13,14},{16,19},{17,... | collective-permute-start | bytes 589832 | tf_op jit(solution)/shard_map/ppermute | solution.py:843
  174.5 9.3 %collective-permute-done.33.refs_2_ = bf16[64,1536]{1,0:T(8,128)(2,1)S(1)} collective-permute-done((bf16[64,1536]{1,0:T(8,128)(2,1)S(1)}, bf16[64,1536]{1,0:T(8,128)(2,1)S(1)}, u32[]{:S(2)}, u32[]{:S(2)}) %collective-permute-start.33) | collective-permute-done | bytes 196640 | tf_op jit(solution)/shard_map/ppermute | solution.py:574
  193.6 8.0 %collective-permute-done.36.refs_10_ = bf16[64,1536]{1,0:T(8,128)(2,1)S(1)} collective-permute-done((bf16[64,1536]{1,0:T(8,128)(2,1)S(1)}, bf16[64,1536]{1,0:T(8,128)(2,1)S(1)}, u32[]{:S(2)}, u32[]{:S(2)}) %collective-permute-start.36) | collective-permute-done | bytes 196640 | tf_op jit(solution)/shard_map/ppermute | solution.py:574
  201.5 8.2 %mlp_1.1 = (f32[256,1536]{1,0:T(8,128)}, bf16[256,1536]{1,0:T(8,128)(2,1)}, f32[256,1024]{1,0:T(8,128)}, f32[256,1024]{1,0:T(8,128)}, bf16[256,512]{1,0:T(8,128)...) custom-call(bf16[1,1536,1024]{2,1,0:T(8,128)(2,1)} %refs_0_.17, ...), custom_call_target="tpu_custom_call" | custom-call | flops 6000000000 | tf_op jit(solution)/shard_map/mlp_1/pallas_call | solution.py:143
  209.8 10.1 %mlp_back_1.1 = (bf16[256,1024]{1,0:T(8,128)(2,1)}, bf16[256,1024]{1,0:T(8,128)(2,1)}, bf16[64,1536]{1,0:T(8,128)(2,1)S(1)}, bf16[64,1536]{1,0:T(8,128)(2,1)S(1)...) custom-call(bf16[1,1536,1024]{2,1,0:T(8,128)(2,1)} %refs_0_.17, ...), custom_call_target="tpu_custom_call" | custom-call | flops 8000000000 | tf_op jit(solution)/shard_map/mlp_back_1/pallas_call | solution.py:143
  231.1 8.4 %collective-permute-done.43.refs_2_ = bf16[64,1536]{1,0:T(8,128)(2,1)S(1)} collective-permute-done((bf16[64,1536]{1,0:T(8,128)(2,1)S(1)}, bf16[64,1536]{1,0:T(8,128)(2,1)S(1)}, u32[]{:S(2)}, u32[]{:S(2)}) %collective-permute-start.43) | collective-permute-done | bytes 196640 | tf_op jit(solution)/shard_map/ppermute | solution.py:574
  250.6 10.8 %collective-permute-done.50.refs_17_ = bf16[64,1536]{1,0:T(8,128)(2,1)S(1)} collective-permute-done((bf16[64,1536]{1,0:T(8,128)(2,1)S(1)}, bf16[64,1536]{1,0:T(8,128)(2,1)S(1)}, u32[]{:S(2)}, u32[]{:S(2)}) %collective-permute-start.50) | collective-permute-done | bytes 196640 | tf_op jit(solution)/shard_map/ppermute | solution.py:574
  261.5 10.5 %attention_back_1.1 = (f32[256,1536]{1,0:T(8,128)}, bf16[256,1536]{1,0:T(8,128)(2,1)}, f32[1,1536]{1,0:T(1,128)}, bf16[256,384]{1,0:T(8,128)(2,1)}, f32[256,384]...) custom-call(bf16[1,384,1536]{2,1,0:T(8,128)(2,1)} %refs_0_.18, ...), custom_call_target="tpu_custom_call" | custom-call | flops 8999999488 | tf_op jit(solution)/shard_map/attention_back_1/pallas_call | solution.py:143
  302.7 8.1 %collective-permute-done.60.refs_2_ = bf16[64,1536]{1,0:T(8,128)(2,1)S(1)} collective-permute-done((bf16[64,1536]{1,0:T(8,128)(2,1)S(1)}, bf16[64,1536]{1,0:T(8,128)(2,1)S(1)}, u32[]{:S(2)}, u32[]{:S(2)}) %collective-permute-start.60) | collective-permute-done | bytes 196640 | tf_op jit(solution)/shard_map/ppermute | solution.py:574
  326.6 8.6 %collective-permute-done.64.refs_13_ = bf16[64,1536]{1,0:T(8,128)(2,1)S(1)} collective-permute-done((bf16[64,1536]{1,0:T(8,128)(2,1)S(1)}, bf16[64,1536]{1,0:T(8,128)(2,1)S(1)}, u32[]{:S(2)}, u32[]{:S(2)}) %collective-permute-start.64) | collective-permute-done | bytes 196640 | tf_op jit(solution)/shard_map/ppermute | solution.py:574
  335.2 11.2 %mlp_back_0.1 = (bf16[256,1024]{1,0:T(8,128)(2,1)}, bf16[256,1024]{1,0:T(8,128)(2,1)}, bf16[64,1536]{1,0:T(8,128)(2,1)S(1)}, bf16[64,1536]{1,0:T(8,128)(2,1)S(1)...) custom-call(bf16[1,1536,1024]{2,1,0:T(8,128)(2,1)} %refs_0_.17, ...), custom_call_target="tpu_custom_call" | custom-call | flops 8000000000 | tf_op jit(solution)/shard_map/mlp_back_0/pallas_call | solution.py:143
  357.5 6.6 %collective-permute-done.67.refs_2_ = bf16[64,1536]{1,0:T(8,128)(2,1)S(1)} collective-permute-done((bf16[64,1536]{1,0:T(8,128)(2,1)S(1)}, bf16[64,1536]{1,0:T(8,128)(2,1)S(1)}, u32[]{:S(2)}, u32[]{:S(2)}) %collective-permute-start.67) | collective-permute-done | bytes 196640 | tf_op jit(solution)/shard_map/ppermute | solution.py:574
  364.2 6.7 %grad_mlp_0.1.refs_19_ = bf16[4,384,1536]{2,1,0:T(8,128)(2,1)} custom-call(bf16[256,1536]{1,0:T(8,128)(2,1)} %get-tuple-element.123.refs_0_, bf16[256,1536]{1,0:T(8,128)(2,1)S(1)} %collective-permute-done.27.refs_15_.refs_1_, bf16[256,1024]{1,0:T(8,128)(2,1)} %get-tuple-element.177.refs_2_, bf16[256,1024]{1,0:T(8,128)(2,1)S(1)} %collective-permute-done.70.refs_5_.refs_3_, ...), custom_call_target="tpu_custom_call" | custom-call | flops 8000000000 | tf_op jit(solution)/shard_map/grad_mlp_0/pallas_call | solution.py:143
  378.8 12.3 %collective-permute-done.72.refs_17_ = bf16[64,1536]{1,0:T(8,128)(2,1)S(1)} collective-permute-done((bf16[64,1536]{1,0:T(8,128)(2,1)S(1)}, bf16[64,1536]{1,0:T(8,128)(2,1)S(1)}, u32[]{:S(2)}, u32[]{:S(2)}) %collective-permute-start.72) | collective-permute-done | bytes 196640 | tf_op jit(solution)/shard_map/ppermute | solution.py:574
  391.1 10.4 %attention_back_0.1 = (f32[256,1536]{1,0:T(8,128)}, bf16[256,1536]{1,0:T(8,128)(2,1)}, f32[1,1536]{1,0:T(1,128)}, bf16[256,384]{1,0:T(8,128)(2,1)}, f32[256,384]...) custom-call(bf16[1,384,1536]{2,1,0:T(8,128)(2,1)} %refs_0_.18, ...), custom_call_target="tpu_custom_call" | custom-call | flops 8999999488 | tf_op jit(solution)/shard_map/attention_back_0/pallas_call | solution.py:143
  412.6 8.0 %collective-permute-done.53.refs_3_ = bf16[64,1536]{1,0:T(8,128)(2,1)S(1)} collective-permute-done((bf16[64,1536]{1,0:T(8,128)(2,1)S(1)}, bf16[64,1536]{1,0:T(8,128)(2,1)S(1)}, u32[]{:S(2)}, u32[]{:S(2)}) %collective-permute-start.53) | collective-permute-done | bytes 196640 | tf_op jit(solution)/shard_map/ppermute | solution.py:574
  424.7 10.4 %collective-permute-done.77.refs_12_ = bf16[256,384]{1,0:T(8,128)(2,1)S(1)} collective-permute-done((bf16[256,384]{1,0:T(8,128)(2,1)}, bf16[256,384]{1,0:T(8,128)(2,1)S(1)}, u32[]{:S(2)}, u32[]{:S(2)}) %collective-permute-start.77) | collective-permute-done | bytes 196640 | tf_op jit(solution)/shard_map/ppermute | solution.py:895
  466.2 15.6 %collective-permute-done.88.refs_3_ = bf16[384,576]{1,0:T(8,128)(2,1)S(1)} collective-permute-done((bf16[384,576]{1,0:T(8,128)(2,1)}, bf16[384,576]{1,0:T(8,128)(2,1)S(1)}, u32[]{:S(2)}, u32[]{:S(2)}) %collective-permute-start.88) | collective-permute-done | bytes 442400 | tf_op jit(solution)/shard_map/ppermute | solution.py:810
  (326 shorter events, 276.1 us)
Async XLA Ops:
  7.2 427.9 %reduce-scatter.12.cloned.1.call-start = ((), (), s32[]{:S(2)}) async-start(), calls=%async_computation.4 | async-start | bytes 2457600
  7.8 41.8 %collective-permute-start.4 = (bf16[1,1536,1024]{2,1,0:T(8,128)(2,1)}, bf16[1,1536,1024]{2,1,0:T(8,128)(2,1)}, u32[]{:S(2)}, u32[]{:S(2)}) collective-permute-start(bf16[1,1536,1024]{2,1,0:T(8,128)(2,1)} %refs_0_.17), channel_id=1, source_target_pairs={{0,16},{16,0},{1,17},{17,1},{2,18},{18,2},{3,19},{19,3},{4,20},{20... | collective-permute-start | bytes 9437192 | tf_op jit(solution)/shard_map/ppermute | solution.py:34
  8.3 41.3 %collective-permute-start.5 = (bf16[1,1536,1024]{2,1,0:T(8,128)(2,1)}, bf16[1,1536,1024]{2,1,0:T(8,128)(2,1)}, u32[]{:S(2)}, u32[]{:S(2)}) collective-permute-start(bf16[1,1536,1024]{2,1,0:T(8,128)(2,1)} %refs_2_.7), channel_id=1, source_target_pairs={{0,16},{16,0},{1,17},{17,1},{2,18},{18,2},{3,19},{19,3},{4,20},{20... | collective-permute-start | bytes 9437192 | tf_op jit(solution)/shard_map/ppermute | solution.py:34
  8.3 41.3 %collective-permute-start.6 = (bf16[1,1024,1536]{2,1,0:T(8,128)(2,1)}, bf16[1,1024,1536]{2,1,0:T(8,128)(2,1)}, u32[]{:S(2)}, u32[]{:S(2)}) collective-permute-start(bf16[1,1024,1536]{2,1,0:T(8,128)(2,1)} %refs_4_.7), channel_id=1, source_target_pairs={{0,16},{16,0},{1,17},{17,1},{2,18},{18,2},{3,19},{19,3},{4,20},{20... | collective-permute-start | bytes 9437192 | tf_op jit(solution)/shard_map/ppermute | solution.py:34
  20.1 18.7 %collective-permute-start.8 = (bf16[1,384,1536]{2,1,0:T(8,128)(2,1)}, bf16[1,384,1536]{2,1,0:T(8,128)(2,1)S(1)}, u32[]{:S(2)}, u32[]{:S(2)}) collective-permute-start(bf16[1,384,1536]{2,1,0:T(8,128)(2,1)} %refs_0_.18), channel_id=1, source_target_pairs={{0,16},{16,0},{1,17},{17,1},{2,18},{18,2},{3,19},{19,3},{4,20},{20... | collective-permute-start | bytes 3538952 | tf_op jit(solution)/shard_map/ppermute | solution.py:34
  47.6 33.9 %collective-permute-start.19 = (bf16[256,1536]{1,0:T(8,128)(2,1)}, bf16[256,1536]{1,0:T(8,128)(2,1)S(1)}, u32[]{:S(2)}, u32[]{:S(2)}) collective-permute-start(bf16[256,1536]{1,0:T(8,128)(2,1)} %get-tuple-element.116.refs_4_), channel_id=1, source_target_pairs={{0,16},{16,0},{1,17},{17,1},{2,18},{18,2},{3,19},{19,3},{4,20},{20... | collective-permute-start | bytes 2359304 | tf_op jit(solution)/shard_map/ppermute | solution.py:34
  60.5 20.4 %collective-permute-start.7 = (f32[1,1536]{1,0:T(1,128)S(1)}, f32[1,1536]{1,0:T(1,128)S(1)}, u32[]{:S(2)}, u32[]{:S(2)}) collective-permute-start(f32[1,1536]{1,0:T(1,128)S(1)} %copy-done.26), channel_id=1, source_target_pairs={{0,16},{16,0},{1,17},{17,1},{2,18},{18,2},{3,19},{19,3},{4,20},{20... | collective-permute-start | bytes 18440 | tf_op jit(solution)/shard_map/ppermute | solution.py:34
  102.6 38.1 %collective-permute-start.27 = (bf16[256,1536]{1,0:T(8,128)(2,1)}, bf16[256,1536]{1,0:T(8,128)(2,1)S(1)}, u32[]{:S(2)}, u32[]{:S(2)}) collective-permute-start(bf16[256,1536]{1,0:T(8,128)(2,1)} %get-tuple-element.123.refs_0_), channel_id=1, source_target_pairs={{0,16},{16,0},{1,17},{17,1},{2,18},{18,2},{3,19},{19,3},{4,20},{20... | collective-permute-start | bytes 2359304 | tf_op jit(solution)/shard_map/ppermute | solution.py:34
  107.1 24.7 %collective-permute-start.28 = (bf16[256,192]{1,0:T(8,128)(2,1)S(1)}, bf16[256,192]{1,0:T(8,128)(2,1)S(1)}, u32[]{:S(2)}, u32[]{:S(2)}) collective-permute-start(bf16[256,192]{1,0:T(8,128)(2,1)S(1)} %copy-done.40), channel_id=1, source_target_pairs={{0,16},{16,0},{1,17},{17,1},{2,18},{18,2},{3,19},{19,3},{4,20},{20... | collective-permute-start | bytes 294920 | tf_op jit(solution)/shard_map/ppermute | solution.py:34
  156.1 45.4 %collective-permute-start.38 = (bf16[256,1536]{1,0:T(8,128)(2,1)}, bf16[256,1536]{1,0:T(8,128)(2,1)S(1)}, u32[]{:S(2)}, u32[]{:S(2)}) collective-permute-start(bf16[256,1536]{1,0:T(8,128)(2,1)} %get-tuple-element.133.refs_4_), channel_id=1, source_target_pairs={{0,16},{16,0},{1,17},{17,1},{2,18},{18,2},{3,19},{19,3},{4,20},{20... | collective-permute-start | bytes 2359304 | tf_op jit(solution)/shard_map/ppermute | solution.py:34
  209.7 29.8 %collective-permute-start.46 = (bf16[256,1536]{1,0:T(8,128)(2,1)}, bf16[256,1536]{1,0:T(8,128)(2,1)S(1)}, u32[]{:S(2)}, u32[]{:S(2)}) collective-permute-start(bf16[256,1536]{1,0:T(8,128)(2,1)} %get-tuple-element.147.refs_0_), channel_id=1, source_target_pairs={{0,16},{16,0},{1,17},{17,1},{2,18},{18,2},{3,19},{19,3},{4,20},{20... | collective-permute-start | bytes 2359304 | tf_op jit(solution)/shard_map/ppermute | solution.py:34
  219.9 19.6 %collective-permute-start.48 = (bf16[256,1024]{1,0:T(8,128)(2,1)}, bf16[256,1024]{1,0:T(8,128)(2,1)S(1)}, u32[]{:S(2)}, u32[]{:S(2)}) collective-permute-start(bf16[256,1024]{1,0:T(8,128)(2,1)} %get-tuple-element.149), channel_id=1, source_target_pairs={{0,16},{16,0},{1,17},{17,1},{2,18},{18,2},{3,19},{19,3},{4,20},{20... | collective-permute-start | bytes 1572872 | tf_op jit(solution)/shard_map/ppermute | solution.py:34
  220.8 18.7 %collective-permute-start.45 = (bf16[256,512]{1,0:T(8,128)(2,1)S(1)}, bf16[256,512]{1,0:T(8,128)(2,1)S(1)}, u32[]{:S(2)}, u32[]{:S(2)}) collective-permute-start(bf16[256,512]{1,0:T(8,128)(2,1)S(1)} %copy-done.30), channel_id=1, source_target_pairs={{0,16},{16,0},{1,17},{17,1},{2,18},{18,2},{3,19},{19,3},{4,20},{20... | collective-permute-start | bytes 786440 | tf_op jit(solution)/shard_map/ppermute | solution.py:34
  242.2 19.3 %collective-permute-start.50 = (bf16[64,1536]{1,0:T(8,128)(2,1)S(1)}, bf16[64,1536]{1,0:T(8,128)(2,1)S(1)}, u32[]{:S(2)}, u32[]{:S(2)}) collective-permute-start(bf16[64,1536]{1,0:T(8,128)(2,1)S(1)} %add_shares.11.refs_15_.refs_19_), channel_id=1, source_target_pairs={{0,8},{4,12},{8,0},{12,4},{1,9},{5,13},{9,1},{13,5},{2,10},{6,14},... | collective-permute-start | bytes 589832 | tf_op jit(solution)/shard_map/ppermute | solution.py:574
  245.5 29.0 %collective-permute-start.39 = (bf16[64,1536]{1,0:T(8,128)(2,1)S(1)}, bf16[64,1536]{1,0:T(8,128)(2,1)S(1)}, u32[]{:S(2)}, u32[]{:S(2)}) collective-permute-start(bf16[64,1536]{1,0:T(8,128)(2,1)S(1)} %copy-done.39), channel_id=1, source_target_pairs={{0,4},{4,0},{8,12},{12,8},{1,5},{5,1},{9,13},{13,9},{2,6},{6,2},{1... | collective-permute-start | bytes 589832 | tf_op jit(solution)/shard_map/ppermute | solution.py:574
  247.4 28.6 %collective-permute-start.40 = (bf16[64,1536]{1,0:T(8,128)(2,1)S(1)}, bf16[64,1536]{1,0:T(8,128)(2,1)S(1)}, u32[]{:S(2)}, u32[]{:S(2)}) collective-permute-start(bf16[64,1536]{1,0:T(8,128)(2,1)S(1)} %copy-done.38), channel_id=1, source_target_pairs={{0,8},{4,12},{8,0},{12,4},{1,9},{5,13},{9,1},{13,5},{2,10},{6,14},... | collective-permute-start | bytes 589832 | tf_op jit(solution)/shard_map/ppermute | solution.py:574
  249.0 27.1 %collective-permute-start.41 = (bf16[64,1536]{1,0:T(8,128)(2,1)S(1)}, bf16[64,1536]{1,0:T(8,128)(2,1)S(1)}, u32[]{:S(2)}, u32[]{:S(2)}) collective-permute-start(bf16[64,1536]{1,0:T(8,128)(2,1)S(1)} %copy-done.37), channel_id=1, source_target_pairs={{0,12},{4,8},{8,4},{12,0},{1,13},{5,9},{9,5},{13,1},{2,14},{6,10},... | collective-permute-start | bytes 589832 | tf_op jit(solution)/shard_map/ppermute | solution.py:574
  315.9 119.1 %reduce-scatter.10.cloned.1.call-start = ((), (), s32[]{:S(2)}) async-start(), calls=%async_computation.3 | async-start | bytes 5898240
  316.7 177.6 %reduce-scatter.14.cloned.1.call-start = ((), (), s32[]{:S(2)}) async-start(), calls=%async_computation.5 | async-start | bytes 5898240
  401.5 33.6 %collective-permute-start.78 = (bf16[256,1536]{1,0:T(8,128)(2,1)}, bf16[256,1536]{1,0:T(8,128)(2,1)S(1)}, u32[]{:S(2)}, u32[]{:S(2)}) collective-permute-start(bf16[256,1536]{1,0:T(8,128)(2,1)} %get-tuple-element.186.refs_0_), channel_id=1, source_target_pairs={{0,16},{16,0},{1,17},{17,1},{2,18},{18,2},{3,19},{19,3},{4,20},{20... | collective-permute-start | bytes 2359304 | tf_op jit(solution)/shard_map/ppermute | solution.py:34
  450.0 31.8 %collective-permute-start.88 = (bf16[384,576]{1,0:T(8,128)(2,1)}, bf16[384,576]{1,0:T(8,128)(2,1)S(1)}, u32[]{:S(2)}, u32[]{:S(2)}) collective-permute-start(bf16[384,576]{1,0:T(8,128)(2,1)} %get-tuple-element.197), channel_id=1, source_target_pairs={{0,3},{1,2},{2,1},{3,0},{4,7},{5,6},{6,5},{7,4},{8,11},{9,10},{10,... | collective-permute-start | bytes 1327112 | tf_op jit(solution)/shard_map/ppermute | solution.py:810
  457.3 26.8 %collective-permute-start.85 = (bf16[64,1536]{1,0:T(8,128)(2,1)S(1)}, bf16[64,1536]{1,0:T(8,128)(2,1)S(1)}, u32[]{:S(2)}, u32[]{:S(2)}) collective-permute-start(bf16[64,1536]{1,0:T(8,128)(2,1)S(1)} %add_shares.15.refs_4_.refs_3_), channel_id=1, source_target_pairs={{0,12},{4,8},{8,4},{12,0},{1,13},{5,9},{9,5},{13,1},{2,14},{6,10},... | collective-permute-start | bytes 589832 | tf_op jit(solution)/shard_map/ppermute | solution.py:574
  458.8 25.3 %collective-permute-start.84 = (bf16[64,1536]{1,0:T(8,128)(2,1)S(1)}, bf16[64,1536]{1,0:T(8,128)(2,1)S(1)}, u32[]{:S(2)}, u32[]{:S(2)}) collective-permute-start(bf16[64,1536]{1,0:T(8,128)(2,1)S(1)} %add_shares.15.refs_4_.refs_3_), channel_id=1, source_target_pairs={{0,8},{4,12},{8,0},{12,4},{1,9},{5,13},{9,1},{13,5},{2,10},{6,14},... | collective-permute-start | bytes 589832 | tf_op jit(solution)/shard_map/ppermute | solution.py:574
  464.9 19.2 %collective-permute-start.83 = (bf16[64,1536]{1,0:T(8,128)(2,1)S(1)}, bf16[64,1536]{1,0:T(8,128)(2,1)S(1)}, u32[]{:S(2)}, u32[]{:S(2)}) collective-permute-start(bf16[64,1536]{1,0:T(8,128)(2,1)S(1)} %add_shares.15.refs_4_.refs_3_), channel_id=1, source_target_pairs={{0,4},{4,0},{8,12},{12,8},{1,5},{5,1},{9,13},{13,9},{2,6},{6,2},{1... | collective-permute-start | bytes 589832 | tf_op jit(solution)/shard_map/ppermute | solution.py:574
  (116 other events, 1213.6 us)
Sparse Core Ops, SparseCore 0:
  316.1 35.6 reduce-scatter.11
  354.7 57.0 reduce-scatter.9
  414.8 74.1 reduce-scatter.13

commit v3 on v2

--- a/solution.py
+++ b/solution.py
@@ -15,7 +15,6 @@
 F32 = jnp.float32
 FACTOR = HEAD_DIM ** (-0.5)
 TILE = 256
-AHEAD = 6
 
 
 def dot(left, right):
@@ -93,6 +92,10 @@
     other = swap(value)
     Order.pending.append(other)
     return other
+
+
+def follow(own, value):
+    return [(weight, swap(weight)) for weight in lax.optimization_barrier((*own, value))[:-1]]
 
 
 def collect():
@@ -184,6 +187,49 @@
     pltpu.make_async_copy(own, buffer, sem).wait()
 
 
+def bring_body(layer, groups, ins, outs, sem):
+    copies, place = [], 0
+    for group, out in zip(groups, outs):
+        start = 0
+        for _ in range(group):
+            own, other = ins[2 * place : 2 * place + 2]
+            count = own.shape[1]
+            copies.append((own.at[0], other.at[0], out.at[pl.ds(start, count)], sem.at[place]))
+            start += count
+            place += 1
+    if copies:
+        fetch(layer, copies)
+    rest = [
+        pltpu.make_async_copy(source, out, sem.at[index])
+        for index, (source, out) in enumerate(zip(ins[2 * place :], outs[len(groups) :]), place)
+    ]
+    for copy in rest:
+        copy.start()
+    for own, _, buffer, one in copies:
+        arrived(own, buffer, one)
+    for copy in rest:
+        copy.wait()
+
+
+def bring(layer, name, groups, values):
+    shapes = []
+    for group in groups:
+        count = sum(own.shape[1] for own, _ in group)
+        shapes.append(shape((count, group[0][0].shape[2]), BF))
+    shapes += [shape(value.shape, value.dtype) for value in values]
+    pairs = [pair for group in groups for pair in group]
+    return near(
+        kernel_call(
+            functools.partial(bring_body, layer, [len(group) for group in groups]),
+            name,
+            weights(pairs) + raw(values),
+            near(shapes),
+            [pltpu.SemaphoreType.DMA((len(pairs) + len(values),))],
+            cost=2.0,
+        )
+    )
+
+
 def share_of(step, size):
     start = lax.bitwise_xor(lax.axis_index("tensor"), step) * size
     return pl.ds(pl.multiple_of(start, size), size)
@@ -207,6 +253,17 @@
     left, right = value[:, :half], value[:, half:]
     mine_out[...] = jnp.where(early, left, right)
     theirs_out[...] = jnp.where(early, right, left)
+
+
+def send_half(source, mine_out, theirs_out, place, in_first):
+    mine = (lax.axis_index("section") == 0) == in_first
+    for chosen, out in ((mine, mine_out), (jnp.logical_not(mine), theirs_out)):
+
+        @pl.when(chosen)
+        def _(out=out):
+            pltpu.make_async_copy(source, out.target.at[:, place], out.sem).start()
+
+        out.started = True
 
 
 def norm_scale(values):
@@ -244,18 +301,20 @@
     ]
 
 
-def norm_qkv(layer, first, ins, outs, q_buf, kv_buf, rows_buf, sem):
+def norm_qkv(layer, first, ins, outs, *scratch):
     gain, cosine, sine = ins[:3]
-    wq, wk, wv = ins[3:5], ins[5:7], ins[7:9]
-    query_out, kv_out, normed_out = outs[:3]
-    copies = qkv_copies(wq, wk, wv, q_buf, kv_buf, sem)
-    fetch(layer, copies)
+    query_out, kv_out, normed_out, query_saved = outs[:4]
+    copies = []
     if first:
+        q_buf, kv_buf, sem = scratch
+        copies = qkv_copies(ins[3:5], ins[5:7], ins[7:9], q_buf, kv_buf, sem)
+        fetch(layer, copies)
         hidden = ins[9][...].astype(F32)
     else:
-        low = (ins[9][...] + summed(ins[10:], rows_buf)).astype(BF)
-        outs[3][...] = low
-        outs[3].send()
+        q_buf, kv_buf = ins[3:5]
+        low = (ins[5][...].astype(F32) + summed(ins[6:], scratch[0])).astype(BF)
+        outs[4][...] = low
+        outs[4].send()
         hidden = low.astype(F32)
     normed = (hidden * norm_scale(hidden) * gain[...]).astype(BF)
     normed_out[...] = normed
@@ -264,9 +323,11 @@
     key_cos, key_sin = key_tables(cos, sin)
     for own, _, buffer, one in copies:
         arrived(own, buffer, one)
+    query = rotate(dot(normed, q_buf[...]), cos, sin).astype(BF)
+    query_saved[...] = query
+    query_saved.send()
+    query_out[...] = query
     kv_out[...] = rotate(dot_t(normed, kv_buf[...]), key_cos, key_sin).astype(BF)
-    kv_out.send()
-    query_out[...] = rotate(dot(normed, q_buf[...]), cos, sin).astype(BF)
 
 
 def split_keys(kv_refs, k_buf, v_buf):
@@ -281,15 +342,16 @@
             v_buf[group, index * rows : (index + 1) * rows, :] = block[:, low : low + HEAD_DIM]
 
 
-def attention(layer, peers, ins, outs, q_buf, k_buf, v_buf, wo_buf, sum_buf, sem):
-    wo, wo_other, query, bias = ins[:4]
-    kv_refs = ins[4:]
-    mine_out, theirs_out, attn_out, lse_out = outs[:4]
-    fetch(layer, [(wo.at[0], wo_other.at[0], wo_buf, sem)])
+def attention(ins, outs, q_buf, sum_buf):
+    wo_buf, bias, query = ins[:3]
+    kv_refs = ins[3:]
+    mine_out, theirs_out, attn_out, lse_out, k_buf, v_buf = outs[:6]
     heads = q_buf.shape[0]
-    group_size = heads // k_buf.shape[0]
+    group_size = heads // k_buf.buffer.shape[0]
     split_query(query[...], q_buf)
-    split_keys(kv_refs, k_buf, v_buf)
+    split_keys(kv_refs, k_buf.buffer, v_buf.buffer)
+    k_buf.send()
+    v_buf.send()
     results, totals = [], []
     for head in range(heads):
         group = head // group_size
@@ -306,9 +368,8 @@
     lse_out[...] = jnp.concatenate(totals, axis=1)
     rows = attn.astype(BF)
     store_halves(rows, mine_out, theirs_out)
-    arrived(wo.at[0], wo_buf, sem)
     sum_buf[...] = dot(rows, wo_buf[...])
-    store_shares(sum_buf, outs[4:])
+    store_shares(sum_buf, outs[6:])
 
 
 def split_query(query, q_buf):
@@ -316,78 +377,54 @@
         q_buf[head] = query[:, head * HEAD_DIM : (head + 1) * HEAD_DIM]
 
 
-def mlp_copies(wg, wu, wd, g_buf, u_buf, d_buf, sem):
-    copies = []
-    for step in range(g_buf.shape[0]):
-        part = pl.ds(step * TILE, TILE)
-        copies.append((wg[0].at[0, :, part], wg[1].at[0, :, part], g_buf.at[step], sem.at[0, step]))
-        copies.append((wu[0].at[0, :, part], wu[1].at[0, :, part], u_buf.at[step], sem.at[1, step]))
-        copies.append((wd[0].at[0, part, :], wd[1].at[0, part, :], d_buf.at[step], sem.at[2, step]))
-    return copies
-
-
-def mlp(layer, ins, outs, g_buf, u_buf, d_buf, total, rows_buf, act_buf, sem):
-    wg, wu, wd = ins[0:2], ins[2:4], ins[4:6]
-    hidden, gain = ins[6:8]
+def mlp(ins, outs, total, rows_buf, act_buf):
+    wg, wu, wd, hidden, gain = ins[:5]
     middle_out, normed_out, gate_out, up_out, mine_out, theirs_out = outs[:6]
-    copies = mlp_copies(wg, wu, wd, g_buf, u_buf, d_buf, sem)
-    fetch(layer, copies[:AHEAD])
-    middle = hidden[...].astype(F32) + summed(ins[8:], rows_buf)
-    middle_out[...] = middle
+    middle = hidden[...].astype(F32) + summed(ins[5:], rows_buf)
+    middle_out[...] = middle.astype(BF)
     middle_out.send()
     normed_out[...] = (middle * norm_scale(middle) * gain[...]).astype(BF)
     normed_out.send()
-    for step in range(g_buf.shape[0]):
-        if len(copies) > 3 * step + AHEAD:
-            fetch(layer, copies[3 * step + AHEAD : 3 * step + 3 + AHEAD])
-        for own, _, buffer, one in copies[3 * step : 3 * step + 3]:
-            arrived(own, buffer, one)
+    for step in range(wg.shape[1] // TILE):
         part = slice(step * TILE, (step + 1) * TILE)
-        gate = dot(normed_out[...], g_buf[step])
-        upward = dot(normed_out[...], u_buf[step])
-        gate_out[:, part] = gate
-        up_out[:, part] = upward
+        gate = dot(normed_out[...], wg[:, part])
+        upward = dot(normed_out[...], wu[:, part])
+        gate_out[:, part] = gate.astype(BF)
+        up_out[:, part] = upward.astype(BF)
         act = (gate * jax.nn.sigmoid(gate) * upward).astype(BF)
         gate_out.send((slice(None), part))
         up_out.send((slice(None), part))
         act_buf[:, part] = act
-        term = dot(act, d_buf[step])
+        half = act_buf.shape[1] // 2
+        place = slice(step * TILE % half, step * TILE % half + TILE)
+        send_half(act_buf.at[:, part], mine_out, theirs_out, place, step * TILE < half)
+        term = dot(act, wd[part, :])
         if step == 0:
             total[...] = term
         else:
             total[...] += term
-    store_halves(act_buf[...], mine_out, theirs_out)
-    theirs_out.send()
-    mine_out.send()
     store_shares(total, outs[6:])
 
 
-def mlp_back(layer, last, ins, outs, g_buf, u_buf, d_buf, total, rows_buf, sem):
-    wg, wu, wd = ins[0:2], ins[2:4], ins[4:6]
-    gate_ref, up_ref = ins[6:8]
+def mlp_back(last, ins, outs, total, rows_buf):
+    wg, wu, wd, gate_ref, up_ref = ins[:5]
     mine_out, theirs_out = outs[:2]
     shares = outs[2:] if last else outs[2:-2]
-    copies = mlp_copies(wg, wu, wd, g_buf, u_buf, d_buf, sem)
-    fetch(layer, copies[:AHEAD])
     early = lax.axis_index("section") == 0
     if last:
-        grad_ref = ins[8]
+        grad_ref = ins[5]
     else:
-        middle_grad, hidden, gain = ins[8:11]
+        middle_grad, hidden, gain = ins[5:8]
         grad_ref, gain_out = outs[-2:]
-        values, grad = hidden[...].astype(F32), summed(ins[11:], rows_buf)
+        values, grad = hidden[...].astype(F32), summed(ins[8:], rows_buf)
         scale = norm_scale(values)
         gain_out[...] = jnp.sum(grad * values * scale, axis=0, keepdims=True)
-        grad_ref[...] = (middle_grad[...] + norm_back(values, scale, gain[...], grad)).astype(BF)
+        grad_ref[...] = (middle_grad[...].astype(F32) + norm_back(values, scale, gain[...], grad)).astype(BF)
         grad_ref.send()
-    for step in range(g_buf.shape[0]):
-        if len(copies) > 3 * step + AHEAD:
-            fetch(layer, copies[3 * step + AHEAD : 3 * step + 3 + AHEAD])
-        for own, _, buffer, one in copies[3 * step : 3 * step + 3]:
-            arrived(own, buffer, one)
+    for step in range(wg.shape[1] // TILE):
         part = slice(step * TILE, (step + 1) * TILE)
-        act_grad = dot_t(grad_ref[...], d_buf[step])
-        gate, upward = gate_ref[:, part], up_ref[:, part]
+        act_grad = dot_t(grad_ref[...], wd[part, :])
+        gate, upward = gate_ref[:, part].astype(F32), up_ref[:, part].astype(F32)
         sigma = jax.nn.sigmoid(gate)
         gate_grad = (act_grad * upward * sigma * (1.0 + gate * (1.0 - sigma))).astype(BF)
         up_grad = (act_grad * gate * sigma).astype(BF)
@@ -395,7 +432,7 @@
         theirs_out[:, part] = jnp.where(early, up_grad, gate_grad)
         theirs_out.send((slice(None), part))
         mine_out.send((slice(None), part))
-        term = dot_t(gate_grad, g_buf[step]) + dot_t(up_grad, u_buf[step])
+        term = dot_t(gate_grad, wg[:, part]) + dot_t(up_grad, wu[:, part])
         if step == 0:
             total[...] = term
         else:
@@ -403,27 +440,22 @@
     store_shares(total, shares)
 
 
-def attention_back(layer, peers, ins, outs, q_buf, k_buf, v_buf, dk_buf, dv_buf, wo_buf, rows_buf, sem):
-    wo, wo_other, grad_in, middle, gain, query, bias, attn, lse, cosine, sine = ins[:11]
-    kv_refs, sums = ins[11 : 11 + peers], ins[11 + peers :]
-    middle_grad_out, low_out, gain_out, pre_out = outs[:4]
-    block_outs = outs[4:]
-    fetch(layer, [(wo.at[0], wo_other.at[0], wo_buf, sem)])
+def attention_back(peers, ins, outs, q_buf, dk_buf, dv_buf, rows_buf):
+    wo_buf, grad_in, middle, gain, query, bias, attn, lse, cosine, sine, k_buf, v_buf = ins[:12]
+    sums = ins[12:]
+    low_out, gain_out, pre_out = outs[:3]
+    block_outs = outs[3:]
     heads, groups = q_buf.shape[0], k_buf.shape[0]
     group_size = heads // groups
     grad = summed(sums, rows_buf)
-    values = middle[...]
+    values = middle[...].astype(F32)
     scale = norm_scale(values)
     gain_out[...] = jnp.sum(grad * values * scale, axis=0, keepdims=True)
     middle_grad = grad_in[...].astype(F32) + norm_back(values, scale, gain[...], grad)
-    middle_grad_out[...] = middle_grad
-    middle_grad_out.send()
     low_out[...] = middle_grad.astype(BF)
     low_out.send()
-    arrived(wo.at[0], wo_buf, sem)
     attn_grad = dot_t(low_out[...], wo_buf[...]).astype(BF)
     split_query(query[...], q_buf)
-    split_keys(kv_refs, k_buf, v_buf)
     query_grads = []
     for head in range(heads):
         group = head // group_size
@@ -457,14 +489,11 @@
     pre_out[...] = rotate(query_grad, cosine[...], -sine[...]).astype(BF)
 
 
-def qkv_back(layer, ins, outs, q_buf, kv_buf, total, sem):
-    wq, wk, wv = ins[0:2], ins[2:4], ins[4:6]
-    pre_query, cosine, sine, own = ins[6:10]
+def qkv_back(ins, outs, total):
+    q_buf, kv_buf, cosine, sine, pre_query, own = ins[:6]
     mine_out, theirs_out = outs[:2]
-    copies = qkv_copies(wq, wk, wv, q_buf, kv_buf, sem)
-    fetch(layer, copies)
     both = own[...]
-    for ref in ins[10:]:
+    for ref in ins[6:]:
         both = both + ref[...].astype(F32)
     key_cos, key_sin = key_tables(cosine[...], sine[...])
     pre = rotate(both, key_cos, -key_sin).astype(BF)
@@ -474,21 +503,19 @@
     theirs_out[...] = jnp.where(early, pre, pre_q)
     theirs_out.send()
     mine_out.send()
-    for own_weight, _, buffer, one in copies:
-        arrived(own_weight, buffer, one)
     total[...] = dot_t(pre_q, q_buf[...]) + dot(pre, kv_buf[...])
     store_shares(total, outs[2:])
 
 
 def last_output(ins, outs, rows_buf):
-    outs[0][...] = (ins[0][...] + summed(ins[1:], rows_buf)).astype(BF)
+    outs[0][...] = (ins[0][...].astype(F32) + summed(ins[1:], rows_buf)).astype(BF)
 
 
 def finish(ins, outs, rows_buf):
     middle_grad, hidden, gain = ins[:3]
     values, grad = hidden[...].astype(F32), summed(ins[3:], rows_buf)
     scale = norm_scale(values)
-    outs[0][...] = (middle_grad[...] + norm_back(values, scale, gain[...], grad)).astype(BF)
+    outs[0][...] = (middle_grad[...].astype(F32) + norm_back(values, scale, gain[...], grad)).astype(BF)
     outs[0].send()
     outs[1][...] = jnp.sum(grad * values * scale, axis=0, keepdims=True)
 
@@ -640,15 +667,13 @@
     q_width, kv_width, ff = w_query.shape[2], w_key.shape[2], w_gate.shape[2]
     heads, groups = q_width // HEAD_DIM, kv_width // HEAD_DIM
     tokens = rows * peers
-    steps = ff // TILE
     shares = lax.axis_size("tensor")
 
     def pick(early, late):
         return jnp.where(first, early, late)
 
     own = [w_query, jnp.swapaxes(w_key, 1, 2), jnp.swapaxes(w_value, 1, 2), w_out, w_gate, w_up, w_down]
-    pairs = [(weight, swap(weight)) for weight in own]
-    wq, wk, wv, wo, wg, wu, wd = pairs
+    wq, wk, wv = [(weight, swap(weight)) for weight in own[:3]]
     gains = []
     for gain in (norm1_gain, norm2_gain):
         other = swap(gain)
@@ -686,100 +711,87 @@
         pltpu.VMEM((width, q_width), BF),
         pltpu.VMEM((2 * kv_width, width), BF),
     ]
-    mlp_scratch = [
-        pltpu.VMEM((steps, width, TILE), BF),
-        pltpu.VMEM((steps, width, TILE), BF),
-        pltpu.VMEM((steps, TILE, width), BF),
-        total_buf,
-        rows_buf,
-    ]
-    head_scratch = [
-        pltpu.VMEM((heads, rows, HEAD_DIM), BF),
-        pltpu.VMEM((groups, tokens, HEAD_DIM), BF),
-        pltpu.VMEM((groups, tokens, HEAD_DIM), BF),
-    ]
-
-    def run_qkv(layer, source, sums, after):
+    mlp_scratch = [total_buf, rows_buf]
+    keys_bf = shape((groups, tokens, HEAD_DIM), BF)
+    head_scratch = [pltpu.VMEM((heads, rows, HEAD_DIM), BF)]
+
+    def run_qkv(layer, ins, after):
         start = layer == 0
-        outs = [head_bf, kv_bf, row_bf]
+        outs = near([head_bf, kv_bf]) + far([row_bf, head_bf])
         return kernel_call(
             functools.partial(norm_qkv, layer, start),
             f"norm_qkv_{layer}",
-            far([gains[0][layer], cosine, sine]) + weights([wq, wk, wv]) + far([source]) + near(sums),
-            far(outs if start else outs + [row_bf]),
-            qkv_scratch + [rows_buf, dma((3,))],
+            ins,
+            outs if start else outs + far([row_bf]),
+            qkv_scratch + [dma((3,))] if start else [rows_buf],
             after,
             cost=4.0,
         )
 
-    def run_attention(layer, query, blocks, after):
-        outs = [half_head] * 2 + [shape((rows, q_width), F32), shape((rows, heads), F32)]
+    def run_attention(layer, brought, query, blocks, after):
+        outs = [half_head] * 2 + [shape((rows, q_width), F32), shape((rows, heads), F32)] + [keys_bf] * 2
         return kernel_call(
-            functools.partial(attention, layer, peers),
+            attention,
             f"attention_{layer}",
-            weights([wo]) + far([query, bias, *blocks]),
+            brought + near([query, *blocks]),
             far(outs) + share_outs,
-            head_scratch + [pltpu.VMEM((q_width, width), BF), total_buf, dma],
+            head_scratch + [total_buf],
             after,
             cost=5.0,
-            limit=min(8 + 4 * peers, 56),
-        )
-
-    def run_mlp(layer, hidden, sums, after):
+            limit=min(8 + 4 * peers, 28),
+        )
+
+    def run_mlp(layer, brought, sums, after):
         return kernel_call(
-            functools.partial(mlp, layer),
+            mlp,
             f"mlp_{layer}",
-            weights([wg, wu, wd]) + far([hidden, gains[1][layer]]) + near(sums),
-            far([row_f32, row_bf, wide_f32, wide_f32, half_wide, half_wide])
+            brought + near(sums),
+            far([row_bf, row_bf, wide_bf, wide_bf, half_wide, half_wide])
             + (share_outs if layer == 0 else far([share] * shares)),
-            mlp_scratch + [pltpu.VMEM((rows, ff), BF), dma((3, steps))],
+            mlp_scratch + [pltpu.VMEM((rows, ff), BF)],
             after,
             cost=6.0,
-            limit=32,
-        )
-
-    def run_mlp_back(layer, source, sums, gate, upward, after):
+            limit=24,
+        )
+
+    def run_mlp_back(layer, brought, sums, after):
         last = layer == 1
         outs = far([wide_bf, wide_bf]) + share_outs
         return kernel_call(
-            functools.partial(mlp_back, layer, last),
+            functools.partial(mlp_back, last),
             f"mlp_back_{layer}",
-            weights([wg, wu, wd]) + far([gate, upward, *source]) + near(sums),
+            brought + near(sums),
             outs if last else outs + far([row_bf, line]),
-            mlp_scratch + [dma((3, steps))],
+            mlp_scratch,
             after,
             cost=8.0,
-            limit=32,
-        )
-
-    def run_attention_back(layer, grad, middle, sums, query, blocks, attn, lse, after):
+            limit=24,
+        )
+
+    def run_attention_back(layer, brought, sums, after):
         return kernel_call(
-            functools.partial(attention_back, layer, peers),
+            functools.partial(attention_back, peers),
             f"attention_back_{layer}",
-            weights([wo])
-            + far([grad, middle, gains[1][layer], query, bias, attn, lse, cosine, sine, *blocks])
-            + near(sums),
-            far([row_f32, row_bf, line, head_bf, shape((rows, 2 * kv_width), F32)] + [kv_bf] * (peers - 1)),
+            brought + near(sums),
+            far([row_bf, line, head_bf, shape((rows, 2 * kv_width), F32)] + [kv_bf] * (peers - 1)),
             head_scratch
             + [
                 pltpu.VMEM((groups, tokens, HEAD_DIM), F32),
                 pltpu.VMEM((groups, tokens, HEAD_DIM), F32),
-                pltpu.VMEM((q_width, width), BF),
                 rows_buf,
-                dma,
             ],
             after,
             cost=9.0,
-            limit=min(16 + 4 * peers, 56),
-        )
-
-    def run_qkv_back(layer, pre_query, pieces, after):
+            limit=min(8 + 4 * peers, 40),
+        )
+
+    def run_qkv_back(layer, brought, pieces, after):
         return kernel_call(
-            functools.partial(qkv_back, layer),
+            qkv_back,
             f"qkv_back_{layer}",
-            weights([wq, wk, wv]) + far([pre_query, cosine, sine]) + loose(pieces),
+            brought + loose(pieces),
             far([kv_bf, kv_bf]) + share_outs,
-            qkv_scratch + [total_buf, dma((3,))],
+            [total_buf],
             after,
             cost=4.0,
         )
@@ -831,35 +843,53 @@
     hidden = pick(layer_input[0], layer_input[1])
     grad = pick(out_grad[0], out_grad[1])
     saved, outputs = [], []
-    grad_other = soon(grad)
     for layer in range(2):
         if layer == 0:
-            query, kv, normed_one = run_qkv(layer, hidden, [], [])
+            ins = far([gains[0][layer], cosine, sine]) + weights([wq, wk, wv]) + far([hidden])
+            query, kv, normed_one, query_saved = run_qkv(layer, ins, [])
         else:
-            query, kv, normed_one, hidden = run_qkv(layer, middle, sums, collect())
+            ins = ready[2:5] + ready[:2] + ready[5:] + near(sums)
+            query, kv, normed_one, query_saved, hidden = run_qkv(layer, ins, collect())
             outputs.append(hidden)
+        if layer == 0:
+            wo, wg = follow(own[3:5], normed_one)
         blocks = [kv]
         for step in range(1, peers):
             blocks.append(lax.ppermute(kv, "dp", peer_pairs(peers, step, False)))
         early = collect()
         if layer == 0:
-            early += raw([other for _, other in pairs])
-        normed_one = (normed_one, soon(normed_one))
-        *results, attn, lse = (outs := run_attention(layer, query, blocks, early))[:-shares]
-        sums = sum_tensor(outs[-shares:])
+            early += raw([wg[1]])
+        else:
+            grad_other = soon(grad)
+            early += collect()
+        ready = bring(layer, f"bring_attention_{layer}", [[wo]], [bias])
+        *results, attn, lse, keys, values = (outs := run_attention(layer, ready, query, blocks, early))[:-shares]
+        received = spread(outs[-shares:])
+        if layer == 0:
+            wu, wd = follow(own[5:], results[1])
+            total = add_rows(received, raw([wu[1], wd[1]]))
+        else:
+            total = add_rows(received)
+        swapped, theirs, _ = lax.optimization_barrier((normed_one, results[1], total))
+        normed_one = (normed_one, soon(swapped))
+        head_halves = (results[0], soon(theirs))
+        sums = spread([total] * shares)
+        ready = bring(layer, f"bring_mlp_{layer}", [[wg], [wu], [wd]], [hidden, gains[1][layer]])
         early = collect()
-        head_halves = (results[0], soon(results[1]))
         middle, normed_two, gate, upward, act_mine, act_theirs, *parts = run_mlp(
-            layer, hidden, sums, early
+            layer, ready, sums, early
         )
         if layer == 0:
             sums = sum_tensor(parts)
+            ready = bring(
+                1, "bring_qkv_1", [[wq], [wk, wv]], [gains[0][1], cosine, sine, middle]
+            )
         early = collect()
         act_halves = (act_mine, soon(act_theirs))
         normed_two = (normed_two, soon(normed_two))
         Order.pending += [value for value, _ in early]
         saved.append(
-            (hidden, query, blocks, normed_one, head_halves, attn, lse)
+            (hidden, query_saved, (keys, values), normed_one, head_halves, attn, lse)
             + (middle, normed_two, gate, upward, act_halves)
         )
 
@@ -870,10 +900,10 @@
         (hidden, query, blocks, normed_one, head_halves, attn, lse) = saved[layer][:7]
         (middle, normed_two, gate, upward, act_halves) = saved[layer][7:]
         if layer == 1:
-            mine, theirs, *parts = run_mlp_back(layer, source, sums, gate, upward, [])
+            mine, theirs, *parts = run_mlp_back(layer, ready[:3] + far([gate, upward, grad]), [], [])
         else:
             mine, theirs, *parts, grad, gain_one = run_mlp_back(
-                layer, source, sums, gate, upward, []
+                layer, ready + far([gate, upward, *source]), sums, []
             )
             in_grads[1] = grad
         if layer == 0:
@@ -887,9 +917,13 @@
         else:
             mlp_totals[0] = weight_grad(mlp_groups, "grad_mlp_0", False)
             due = []
-        middle_grad, low, gain_two, pre_query, *pieces = run_attention_back(
-            layer, grad, middle, sums, query, blocks, attn, lse, due
-        )
+        brought = bring(
+            layer,
+            f"bring_attention_back_{layer}",
+            [[wo]],
+            [grad, middle, gains[1][layer], query, bias, attn, lse, cosine, sine, *blocks],
+        )
+        low, gain_two, pre_query, *pieces = run_attention_back(layer, brought, sums, due)
         low_other = soon(low)
         far_pieces = [
             lax.ppermute(pieces[step], "dp", peer_pairs(peers, step, True))
@@ -910,8 +944,14 @@
                 cost=2.0,
             )
             outputs.append(output)
+        ready = bring(
+            layer,
+            f"bring_qkv_back_{layer}",
+            [[wq], [wk, wv]],
+            [cosine, sine, pre_query, pieces[0]],
+        )
         mine, theirs, *parts = run_qkv_back(
-            layer, pre_query, [pieces[0]] + far_pieces, collect() + (raw([mlp_totals[1], head_later]) if layer == 0 else [])
+            layer, ready, far_pieces, collect() + (raw([mlp_totals[1], head_later]) if layer == 0 else [])
         )
         head_groups = [(low, low_other, *head_halves), (*normed_one, mine, soon(theirs))]
         received = spread(parts)
@@ -922,12 +962,13 @@
         else:
             sums = spread([add_rows(received, collect())] * shares)
             head_later = weight_grad(head_groups, "grad_head_1", False)
-        source = [middle_grad, hidden, gains[0][layer]]
+            ready = bring(0, "bring_mlp_back_0", [[wg], [wu], [wd]], [])
+        source = [low, hidden, gains[0][layer]]
         vectors[layer] = gain_two
     in_grads[0], last_line = kernel_call(
         finish,
         "finish",
-        far(source) + near(sums),
+        bring(0, "bring_finish", [], source) + near(sums),
         far([row_bf, line]),
         [rows_buf],
     )

time: 518 us -> 489 us (0.944)
  waiting for transfers between devices: 226 us -> 185 us
  local copies, waits for them, and re-layouts: 7.07 us -> 18.1 us
  starting transfers between devices: 124 us -> 130 us
    ppermute x29, waiting for transfers between devices: 12.2 us -> 1.05 us  [swap(): return lax.ppermute(value, 'section', [(0, 1), (1, 0)])]
    unnamed x84 -> x100, local copies, waits for them, and re-layouts: 5.15 us -> 16.2 us
    ppermute x6, waiting for transfers between devices: 15 us -> 4.12 us  [per_device(): lax.ppermute(pieces[step], 'dp', peer_pairs(peers, step, True))]
    ppermute x48, waiting for transfers between devices: 170 us -> 159 us  [spread(): lax.ppermute(values[step], 'tensor', [(peer, peer ^ step) for peer in ran...]
    ppermute x6, waiting for transfers between devices: 8.65 us -> 1.93 us  [per_device(): blocks.append(lax.ppermute(kv, 'dp', peer_pairs(peers, step, False)))]
    ppermute x3, waiting for transfers between devices: 15.6 us -> 10.3 us  [weight_grad(): pieces.append(lax.ppermute(blocks[step], 'dp', pairing))]
    pallas_call x29 -> x40, Pallas kernels: 125 us -> 121 us  [kernel_call(): results = call(*[fixed(value, where) for value, where in [*ins, *after]])]
  transfers between devices with their start and end apart: 98 -> 98, of which waited for: 40 -> 31; matrix products, arithmetic and copies ran while one was open for 4% -> 4% of each run, Pallas kernels for 18% -> 18%
where the time goes in v3:
time: 489 us; the launch traced here: 485 us
  waiting for transfers between devices  185 us (38%)
  starting transfers between devices  130 us (27%)
  Pallas kernels  121 us (25%)
  local copies, waits for them, and re-layouts  18.1 us (4%)
  other arithmetic  16.5 us (3%)
  between operations  15.4 us (3%)
    ppermute x48, waiting for transfers between devices, spread(): lax.ppermute(values[step], 'tensor', [(peer, peer ^ step) for peer in ran...  159 us
    pallas_call x40, Pallas kernels, kernel_call(): results = call(*[fixed(value, where) for value, where in [*ins, *after]])  121 us
    ppermute x48, starting transfers between devices, spread(): lax.ppermute(values[step], 'tensor', [(peer, peer ^ step) for peer in ran...  89.4 us
    ppermute x6, starting transfers between devices, per_device(): blocks.append(lax.ppermute(kv, 'dp', peer_pairs(peers, step, False)))  19.2 us
    unnamed x100, local copies, waits for them, and re-layouts  16.2 us
    ppermute x3, waiting for transfers between devices, weight_grad(): pieces.append(lax.ppermute(blocks[step], 'dp', pairing))  10.3 us
  transfers between devices with their start and end apart: 98, of which 31 were waited for; matrix products, arithmetic and copies ran while one was open for 4% of the time, Pallas kernels for 18%

profile of v3, /device:TPU:0, one launch (start us, length us, event | category | flops | bytes accessed | tf_op | source)
XLA Modules:
  0.0 485.3 jit_solution(15664989610952699114)
XLA Ops:
  47.7 6.1 %collective-permute-done.12.refs_1_ = bf16[64,1536]{1,0:T(8,128)(2,1)S(1)} collective-permute-done((bf16[64,1536]{1,0:T(8,128)(2,1)S(1)}, bf16[64,1536]{1,0:T(8,128)(2,1)S(1)}, u32[]{:S(2)}, u32[]{:S(2)}) %collective-permute-start.12) | collective-permute-done | bytes 196640 | tf_op jit(solution)/shard_map/ppermute | solution.py:601
  53.8 8.2 %collective-permute-done.13.refs_2_ = bf16[64,1536]{1,0:T(8,128)(2,1)S(1)} collective-permute-done((bf16[64,1536]{1,0:T(8,128)(2,1)S(1)}, bf16[64,1536]{1,0:T(8,128)(2,1)S(1)}, u32[]{:S(2)}, u32[]{:S(2)}) %collective-permute-start.13) | collective-permute-done | bytes 196640 | tf_op jit(solution)/shard_map/ppermute | solution.py:601
  76.0 11.4 %collective-permute-done.16.refs_7_ = bf16[64,1536]{1,0:T(8,128)(2,1)S(1)} collective-permute-done((bf16[64,1536]{1,0:T(8,128)(2,1)S(1)}, bf16[64,1536]{1,0:T(8,128)(2,1)S(1)}, u32[]{:S(2)}, u32[]{:S(2)}) %collective-permute-start.16) | collective-permute-done | bytes 196640 | tf_op jit(solution)/shard_map/ppermute | solution.py:601
  96.0 6.6 %collective-permute-done.20.refs_1_ = bf16[64,1536]{1,0:T(8,128)(2,1)S(1)} collective-permute-done((bf16[64,1536]{1,0:T(8,128)(2,1)S(1)}, bf16[64,1536]{1,0:T(8,128)(2,1)S(1)}, u32[]{:S(2)}, u32[]{:S(2)}) %collective-permute-start.20) | collective-permute-done | bytes 196640 | tf_op jit(solution)/shard_map/ppermute | solution.py:601
  111.4 9.1 %collective-permute-start.24 = (bf16[64,1536]{1,0:T(8,128)(2,1)S(1)}, bf16[64,1536]{1,0:T(8,128)(2,1)S(1)}, u32[]{:S(2)}, u32[]{:S(2)}) collective-permute-start(bf16[64,1536]{1,0:T(8,128)(2,1)S(1)} %add_shares.9.refs_10_.refs_6_), channel_id=1, source_target_pairs={{0,8},{4,12},{8,0},{12,4},{1,9},{5,13},{9,1},{13,5},{2,10},{6,14},... | collective-permute-start | bytes 589832 | tf_op jit(solution)/shard_map/ppermute | solution.py:601
  123.2 6.1 %collective-permute-done.24.refs_8_ = bf16[64,1536]{1,0:T(8,128)(2,1)S(1)} collective-permute-done((bf16[64,1536]{1,0:T(8,128)(2,1)S(1)}, bf16[64,1536]{1,0:T(8,128)(2,1)S(1)}, u32[]{:S(2)}, u32[]{:S(2)}) %collective-permute-start.24) | collective-permute-done | bytes 196640 | tf_op jit(solution)/shard_map/ppermute | solution.py:601
  169.7 12.0 %collective-permute-done.36.refs_7_ = bf16[64,1536]{1,0:T(8,128)(2,1)S(1)} collective-permute-done((bf16[64,1536]{1,0:T(8,128)(2,1)S(1)}, bf16[64,1536]{1,0:T(8,128)(2,1)S(1)}, u32[]{:S(2)}, u32[]{:S(2)}) %collective-permute-start.36) | collective-permute-done | bytes 196640 | tf_op jit(solution)/shard_map/ppermute | solution.py:601
  186.3 6.2 %mlp_back_1.1 = (bf16[256,1024]{1,0:T(8,128)(2,1)}, bf16[256,1024]{1,0:T(8,128)(2,1)}, bf16[64,1536]{1,0:T(8,128)(2,1)S(1)}, bf16[64,1536]{1,0:T(8,128)(2,1)S(1)...) custom-call(bf16[1536,1024]{1,0:T(8,128)(2,1)S(1)} %get-tuple-element.228.refs_0_, ...), custom_call_target="tpu_custom_call" | custom-call | flops 8000000000 | tf_op jit(solution)/shard_map/mlp_back_1/pallas_call | solution.py:146
  195.4 7.5 %collective-permute-done.43.refs_1_ = bf16[64,1536]{1,0:T(8,128)(2,1)S(1)} collective-permute-done((bf16[64,1536]{1,0:T(8,128)(2,1)S(1)}, bf16[64,1536]{1,0:T(8,128)(2,1)S(1)}, u32[]{:S(2)}, u32[]{:S(2)}) %collective-permute-start.43) | collective-permute-done | bytes 196640 | tf_op jit(solution)/shard_map/ppermute | solution.py:601
  225.8 7.8 %collective-permute-done.50.refs_14_ = bf16[64,1536]{1,0:T(8,128)(2,1)S(1)} collective-permute-done((bf16[64,1536]{1,0:T(8,128)(2,1)S(1)}, bf16[64,1536]{1,0:T(8,128)(2,1)S(1)}, u32[]{:S(2)}, u32[]{:S(2)}) %collective-permute-start.50) | collective-permute-done | bytes 196640 | tf_op jit(solution)/shard_map/ppermute | solution.py:601
  233.6 7.3 %attention_back_1.1 = (bf16[256,1536]{1,0:T(8,128)(2,1)}, f32[1,1536]{1,0:T(1,128)}, bf16[256,384]{1,0:T(8,128)(2,1)}, f32[256,384]{1,0:T(8,128)}, bf16[256,384]...) custom-call(bf16[384,1536]{1,0:T(8,128)(2,1)S(1)} %get-tuple-element.255.refs_0_, ...), custom_call_target="tpu_custom_call" | custom-call | flops 8999999488 | tf_op jit(solution)/shard_map/attention_back_1/pallas_call | solution.py:146
  249.1 6.5 %grad_mlp_1.1.refs_10_ = bf16[4,384,1536]{2,1,0:T(8,128)(2,1)} custom-call(bf16[256,1536]{1,0:T(8,128)(2,1)} %get-tuple-element.253.refs_0_, bf16[256,1536]{1,0:T(8,128)(2,1)S(1)} %collective-permute-done.47.refs_5_.refs_1_, bf16[256,1024]{1,0:T(8,128)(2,1)} %get-tuple-element.272.refs_2_, bf16[256,1024]{1,0:T(8,128)(2,1)S(1)} %collective-permute-done.48.refs_6_.refs_3_, ...), custom_call_target="tpu_custom_call" | custom-call | flops 8000000000 | tf_op jit(solution)/shard_map/grad_mlp_1/pallas_call | solution.py:146
  260.5 8.3 %collective-permute-start.61 = (bf16[64,1536]{1,0:T(8,128)(2,1)S(1)}, bf16[64,1536]{1,0:T(8,128)(2,1)S(1)}, u32[]{:S(2)}, u32[]{:S(2)}) collective-permute-start(bf16[64,1536]{1,0:T(8,128)(2,1)S(1)} %get-tuple-element.287), channel_id=1, source_target_pairs={{0,8},{4,12},{8,0},{12,4},{1,9},{5,13},{9,1},{13,5},{2,10},{6,14},... | collective-permute-start | bytes 589832 | tf_op jit(solution)/shard_map/ppermute | solution.py:601
  268.8 14.1 %collective-permute-done.61.refs_2_ = bf16[64,1536]{1,0:T(8,128)(2,1)S(1)} collective-permute-done((bf16[64,1536]{1,0:T(8,128)(2,1)S(1)}, bf16[64,1536]{1,0:T(8,128)(2,1)S(1)}, u32[]{:S(2)}, u32[]{:S(2)}) %collective-permute-start.61) | collective-permute-done | bytes 196640 | tf_op jit(solution)/shard_map/ppermute | solution.py:601
  298.4 10.4 %collective-permute-done.64.refs_10_ = bf16[64,1536]{1,0:T(8,128)(2,1)S(1)} collective-permute-done((bf16[64,1536]{1,0:T(8,128)(2,1)S(1)}, bf16[64,1536]{1,0:T(8,128)(2,1)S(1)}, u32[]{:S(2)}, u32[]{:S(2)}) %collective-permute-start.64) | collective-permute-done | bytes 196640 | tf_op jit(solution)/shard_map/ppermute | solution.py:601
  308.9 7.4 %mlp_back_0.1 = (bf16[256,1024]{1,0:T(8,128)(2,1)}, bf16[256,1024]{1,0:T(8,128)(2,1)}, bf16[64,1536]{1,0:T(8,128)(2,1)S(1)}, bf16[64,1536]{1,0:T(8,128)(2,1)S(1)...) custom-call(bf16[1536,1024]{1,0:T(8,128)(2,1)S(1)} %get-tuple-elemen, ...), custom_call_target="tpu_custom_call" | custom-call | flops 8000000000 | tf_op jit(solution)/shard_map/mlp_back_0/pallas_call | solution.py:146
  321.3 6.1 %collective-permute-done.68.refs_1_ = bf16[64,1536]{1,0:T(8,128)(2,1)S(1)} collective-permute-done((bf16[64,1536]{1,0:T(8,128)(2,1)S(1)}, bf16[64,1536]{1,0:T(8,128)(2,1)S(1)}, u32[]{:S(2)}, u32[]{:S(2)}) %collective-permute-start.68) | collective-permute-done | bytes 196640 | tf_op jit(solution)/shard_map/ppermute | solution.py:601
  327.4 6.6 %collective-permute-done.69.refs_2_ = bf16[64,1536]{1,0:T(8,128)(2,1)S(1)} collective-permute-done((bf16[64,1536]{1,0:T(8,128)(2,1)S(1)}, bf16[64,1536]{1,0:T(8,128)(2,1)S(1)}, u32[]{:S(2)}, u32[]{:S(2)}) %collective-permute-start.69) | collective-permute-done | bytes 196640 | tf_op jit(solution)/shard_map/ppermute | solution.py:601
  334.1 6.6 %grad_mlp_0.1.refs_13_ = bf16[4,384,1536]{2,1,0:T(8,128)(2,1)} custom-call(bf16[256,1536]{1,0:T(8,128)(2,1)} %get-tuple-element.217.refs_0_, bf16[256,1536]{1,0:T(8,128)(2,1)S(1)} %collective-permute-done.27.refs_11_.refs_1_, bf16[256,1024]{1,0:T(8,128)(2,1)} %get-tuple-element.299.refs_2_, bf16[256,1024]{1,0:T(8,128)(2,1)S(1)} %collective-permute-done.66.refs_5_.refs_3_, ...), custom_call_target="tpu_custom_call" | custom-call | flops 8000000000 | tf_op jit(solution)/shard_map/grad_mlp_0/pallas_call | solution.py:146
  349.3 11.3 %collective-permute-done.72.refs_14_ = bf16[64,1536]{1,0:T(8,128)(2,1)S(1)} collective-permute-done((bf16[64,1536]{1,0:T(8,128)(2,1)S(1)}, bf16[64,1536]{1,0:T(8,128)(2,1)S(1)}, u32[]{:S(2)}, u32[]{:S(2)}) %collective-permute-start.72) | collective-permute-done | bytes 196640 | tf_op jit(solution)/shard_map/ppermute | solution.py:601
  360.6 7.0 %attention_back_0.1 = (bf16[256,1536]{1,0:T(8,128)(2,1)}, f32[1,1536]{1,0:T(1,128)}, bf16[256,384]{1,0:T(8,128)(2,1)}, f32[256,384]{1,0:T(8,128)}, bf16[256,384]...) custom-call(bf16[384,1536]{1,0:T(8,128)(2,1)S(1)} %get-tuple-element.307.refs_0_, ...), custom_call_target="tpu_custom_call" | custom-call | flops 8999999488 | tf_op jit(solution)/shard_map/attention_back_0/pallas_call | solution.py:146
  378.8 7.9 %collective-permute-done.53.refs_3_ = bf16[64,1536]{1,0:T(8,128)(2,1)S(1)} collective-permute-done((bf16[64,1536]{1,0:T(8,128)(2,1)S(1)}, bf16[64,1536]{1,0:T(8,128)(2,1)S(1)}, u32[]{:S(2)}, u32[]{:S(2)}) %collective-permute-start.53) | collective-permute-done | bytes 196640 | tf_op jit(solution)/shard_map/ppermute | solution.py:601
  419.7 11.3 %collective-permute-done.84.refs_2_ = bf16[64,1536]{1,0:T(8,128)(2,1)S(1)} collective-permute-done((bf16[64,1536]{1,0:T(8,128)(2,1)S(1)}, bf16[64,1536]{1,0:T(8,128)(2,1)S(1)}, u32[]{:S(2)}, u32[]{:S(2)}) %collective-permute-start.84) | collective-permute-done | bytes 196640 | tf_op jit(solution)/shard_map/ppermute | solution.py:601
  437.3 10.3 %collective-permute-done.82.refs_3_ = bf16[384,576]{1,0:T(8,128)(2,1)S(1)} collective-permute-done((bf16[384,576]{1,0:T(8,128)(2,1)}, bf16[384,576]{1,0:T(8,128)(2,1)S(1)}, u32[]{:S(2)}, u32[]{:S(2)}) %collective-permute-start.82) | collective-permute-done | bytes 442400 | tf_op jit(solution)/shard_map/ppermute | solution.py:822
  (353 shorter events, 267.5 us)
Async XLA Ops:
  7.2 388.9 %reduce-scatter.12.cloned.1.call-start = ((), (), s32[]{:S(2)}) async-start(), calls=%async_computation.4 | async-start | bytes 2457600
  42.7 19.3 %collective-permute-start.9 = (bf16[1,1536,1024]{2,1,0:T(8,128)(2,1)S(1)}, bf16[1,1536,1024]{2,1,0:T(8,128)(2,1)S(1)}, u32[]{:S(2)}, u32[]{:S(2)}) collective-permute-start(bf16[1,1536,1024]{2,1,0:T(8,128)(2,1)S(1)} %copy-done.18), channel_id=1, source_target_pairs={{0,16},{16,0},{1,17},{17,1},{2,18},{18,2},{3,19},{19,3},{4,20},{20... | collective-permute-start | bytes 9437192 | tf_op jit(solution)/shard_map/ppermute | solution.py:33
  65.7 21.8 %collective-permute-start.18 = (bf16[256,1536]{1,0:T(8,128)(2,1)S(1)}, bf16[256,1536]{1,0:T(8,128)(2,1)S(1)}, u32[]{:S(2)}, u32[]{:S(2)}) collective-permute-start(bf16[256,1536]{1,0:T(8,128)(2,1)S(1)} %copy-done.42), channel_id=1, source_target_pairs={{0,16},{16,0},{1,17},{17,1},{2,18},{18,2},{3,19},{19,3},{4,20},{20... | collective-permute-start | bytes 2359304 | tf_op jit(solution)/shard_map/ppermute | solution.py:33
  91.4 37.9 %collective-permute-start.27 = (bf16[256,1536]{1,0:T(8,128)(2,1)}, bf16[256,1536]{1,0:T(8,128)(2,1)S(1)}, u32[]{:S(2)}, u32[]{:S(2)}) collective-permute-start(bf16[256,1536]{1,0:T(8,128)(2,1)} %get-tuple-element.217.refs_0_), channel_id=1, source_target_pairs={{0,16},{16,0},{1,17},{17,1},{2,18},{18,2},{3,19},{19,3},{4,20},{20... | collective-permute-start | bytes 2359304 | tf_op jit(solution)/shard_map/ppermute | solution.py:33
  95.9 24.6 %collective-permute-start.26 = (bf16[256,512]{1,0:T(8,128)(2,1)}, bf16[256,512]{1,0:T(8,128)(2,1)S(1)}, u32[]{:S(2)}, u32[]{:S(2)}) collective-permute-start(bf16[256,512]{1,0:T(8,128)(2,1)} %get-tuple-element.216), channel_id=1, source_target_pairs={{0,16},{16,0},{1,17},{17,1},{2,18},{18,2},{3,19},{19,3},{4,20},{20... | collective-permute-start | bytes 786440 | tf_op jit(solution)/shard_map/ppermute | solution.py:33
  102.7 39.8 %collective-permute-start.31 = (bf16[256,1536]{1,0:T(8,128)(2,1)S(1)}, bf16[256,1536]{1,0:T(8,128)(2,1)S(1)}, u32[]{:S(2)}, u32[]{:S(2)}) collective-permute-start(bf16[256,1536]{1,0:T(8,128)(2,1)S(1)} %select_bitcast_fusion.4.refs_5_.refs_2_.refs_4_), channel_id=1, source_target_pairs={{0,16},{16,0},{1,17},{17,1},{2,18},{18,2},{3,19},{19,3},{4,20},{20... | collective-permute-start | bytes 2359304 | tf_op jit(solution)/shard_map/ppermute | solution.py:33
  159.9 21.8 %collective-permute-start.38 = (bf16[256,1536]{1,0:T(8,128)(2,1)S(1)}, bf16[256,1536]{1,0:T(8,128)(2,1)S(1)}, u32[]{:S(2)}, u32[]{:S(2)}) collective-permute-start(bf16[256,1536]{1,0:T(8,128)(2,1)S(1)} %copy-done.43), channel_id=1, source_target_pairs={{0,16},{16,0},{1,17},{17,1},{2,18},{18,2},{3,19},{19,3},{4,20},{20... | collective-permute-start | bytes 2359304 | tf_op jit(solution)/shard_map/ppermute | solution.py:33
  161.8 19.9 %collective-permute-start.36 = (bf16[64,1536]{1,0:T(8,128)(2,1)S(1)}, bf16[64,1536]{1,0:T(8,128)(2,1)S(1)}, u32[]{:S(2)}, u32[]{:S(2)}) collective-permute-start(bf16[64,1536]{1,0:T(8,128)(2,1)S(1)} %add_shares.10.refs_8_.refs_5_), channel_id=1, source_target_pairs={{0,8},{4,12},{8,0},{12,4},{1,9},{5,13},{9,1},{13,5},{2,10},{6,14},... | collective-permute-start | bytes 589832 | tf_op jit(solution)/shard_map/ppermute | solution.py:601
  186.1 24.7 %collective-permute-start.47 = (bf16[256,1536]{1,0:T(8,128)(2,1)}, bf16[256,1536]{1,0:T(8,128)(2,1)S(1)}, u32[]{:S(2)}, u32[]{:S(2)}) collective-permute-start(bf16[256,1536]{1,0:T(8,128)(2,1)} %get-tuple-element.253.refs_0_), channel_id=1, source_target_pairs={{0,16},{16,0},{1,17},{17,1},{2,18},{18,2},{3,19},{19,3},{4,20},{20... | collective-permute-start | bytes 2359304 | tf_op jit(solution)/shard_map/ppermute | solution.py:33
  213.1 20.5 %collective-permute-start.50 = (bf16[64,1536]{1,0:T(8,128)(2,1)S(1)}, bf16[64,1536]{1,0:T(8,128)(2,1)S(1)}, u32[]{:S(2)}, u32[]{:S(2)}) collective-permute-start(bf16[64,1536]{1,0:T(8,128)(2,1)S(1)} %add_shares.11.refs_13_.refs_12_), channel_id=1, source_target_pairs={{0,8},{4,12},{8,0},{12,4},{1,9},{5,13},{9,1},{13,5},{2,10},{6,14},... | collective-permute-start | bytes 589832 | tf_op jit(solution)/shard_map/ppermute | solution.py:601
  218.3 25.2 %collective-permute-start.40 = (bf16[64,1536]{1,0:T(8,128)(2,1)S(1)}, bf16[64,1536]{1,0:T(8,128)(2,1)S(1)}, u32[]{:S(2)}, u32[]{:S(2)}) collective-permute-start(bf16[64,1536]{1,0:T(8,128)(2,1)S(1)} %copy-done.47), channel_id=1, source_target_pairs={{0,4},{4,0},{8,12},{12,8},{1,5},{5,1},{9,13},{13,9},{2,6},{6,2},{1... | collective-permute-start | bytes 589832 | tf_op jit(solution)/shard_map/ppermute | solution.py:601
  220.3 24.5 %collective-permute-start.41 = (bf16[64,1536]{1,0:T(8,128)(2,1)S(1)}, bf16[64,1536]{1,0:T(8,128)(2,1)S(1)}, u32[]{:S(2)}, u32[]{:S(2)}) collective-permute-start(bf16[64,1536]{1,0:T(8,128)(2,1)S(1)} %copy-done.46), channel_id=1, source_target_pairs={{0,8},{4,12},{8,0},{12,4},{1,9},{5,13},{9,1},{13,5},{2,10},{6,14},... | collective-permute-start | bytes 589832 | tf_op jit(solution)/shard_map/ppermute | solution.py:601
  223.3 21.6 %collective-permute-start.42 = (bf16[64,1536]{1,0:T(8,128)(2,1)S(1)}, bf16[64,1536]{1,0:T(8,128)(2,1)S(1)}, u32[]{:S(2)}, u32[]{:S(2)}) collective-permute-start(bf16[64,1536]{1,0:T(8,128)(2,1)S(1)} %copy-done.45), channel_id=1, source_target_pairs={{0,12},{4,8},{8,4},{12,0},{1,13},{5,9},{9,5},{13,1},{2,14},{6,10},... | collective-permute-start | bytes 589832 | tf_op jit(solution)/shard_map/ppermute | solution.py:601
  260.5 22.4 %collective-permute-start.61 = (bf16[64,1536]{1,0:T(8,128)(2,1)S(1)}, bf16[64,1536]{1,0:T(8,128)(2,1)S(1)}, u32[]{:S(2)}, u32[]{:S(2)}) collective-permute-start(bf16[64,1536]{1,0:T(8,128)(2,1)S(1)} %get-tuple-element.287), channel_id=1, source_target_pairs={{0,8},{4,12},{8,0},{12,4},{1,9},{5,13},{9,1},{13,5},{2,10},{6,14},... | collective-permute-start | bytes 589832 | tf_op jit(solution)/shard_map/ppermute | solution.py:601
  287.4 108.7 %reduce-scatter.10.cloned.1.call-start = ((), (), s32[]{:S(2)}) async-start(), calls=%async_computation.3 | async-start | bytes 5898240
  288.2 179.5 %reduce-scatter.14.cloned.1.call-start = ((), (), s32[]{:S(2)}) async-start(), calls=%async_computation.5 | async-start | bytes 5898240
  367.7 28.4 %collective-permute-start.75 = (bf16[256,1536]{1,0:T(8,128)(2,1)}, bf16[256,1536]{1,0:T(8,128)(2,1)S(1)}, u32[]{:S(2)}, u32[]{:S(2)}) collective-permute-start(bf16[256,1536]{1,0:T(8,128)(2,1)} %get-tuple-element.320.refs_0_), channel_id=1, source_target_pairs={{0,16},{16,0},{1,17},{17,1},{2,18},{18,2},{3,19},{19,3},{4,20},{20... | collective-permute-start | bytes 2359304 | tf_op jit(solution)/shard_map/ppermute | solution.py:33
  372.2 23.9 %collective-permute-start.76 = (bf16[256,384]{1,0:T(8,128)(2,1)}, bf16[256,384]{1,0:T(8,128)(2,1)S(1)}, u32[]{:S(2)}, u32[]{:S(2)}) collective-permute-start(bf16[256,384]{1,0:T(8,128)(2,1)} %get-tuple-element.330), channel_id=1, source_target_pairs={{1,0},{3,2},{5,4},{7,6},{9,8},{11,10},{13,12},{15,14},{17,16},{19,... | collective-permute-start | bytes 589832 | tf_op jit(solution)/shard_map/ppermute | solution.py:929
  409.7 27.6 %collective-permute-start.80 = (bf16[384,576]{1,0:T(8,128)(2,1)}, bf16[384,576]{1,0:T(8,128)(2,1)S(1)}, u32[]{:S(2)}, u32[]{:S(2)}) collective-permute-start(bf16[384,576]{1,0:T(8,128)(2,1)} %get-tuple-element.336), channel_id=1, source_target_pairs={{0,1},{1,0},{2,3},{3,2},{4,5},{5,4},{6,7},{7,6},{8,9},{9,8},{10,11... | collective-permute-start | bytes 1327112 | tf_op jit(solution)/shard_map/ppermute | solution.py:822
  409.8 27.5 %collective-permute-start.81 = (bf16[384,576]{1,0:T(8,128)(2,1)}, bf16[384,576]{1,0:T(8,128)(2,1)S(1)}, u32[]{:S(2)}, u32[]{:S(2)}) collective-permute-start(bf16[384,576]{1,0:T(8,128)(2,1)} %get-tuple-element.337), channel_id=1, source_target_pairs={{0,2},{1,3},{2,0},{3,1},{4,6},{5,7},{6,4},{7,5},{8,10},{9,11},{10,... | collective-permute-start | bytes 1327112 | tf_op jit(solution)/shard_map/ppermute | solution.py:822
  413.6 33.9 %collective-permute-start.82 = (bf16[384,576]{1,0:T(8,128)(2,1)}, bf16[384,576]{1,0:T(8,128)(2,1)S(1)}, u32[]{:S(2)}, u32[]{:S(2)}) collective-permute-start(bf16[384,576]{1,0:T(8,128)(2,1)} %get-tuple-element.338), channel_id=1, source_target_pairs={{0,3},{1,2},{2,1},{3,0},{4,7},{5,6},{6,5},{7,4},{8,11},{9,10},{10,... | collective-permute-start | bytes 1327112 | tf_op jit(solution)/shard_map/ppermute | solution.py:822
  431.1 20.7 %collective-permute-start.88 = (bf16[64,1536]{1,0:T(8,128)(2,1)S(1)}, bf16[64,1536]{1,0:T(8,128)(2,1)S(1)}, u32[]{:S(2)}, u32[]{:S(2)}) collective-permute-start(bf16[64,1536]{1,0:T(8,128)(2,1)S(1)} %add_shares.15.refs_4_.refs_3_), channel_id=1, source_target_pairs={{0,12},{4,8},{8,4},{12,0},{1,13},{5,9},{9,5},{13,1},{2,14},{6,10},... | collective-permute-start | bytes 589832 | tf_op jit(solution)/shard_map/ppermute | solution.py:601
  432.6 19.7 %collective-permute-start.87 = (bf16[64,1536]{1,0:T(8,128)(2,1)S(1)}, bf16[64,1536]{1,0:T(8,128)(2,1)S(1)}, u32[]{:S(2)}, u32[]{:S(2)}) collective-permute-start(bf16[64,1536]{1,0:T(8,128)(2,1)S(1)} %add_shares.15.refs_4_.refs_3_), channel_id=1, source_target_pairs={{0,8},{4,12},{8,0},{12,4},{1,9},{5,13},{9,1},{13,5},{2,10},{6,14},... | collective-permute-start | bytes 589832 | tf_op jit(solution)/shard_map/ppermute | solution.py:601
  455.9 20.0 %collective-permute-start.93 = (bf16[384,576]{1,0:T(8,128)(2,1)}, bf16[384,576]{1,0:T(8,128)(2,1)S(1)}, u32[]{:S(2)}, u32[]{:S(2)}) collective-permute-start(bf16[384,576]{1,0:T(8,128)(2,1)} %get-tuple-element.361), channel_id=1, source_target_pairs={{0,16},{16,0},{1,17},{17,1},{2,18},{18,2},{3,19},{19,3},{4,20},{20... | collective-permute-start | bytes 1327112 | tf_op jit(solution)/shard_map/ppermute | solution.py:33
  (124 other events, 1189.3 us)
Sparse Core Ops, SparseCore 0:
  287.5 37.0 reduce-scatter.11
  327.6 61.1 reduce-scatter.9
  391.8 75.8 reduce-scatter.13

commit v4 on v3

--- a/solution.py
+++ b/solution.py
@@ -858,7 +858,7 @@
             blocks.append(lax.ppermute(kv, "dp", peer_pairs(peers, step, False)))
         early = collect()
         if layer == 0:
-            early += raw([wg[1]])
+            early += [(wg[1], LOOSE_RAW)]
         else:
             grad_other = soon(grad)
             early += collect()
@@ -867,7 +867,7 @@
         received = spread(outs[-shares:])
         if layer == 0:
             wu, wd = follow(own[5:], results[1])
-            total = add_rows(received, raw([wu[1], wd[1]]))
+            total = add_rows(received, [(wu[1], LOOSE_RAW), (wd[1], LOOSE_RAW)])
         else:
             total = add_rows(received)
         swapped, theirs, _ = lax.optimization_barrier((normed_one, results[1], total))

time: 489 us -> 485 us (level)
    unnamed x100 -> x92, local copies, waits for them, and re-layouts: 16.2 us -> 11.5 us
  transfers between devices with their start and end apart: 98 -> 98, of which waited for: 31 -> 32; matrix products, arithmetic and copies ran while one was open for 4% -> 4% of each run, Pallas kernels for 18% -> 19%
where the time goes in v4:
time: 485 us; the launch traced here: 481 us
  waiting for transfers between devices  183 us (38%)
  starting transfers between devices  131 us (27%)
  Pallas kernels  121 us (25%)
  other arithmetic  17.4 us (4%)
  between operations  15.5 us (3%)
  local copies, waits for them, and re-layouts  13.4 us (3%)
    ppermute x48, waiting for transfers between devices, spread(): lax.ppermute(values[step], 'tensor', [(peer, peer ^ step) for peer in ran...  159 us
    pallas_call x40, Pallas kernels, kernel_call(): results = call(*[fixed(value, where) for value, where in [*ins, *after]])  121 us
    ppermute x48, starting transfers between devices, spread(): lax.ppermute(values[step], 'tensor', [(peer, peer ^ step) for peer in ran...  91.5 us
    ppermute x6, starting transfers between devices, per_device(): blocks.append(lax.ppermute(kv, 'dp', peer_pairs(peers, step, False)))  19.2 us
    unnamed x92, local copies, waits for them, and re-layouts  11.5 us
  transfers between devices with their start and end apart: 98, of which 32 were waited for; matrix products, arithmetic and copies ran while one was open for 4% of the time, Pallas kernels for 19%

profile of v4, /device:TPU:0, one launch (start us, length us, event | category | flops | bytes accessed | tf_op | source)
XLA Modules:
  0.0 481.4 jit_solution(14112374253827436768)
XLA Ops:
  52.1 8.2 %collective-permute-done.13.refs_2_ = bf16[64,1536]{1,0:T(8,128)(2,1)S(1)} collective-permute-done((bf16[64,1536]{1,0:T(8,128)(2,1)S(1)}, bf16[64,1536]{1,0:T(8,128)(2,1)S(1)}, u32[]{:S(2)}, u32[]{:S(2)}) %collective-permute-start.13) | collective-permute-done | bytes 196640 | tf_op jit(solution)/shard_map/ppermute | solution.py:601
  73.3 11.5 %collective-permute-done.16.refs_7_ = bf16[64,1536]{1,0:T(8,128)(2,1)S(1)} collective-permute-done((bf16[64,1536]{1,0:T(8,128)(2,1)S(1)}, bf16[64,1536]{1,0:T(8,128)(2,1)S(1)}, u32[]{:S(2)}, u32[]{:S(2)}) %collective-permute-start.16) | collective-permute-done | bytes 196640 | tf_op jit(solution)/shard_map/ppermute | solution.py:601
  93.4 6.6 %collective-permute-done.20.refs_1_ = bf16[64,1536]{1,0:T(8,128)(2,1)S(1)} collective-permute-done((bf16[64,1536]{1,0:T(8,128)(2,1)S(1)}, bf16[64,1536]{1,0:T(8,128)(2,1)S(1)}, u32[]{:S(2)}, u32[]{:S(2)}) %collective-permute-start.20) | collective-permute-done | bytes 196640 | tf_op jit(solution)/shard_map/ppermute | solution.py:601
  108.7 9.1 %collective-permute-start.24 = (bf16[64,1536]{1,0:T(8,128)(2,1)S(1)}, bf16[64,1536]{1,0:T(8,128)(2,1)S(1)}, u32[]{:S(2)}, u32[]{:S(2)}) collective-permute-start(bf16[64,1536]{1,0:T(8,128)(2,1)S(1)} %add_shares.9.refs_10_.refs_6_), channel_id=1, source_target_pairs={{0,8},{4,12},{8,0},{12,4},{1,9},{5,13},{9,1},{13,5},{2,10},{6,14},... | collective-permute-start | bytes 589832 | tf_op jit(solution)/shard_map/ppermute | solution.py:601
  120.5 6.2 %collective-permute-done.24.refs_8_ = bf16[64,1536]{1,0:T(8,128)(2,1)S(1)} collective-permute-done((bf16[64,1536]{1,0:T(8,128)(2,1)S(1)}, bf16[64,1536]{1,0:T(8,128)(2,1)S(1)}, u32[]{:S(2)}, u32[]{:S(2)}) %collective-permute-start.24) | collective-permute-done | bytes 196640 | tf_op jit(solution)/shard_map/ppermute | solution.py:601
  167.1 12.0 %collective-permute-done.36.refs_7_ = bf16[64,1536]{1,0:T(8,128)(2,1)S(1)} collective-permute-done((bf16[64,1536]{1,0:T(8,128)(2,1)S(1)}, bf16[64,1536]{1,0:T(8,128)(2,1)S(1)}, u32[]{:S(2)}, u32[]{:S(2)}) %collective-permute-start.36) | collective-permute-done | bytes 196640 | tf_op jit(solution)/shard_map/ppermute | solution.py:601
  183.7 6.3 %mlp_back_1.1 = (bf16[256,1024]{1,0:T(8,128)(2,1)}, bf16[256,1024]{1,0:T(8,128)(2,1)}, bf16[64,1536]{1,0:T(8,128)(2,1)S(1)}, bf16[64,1536]{1,0:T(8,128)(2,1)S(1)...) custom-call(bf16[1536,1024]{1,0:T(8,128)(2,1)S(1)} %get-tuple-element.228.refs_0_, ...), custom_call_target="tpu_custom_call" | custom-call | flops 8000000000 | tf_op jit(solution)/shard_map/mlp_back_1/pallas_call | solution.py:146
  192.8 7.5 %collective-permute-done.43.refs_1_ = bf16[64,1536]{1,0:T(8,128)(2,1)S(1)} collective-permute-done((bf16[64,1536]{1,0:T(8,128)(2,1)S(1)}, bf16[64,1536]{1,0:T(8,128)(2,1)S(1)}, u32[]{:S(2)}, u32[]{:S(2)}) %collective-permute-start.43) | collective-permute-done | bytes 196640 | tf_op jit(solution)/shard_map/ppermute | solution.py:601
  223.2 7.8 %collective-permute-done.50.refs_14_ = bf16[64,1536]{1,0:T(8,128)(2,1)S(1)} collective-permute-done((bf16[64,1536]{1,0:T(8,128)(2,1)S(1)}, bf16[64,1536]{1,0:T(8,128)(2,1)S(1)}, u32[]{:S(2)}, u32[]{:S(2)}) %collective-permute-start.50) | collective-permute-done | bytes 196640 | tf_op jit(solution)/shard_map/ppermute | solution.py:601
  231.0 7.6 %attention_back_1.1 = (bf16[256,1536]{1,0:T(8,128)(2,1)}, f32[1,1536]{1,0:T(1,128)}, bf16[256,384]{1,0:T(8,128)(2,1)}, f32[256,384]{1,0:T(8,128)}, bf16[256,384]...) custom-call(bf16[384,1536]{1,0:T(8,128)(2,1)S(1)} %get-tuple-element.255.refs_0_, ...), custom_call_target="tpu_custom_call" | custom-call | flops 8999999488 | tf_op jit(solution)/shard_map/attention_back_1/pallas_call | solution.py:146
  246.8 6.5 %grad_mlp_1.1.refs_10_ = bf16[4,384,1536]{2,1,0:T(8,128)(2,1)} custom-call(bf16[256,1536]{1,0:T(8,128)(2,1)} %get-tuple-element.253.refs_0_, bf16[256,1536]{1,0:T(8,128)(2,1)S(1)} %collective-permute-done.47.refs_5_.refs_1_, bf16[256,1024]{1,0:T(8,128)(2,1)} %get-tuple-element.272.refs_2_, bf16[256,1024]{1,0:T(8,128)(2,1)S(1)} %collective-permute-done.48.refs_6_.refs_3_, ...), custom_call_target="tpu_custom_call" | custom-call | flops 8000000000 | tf_op jit(solution)/shard_map/grad_mlp_1/pallas_call | solution.py:146
  257.8 8.4 %collective-permute-start.61 = (bf16[64,1536]{1,0:T(8,128)(2,1)S(1)}, bf16[64,1536]{1,0:T(8,128)(2,1)S(1)}, u32[]{:S(2)}, u32[]{:S(2)}) collective-permute-start(bf16[64,1536]{1,0:T(8,128)(2,1)S(1)} %get-tuple-element.287), channel_id=1, source_target_pairs={{0,8},{4,12},{8,0},{12,4},{1,9},{5,13},{9,1},{13,5},{2,10},{6,14},... | collective-permute-start | bytes 589832 | tf_op jit(solution)/shard_map/ppermute | solution.py:601
  266.2 14.1 %collective-permute-done.61.refs_2_ = bf16[64,1536]{1,0:T(8,128)(2,1)S(1)} collective-permute-done((bf16[64,1536]{1,0:T(8,128)(2,1)S(1)}, bf16[64,1536]{1,0:T(8,128)(2,1)S(1)}, u32[]{:S(2)}, u32[]{:S(2)}) %collective-permute-start.61) | collective-permute-done | bytes 196640 | tf_op jit(solution)/shard_map/ppermute | solution.py:601
  295.8 10.4 %collective-permute-done.64.refs_10_ = bf16[64,1536]{1,0:T(8,128)(2,1)S(1)} collective-permute-done((bf16[64,1536]{1,0:T(8,128)(2,1)S(1)}, bf16[64,1536]{1,0:T(8,128)(2,1)S(1)}, u32[]{:S(2)}, u32[]{:S(2)}) %collective-permute-start.64) | collective-permute-done | bytes 196640 | tf_op jit(solution)/shard_map/ppermute | solution.py:601
  306.2 7.4 %mlp_back_0.1 = (bf16[256,1024]{1,0:T(8,128)(2,1)}, bf16[256,1024]{1,0:T(8,128)(2,1)}, bf16[64,1536]{1,0:T(8,128)(2,1)S(1)}, bf16[64,1536]{1,0:T(8,128)(2,1)S(1)...) custom-call(bf16[1536,1024]{1,0:T(8,128)(2,1)S(1)} %get-tuple-elemen, ...), custom_call_target="tpu_custom_call" | custom-call | flops 8000000000 | tf_op jit(solution)/shard_map/mlp_back_0/pallas_call | solution.py:146
  318.6 6.1 %collective-permute-done.68.refs_1_ = bf16[64,1536]{1,0:T(8,128)(2,1)S(1)} collective-permute-done((bf16[64,1536]{1,0:T(8,128)(2,1)S(1)}, bf16[64,1536]{1,0:T(8,128)(2,1)S(1)}, u32[]{:S(2)}, u32[]{:S(2)}) %collective-permute-start.68) | collective-permute-done | bytes 196640 | tf_op jit(solution)/shard_map/ppermute | solution.py:601
  324.7 6.6 %collective-permute-done.69.refs_2_ = bf16[64,1536]{1,0:T(8,128)(2,1)S(1)} collective-permute-done((bf16[64,1536]{1,0:T(8,128)(2,1)S(1)}, bf16[64,1536]{1,0:T(8,128)(2,1)S(1)}, u32[]{:S(2)}, u32[]{:S(2)}) %collective-permute-start.69) | collective-permute-done | bytes 196640 | tf_op jit(solution)/shard_map/ppermute | solution.py:601
  331.4 6.5 %grad_mlp_0.1.refs_13_ = bf16[4,384,1536]{2,1,0:T(8,128)(2,1)} custom-call(bf16[256,1536]{1,0:T(8,128)(2,1)} %get-tuple-element.217.refs_0_, bf16[256,1536]{1,0:T(8,128)(2,1)S(1)} %collective-permute-done.27.refs_11_.refs_1_, bf16[256,1024]{1,0:T(8,128)(2,1)} %get-tuple-element.299.refs_2_, bf16[256,1024]{1,0:T(8,128)(2,1)S(1)} %collective-permute-done.66.refs_5_.refs_3_, ...), custom_call_target="tpu_custom_call" | custom-call | flops 8000000000 | tf_op jit(solution)/shard_map/grad_mlp_0/pallas_call | solution.py:146
  346.4 11.7 %collective-permute-done.72.refs_14_ = bf16[64,1536]{1,0:T(8,128)(2,1)S(1)} collective-permute-done((bf16[64,1536]{1,0:T(8,128)(2,1)S(1)}, bf16[64,1536]{1,0:T(8,128)(2,1)S(1)}, u32[]{:S(2)}, u32[]{:S(2)}) %collective-permute-start.72) | collective-permute-done | bytes 196640 | tf_op jit(solution)/shard_map/ppermute | solution.py:601
  358.1 7.3 %attention_back_0.1 = (bf16[256,1536]{1,0:T(8,128)(2,1)}, f32[1,1536]{1,0:T(1,128)}, bf16[256,384]{1,0:T(8,128)(2,1)}, f32[256,384]{1,0:T(8,128)}, bf16[256,384]...) custom-call(bf16[384,1536]{1,0:T(8,128)(2,1)S(1)} %get-tuple-element.307.refs_0_, ...), custom_call_target="tpu_custom_call" | custom-call | flops 8999999488 | tf_op jit(solution)/shard_map/attention_back_0/pallas_call | solution.py:146
  376.5 7.9 %collective-permute-done.53.refs_3_ = bf16[64,1536]{1,0:T(8,128)(2,1)S(1)} collective-permute-done((bf16[64,1536]{1,0:T(8,128)(2,1)S(1)}, bf16[64,1536]{1,0:T(8,128)(2,1)S(1)}, u32[]{:S(2)}, u32[]{:S(2)}) %collective-permute-start.53) | collective-permute-done | bytes 196640 | tf_op jit(solution)/shard_map/ppermute | solution.py:601
  416.9 11.1 %collective-permute-done.84.refs_2_ = bf16[64,1536]{1,0:T(8,128)(2,1)S(1)} collective-permute-done((bf16[64,1536]{1,0:T(8,128)(2,1)S(1)}, bf16[64,1536]{1,0:T(8,128)(2,1)S(1)}, u32[]{:S(2)}, u32[]{:S(2)}) %collective-permute-start.84) | collective-permute-done | bytes 196640 | tf_op jit(solution)/shard_map/ppermute | solution.py:601
  429.4 6.2 %collective-permute-start.87 = (bf16[64,1536]{1,0:T(8,128)(2,1)S(1)}, bf16[64,1536]{1,0:T(8,128)(2,1)S(1)}, u32[]{:S(2)}, u32[]{:S(2)}) collective-permute-start(bf16[64,1536]{1,0:T(8,128)(2,1)S(1)} %add_shares.15.refs_4_.refs_3_), channel_id=1, source_target_pairs={{0,8},{4,12},{8,0},{12,4},{1,9},{5,13},{9,1},{13,5},{2,10},{6,14},... | collective-permute-start | bytes 589832 | tf_op jit(solution)/shard_map/ppermute | solution.py:601
  435.6 8.1 %collective-permute-done.82.refs_3_ = bf16[384,576]{1,0:T(8,128)(2,1)S(1)} collective-permute-done((bf16[384,576]{1,0:T(8,128)(2,1)}, bf16[384,576]{1,0:T(8,128)(2,1)S(1)}, u32[]{:S(2)}, u32[]{:S(2)}) %collective-permute-start.82) | collective-permute-done | bytes 442400 | tf_op jit(solution)/shard_map/ppermute | solution.py:822
  (345 shorter events, 264.7 us)
Async XLA Ops:
  7.2 386.7 %reduce-scatter.12.cloned.1.call-start = ((), (), s32[]{:S(2)}) async-start(), calls=%async_computation.4 | async-start | bytes 2457600
  41.1 19.3 %collective-permute-start.9 = (bf16[1,1536,1024]{2,1,0:T(8,128)(2,1)S(1)}, bf16[1,1536,1024]{2,1,0:T(8,128)(2,1)S(1)}, u32[]{:S(2)}, u32[]{:S(2)}) collective-permute-start(bf16[1,1536,1024]{2,1,0:T(8,128)(2,1)S(1)} %copy-done.15), channel_id=1, source_target_pairs={{0,16},{16,0},{1,17},{17,1},{2,18},{18,2},{3,19},{19,3},{4,20},{20... | collective-permute-start | bytes 9437192 | tf_op jit(solution)/shard_map/ppermute | solution.py:33
  41.1 19.2 %collective-permute-start.10 = (bf16[1,1024,1536]{2,1,0:T(8,128)(2,1)S(1)}, bf16[1,1024,1536]{2,1,0:T(8,128)(2,1)S(1)}, u32[]{:S(2)}, u32[]{:S(2)}) collective-permute-start(bf16[1,1024,1536]{2,1,0:T(8,128)(2,1)S(1)} %copy-done.16), channel_id=1, source_target_pairs={{0,16},{16,0},{1,17},{17,1},{2,18},{18,2},{3,19},{19,3},{4,20},{20... | collective-permute-start | bytes 9437192 | tf_op jit(solution)/shard_map/ppermute | solution.py:33
  62.9 21.8 %collective-permute-start.18 = (bf16[256,1536]{1,0:T(8,128)(2,1)S(1)}, bf16[256,1536]{1,0:T(8,128)(2,1)S(1)}, u32[]{:S(2)}, u32[]{:S(2)}) collective-permute-start(bf16[256,1536]{1,0:T(8,128)(2,1)S(1)} %copy-done.38), channel_id=1, source_target_pairs={{0,16},{16,0},{1,17},{17,1},{2,18},{18,2},{3,19},{19,3},{4,20},{20... | collective-permute-start | bytes 2359304 | tf_op jit(solution)/shard_map/ppermute | solution.py:33
  88.7 38.0 %collective-permute-start.27 = (bf16[256,1536]{1,0:T(8,128)(2,1)}, bf16[256,1536]{1,0:T(8,128)(2,1)S(1)}, u32[]{:S(2)}, u32[]{:S(2)}) collective-permute-start(bf16[256,1536]{1,0:T(8,128)(2,1)} %get-tuple-element.217.refs_0_), channel_id=1, source_target_pairs={{0,16},{16,0},{1,17},{17,1},{2,18},{18,2},{3,19},{19,3},{4,20},{20... | collective-permute-start | bytes 2359304 | tf_op jit(solution)/shard_map/ppermute | solution.py:33
  93.3 24.6 %collective-permute-start.26 = (bf16[256,512]{1,0:T(8,128)(2,1)}, bf16[256,512]{1,0:T(8,128)(2,1)S(1)}, u32[]{:S(2)}, u32[]{:S(2)}) collective-permute-start(bf16[256,512]{1,0:T(8,128)(2,1)} %get-tuple-element.216), channel_id=1, source_target_pairs={{0,16},{16,0},{1,17},{17,1},{2,18},{18,2},{3,19},{19,3},{4,20},{20... | collective-permute-start | bytes 786440 | tf_op jit(solution)/shard_map/ppermute | solution.py:33
  100.0 39.8 %collective-permute-start.31 = (bf16[256,1536]{1,0:T(8,128)(2,1)S(1)}, bf16[256,1536]{1,0:T(8,128)(2,1)S(1)}, u32[]{:S(2)}, u32[]{:S(2)}) collective-permute-start(bf16[256,1536]{1,0:T(8,128)(2,1)S(1)} %select_bitcast_fusion.4.refs_5_.refs_2_.refs_4_), channel_id=1, source_target_pairs={{0,16},{16,0},{1,17},{17,1},{2,18},{18,2},{3,19},{19,3},{4,20},{20... | collective-permute-start | bytes 2359304 | tf_op jit(solution)/shard_map/ppermute | solution.py:33
  157.3 21.8 %collective-permute-start.38 = (bf16[256,1536]{1,0:T(8,128)(2,1)S(1)}, bf16[256,1536]{1,0:T(8,128)(2,1)S(1)}, u32[]{:S(2)}, u32[]{:S(2)}) collective-permute-start(bf16[256,1536]{1,0:T(8,128)(2,1)S(1)} %copy-done.39), channel_id=1, source_target_pairs={{0,16},{16,0},{1,17},{17,1},{2,18},{18,2},{3,19},{19,3},{4,20},{20... | collective-permute-start | bytes 2359304 | tf_op jit(solution)/shard_map/ppermute | solution.py:33
  159.2 19.9 %collective-permute-start.36 = (bf16[64,1536]{1,0:T(8,128)(2,1)S(1)}, bf16[64,1536]{1,0:T(8,128)(2,1)S(1)}, u32[]{:S(2)}, u32[]{:S(2)}) collective-permute-start(bf16[64,1536]{1,0:T(8,128)(2,1)S(1)} %add_shares.10.refs_8_.refs_5_), channel_id=1, source_target_pairs={{0,8},{4,12},{8,0},{12,4},{1,9},{5,13},{9,1},{13,5},{2,10},{6,14},... | collective-permute-start | bytes 589832 | tf_op jit(solution)/shard_map/ppermute | solution.py:601
  183.5 24.8 %collective-permute-start.47 = (bf16[256,1536]{1,0:T(8,128)(2,1)}, bf16[256,1536]{1,0:T(8,128)(2,1)S(1)}, u32[]{:S(2)}, u32[]{:S(2)}) collective-permute-start(bf16[256,1536]{1,0:T(8,128)(2,1)} %get-tuple-element.253.refs_0_), channel_id=1, source_target_pairs={{0,16},{16,0},{1,17},{17,1},{2,18},{18,2},{3,19},{19,3},{4,20},{20... | collective-permute-start | bytes 2359304 | tf_op jit(solution)/shard_map/ppermute | solution.py:33
  210.5 20.5 %collective-permute-start.50 = (bf16[64,1536]{1,0:T(8,128)(2,1)S(1)}, bf16[64,1536]{1,0:T(8,128)(2,1)S(1)}, u32[]{:S(2)}, u32[]{:S(2)}) collective-permute-start(bf16[64,1536]{1,0:T(8,128)(2,1)S(1)} %add_shares.11.refs_13_.refs_12_), channel_id=1, source_target_pairs={{0,8},{4,12},{8,0},{12,4},{1,9},{5,13},{9,1},{13,5},{2,10},{6,14},... | collective-permute-start | bytes 589832 | tf_op jit(solution)/shard_map/ppermute | solution.py:601
  215.7 25.5 %collective-permute-start.40 = (bf16[64,1536]{1,0:T(8,128)(2,1)S(1)}, bf16[64,1536]{1,0:T(8,128)(2,1)S(1)}, u32[]{:S(2)}, u32[]{:S(2)}) collective-permute-start(bf16[64,1536]{1,0:T(8,128)(2,1)S(1)} %copy-done.43), channel_id=1, source_target_pairs={{0,4},{4,0},{8,12},{12,8},{1,5},{5,1},{9,13},{13,9},{2,6},{6,2},{1... | collective-permute-start | bytes 589832 | tf_op jit(solution)/shard_map/ppermute | solution.py:601
  217.7 24.8 %collective-permute-start.41 = (bf16[64,1536]{1,0:T(8,128)(2,1)S(1)}, bf16[64,1536]{1,0:T(8,128)(2,1)S(1)}, u32[]{:S(2)}, u32[]{:S(2)}) collective-permute-start(bf16[64,1536]{1,0:T(8,128)(2,1)S(1)} %copy-done.42), channel_id=1, source_target_pairs={{0,8},{4,12},{8,0},{12,4},{1,9},{5,13},{9,1},{13,5},{2,10},{6,14},... | collective-permute-start | bytes 589832 | tf_op jit(solution)/shard_map/ppermute | solution.py:601
  220.7 21.9 %collective-permute-start.42 = (bf16[64,1536]{1,0:T(8,128)(2,1)S(1)}, bf16[64,1536]{1,0:T(8,128)(2,1)S(1)}, u32[]{:S(2)}, u32[]{:S(2)}) collective-permute-start(bf16[64,1536]{1,0:T(8,128)(2,1)S(1)} %copy-done.41), channel_id=1, source_target_pairs={{0,12},{4,8},{8,4},{12,0},{1,13},{5,9},{9,5},{13,1},{2,14},{6,10},... | collective-permute-start | bytes 589832 | tf_op jit(solution)/shard_map/ppermute | solution.py:601
  257.8 22.5 %collective-permute-start.61 = (bf16[64,1536]{1,0:T(8,128)(2,1)S(1)}, bf16[64,1536]{1,0:T(8,128)(2,1)S(1)}, u32[]{:S(2)}, u32[]{:S(2)}) collective-permute-start(bf16[64,1536]{1,0:T(8,128)(2,1)S(1)} %get-tuple-element.287), channel_id=1, source_target_pairs={{0,8},{4,12},{8,0},{12,4},{1,9},{5,13},{9,1},{13,5},{2,10},{6,14},... | collective-permute-start | bytes 589832 | tf_op jit(solution)/shard_map/ppermute | solution.py:601
  284.7 109.1 %reduce-scatter.10.cloned.1.call-start = ((), (), s32[]{:S(2)}) async-start(), calls=%async_computation.3 | async-start | bytes 5898240
  285.5 178.2 %reduce-scatter.14.cloned.1.call-start = ((), (), s32[]{:S(2)}) async-start(), calls=%async_computation.5 | async-start | bytes 5898240
  365.4 28.4 %collective-permute-start.75 = (bf16[256,1536]{1,0:T(8,128)(2,1)}, bf16[256,1536]{1,0:T(8,128)(2,1)S(1)}, u32[]{:S(2)}, u32[]{:S(2)}) collective-permute-start(bf16[256,1536]{1,0:T(8,128)(2,1)} %get-tuple-element.320.refs_0_), channel_id=1, source_target_pairs={{0,16},{16,0},{1,17},{17,1},{2,18},{18,2},{3,19},{19,3},{4,20},{20... | collective-permute-start | bytes 2359304 | tf_op jit(solution)/shard_map/ppermute | solution.py:33
  369.9 23.1 %collective-permute-start.76 = (bf16[256,384]{1,0:T(8,128)(2,1)}, bf16[256,384]{1,0:T(8,128)(2,1)S(1)}, u32[]{:S(2)}, u32[]{:S(2)}) collective-permute-start(bf16[256,384]{1,0:T(8,128)(2,1)} %get-tuple-element.330), channel_id=1, source_target_pairs={{1,0},{3,2},{5,4},{7,6},{9,8},{11,10},{13,12},{15,14},{17,16},{19,... | collective-permute-start | bytes 589832 | tf_op jit(solution)/shard_map/ppermute | solution.py:929
  406.3 29.3 %collective-permute-start.80 = (bf16[384,576]{1,0:T(8,128)(2,1)}, bf16[384,576]{1,0:T(8,128)(2,1)S(1)}, u32[]{:S(2)}, u32[]{:S(2)}) collective-permute-start(bf16[384,576]{1,0:T(8,128)(2,1)} %get-tuple-element.336), channel_id=1, source_target_pairs={{0,1},{1,0},{2,3},{3,2},{4,5},{5,4},{6,7},{7,6},{8,9},{9,8},{10,11... | collective-permute-start | bytes 1327112 | tf_op jit(solution)/shard_map/ppermute | solution.py:822
  406.4 29.2 %collective-permute-start.81 = (bf16[384,576]{1,0:T(8,128)(2,1)}, bf16[384,576]{1,0:T(8,128)(2,1)S(1)}, u32[]{:S(2)}, u32[]{:S(2)}) collective-permute-start(bf16[384,576]{1,0:T(8,128)(2,1)} %get-tuple-element.337), channel_id=1, source_target_pairs={{0,2},{1,3},{2,0},{3,1},{4,6},{5,7},{6,4},{7,5},{8,10},{9,11},{10,... | collective-permute-start | bytes 1327112 | tf_op jit(solution)/shard_map/ppermute | solution.py:822
  409.7 34.0 %collective-permute-start.82 = (bf16[384,576]{1,0:T(8,128)(2,1)}, bf16[384,576]{1,0:T(8,128)(2,1)S(1)}, u32[]{:S(2)}, u32[]{:S(2)}) collective-permute-start(bf16[384,576]{1,0:T(8,128)(2,1)} %get-tuple-element.338), channel_id=1, source_target_pairs={{0,3},{1,2},{2,1},{3,0},{4,7},{5,6},{6,5},{7,4},{8,11},{9,10},{10,... | collective-permute-start | bytes 1327112 | tf_op jit(solution)/shard_map/ppermute | solution.py:822
  428.1 19.7 %collective-permute-start.88 = (bf16[64,1536]{1,0:T(8,128)(2,1)S(1)}, bf16[64,1536]{1,0:T(8,128)(2,1)S(1)}, u32[]{:S(2)}, u32[]{:S(2)}) collective-permute-start(bf16[64,1536]{1,0:T(8,128)(2,1)S(1)} %add_shares.15.refs_4_.refs_3_), channel_id=1, source_target_pairs={{0,12},{4,8},{8,4},{12,0},{1,13},{5,9},{9,5},{13,1},{2,14},{6,10},... | collective-permute-start | bytes 589832 | tf_op jit(solution)/shard_map/ppermute | solution.py:601
  451.7 20.4 %collective-permute-start.93 = (bf16[384,576]{1,0:T(8,128)(2,1)}, bf16[384,576]{1,0:T(8,128)(2,1)S(1)}, u32[]{:S(2)}, u32[]{:S(2)}) collective-permute-start(bf16[384,576]{1,0:T(8,128)(2,1)} %get-tuple-element.361), channel_id=1, source_target_pairs={{0,16},{16,0},{1,17},{17,1},{2,18},{18,2},{3,19},{19,3},{4,20},{20... | collective-permute-start | bytes 1327112 | tf_op jit(solution)/shard_map/ppermute | solution.py:33
  (120 other events, 1151.8 us)
Sparse Core Ops, SparseCore 0:
  284.9 35.7 reduce-scatter.11
  323.7 61.1 reduce-scatter.9
  387.9 75.8 reduce-scatter.13
